TPU v7x, 32 devices: a whole 2x2x4 slice. The times are simulated.
32 devices in a mesh: dp: 4 (over z), head: 4 (over y, x), rep: 2 (over core).
Axes of the slice: x: 2, y: 2, z: 4, core: 2. Of those that a mesh axis runs over, the one named last changes fastest.
Arguments:
- embeddings: bfloat16 [2048, 8, 1152], P(('dp', 'head', 'rep')), may hold values from -6 to 6
- coverage: int32 [2048, 2], P(('dp', 'head', 'rep')), may hold values from 0 to 15, all different within a row; in each aligned block of 64 rows (0 to 63, 64 to 127, ...) at most 16 rows name the same one
- labels: int32 [2048, 2, 8], P(('dp', 'head', 'rep')), may hold values 0 or 1
- w_in: bfloat16 [16, 1152, 768], P(('dp', 'head')), may hold values from -0.1875 to 0.1875
- bias_in: bfloat16 [16, 768], P(('dp', 'head')), may hold values from -3 to 3
- w_out: bfloat16 [16, 768], P(('dp', 'head')), may hold values from -0.21875 to 0.21875
- first_w: float32 [16, 1152, 768], P(('dp', 'head'), 'rep'), may hold values from -0.5 to 0.5
- second_w: float32 [16, 1152, 768], P(('dp', 'head'), 'rep'), may hold values from 0.0001 to 0.001
- first_vec: float32 [16, 2, 768], P(('dp', 'head')), may hold values from -0.5 to 0.5
- second_vec: float32 [16, 2, 768], P(('dp', 'head')), may hold values from 0.0001 to 0.01
Outputs:
- new_w_in: bfloat16 [16, 1152, 768], P(('dp', 'head'))
- new_vec: bfloat16 [16, 2, 768], P(('dp', 'head'))
- new_first_w: float32 [16, 1152, 768], P(('dp', 'head'), 'rep')
- new_second_w: float32 [16, 1152, 768], P(('dp', 'head'), 'rep')
- new_first_vec: float32 [16, 2, 768], P(('dp', 'head'))
- new_second_vec: float32 [16, 2, 768], P(('dp', 'head'))
Inputs may be any that keep to these rules, and one draw needn't show every extreme that they name: `coverage`: each block names 2 different heads. Among the 64 blocks of one device (aligned blocks of rows, in order) no head is named more than 16 times, a bound that some block reaches; every head is named by some block.
All inputs are finite; a program needn't handle non-finite values. No bound on the sum of `labels` on one device may be relied on, other than what follows from the above.
Results may differ from a plain program's by a relative error of at most 0.00155.
Values may be sent and summed in bfloat16 or wider, within the bound.
No kernel may reach another device: no remote copies, remote signals or barrier semaphores. Data moves between devices by JAX's collectives and lax.ppermute only.
A program may use at most 128 MiB of HBM per device.

v0:
```python
import jax
import jax.numpy as jnp
from jax import lax
from jax.sharding import PartitionSpec as P

beta_one = 0.9
beta_two = 0.999
learn_rate = 0.001
epsilon = 1e-08


def per_device(
    embeddings, coverage, labels, w_in, bias_in, w_out, first_w, second_w, first_vec, second_vec
):
    dp_count = lax.axis_size("dp")
    head_count = lax.axis_size("head")
    owners = dp_count * head_count
    block_count, rows_block, feature = embeddings.shape
    per_block = coverage.shape[1]
    slot_count = 2 * block_count * per_block // owners
    entries = block_count * per_block
    heads_flat = coverage.reshape(entries)
    onehot = (heads_flat[:, None] == jnp.arange(owners, dtype=jnp.int32)[None, :]).astype(jnp.int32)
    slot_rank = jnp.sum((jnp.cumsum(onehot, axis=0) - 1) * onehot, axis=1)
    target_slot = heads_flat * slot_count + slot_rank
    picker = jnp.arange(owners * slot_count, dtype=jnp.int32)[:, None] == target_slot[None, :]
    block_pick = jnp.sum(
        picker.reshape(owners * slot_count, block_count, per_block).astype(jnp.int32), axis=2
    ).astype(jnp.bfloat16)
    send_rows = jnp.dot(
        block_pick,
        embeddings.reshape(block_count, rows_block * feature),
        preferred_element_type=jnp.float32,
    ).astype(jnp.bfloat16)
    label_marks = (labels.reshape(entries, rows_block) + 1).astype(jnp.float32)
    send_marks = jnp.dot(
        picker.astype(jnp.float32), label_marks, precision=lax.Precision.HIGHEST
    ).astype(jnp.bfloat16)
    direct_rows = send_rows.reshape(owners, slot_count, rows_block, feature)
    direct_marks = send_marks.reshape(owners, slot_count, rows_block)
    got_rows, got_marks = (
        lax.all_to_all(direct_rows, ("dp", "head"), split_axis=0, concat_axis=0, tiled=True),
        lax.all_to_all(direct_marks, ("dp", "head"), split_axis=0, concat_axis=0, tiled=True),
    )
    row_data = got_rows.reshape(-1, feature)
    marks_all = got_marks.reshape(-1).astype(jnp.float32)
    usable = marks_all > 0.5
    target = marks_all - 1.0
    out_weight = w_out[0].astype(jnp.float32)
    pre_act = (
        jnp.dot(row_data, w_in[0], preferred_element_type=jnp.float32)
        + bias_in[0].astype(jnp.float32)[None, :]
    )
    sig_pre = jax.nn.sigmoid(pre_act)
    hidden = pre_act * sig_pre
    logits = jnp.sum(hidden * out_weight[None, :], axis=1)
    residual = jnp.where(usable, jax.nn.sigmoid(logits) - target, jnp.zeros_like(logits))
    grad_pre = residual[:, None] * out_weight[None, :] * sig_pre * (1.0 + pre_act * (1.0 - sig_pre))
    grad_low = grad_pre.astype(jnp.bfloat16)
    vec_part = jnp.stack([jnp.sum(grad_pre, axis=0), jnp.sum(residual[:, None] * hidden, axis=0)])
    half_rows = feature // lax.axis_size("rep")
    first_row = lax.axis_index("rep") * half_rows
    grad_w = lax.psum_scatter(
        lax.dot_general(
            row_data, grad_low, (((0,), (0,)), ((), ())), preferred_element_type=jnp.float32
        ),
        "rep",
        scatter_dimension=0,
        tiled=True,
    )
    grad_vec = lax.psum(vec_part, "rep")
    new_first_w = beta_one * first_w[0] + (1.0 - beta_one) * grad_w
    new_second_w = beta_two * second_w[0] + (1.0 - beta_two) * grad_w * grad_w
    old_rows = lax.dynamic_slice_in_dim(w_in[0], first_row, half_rows, 0).astype(jnp.float32)
    new_half = (old_rows - learn_rate * new_first_w / (jnp.sqrt(new_second_w) + epsilon)).astype(
        jnp.bfloat16
    )
    new_w_in = lax.all_gather(new_half, "rep", axis=0, tiled=True)
    vector = jnp.stack([bias_in[0], w_out[0]]).astype(jnp.float32)
    new_first_vec = beta_one * first_vec[0] + (1.0 - beta_one) * grad_vec
    new_second_vec = beta_two * second_vec[0] + (1.0 - beta_two) * grad_vec * grad_vec
    new_vec = (vector - learn_rate * new_first_vec / (jnp.sqrt(new_second_vec) + epsilon)).astype(
        jnp.bfloat16
    )
    return (
        new_w_in[None],
        new_vec[None],
        new_first_w[None],
        new_second_w[None],
        new_first_vec[None],
        new_second_vec[None],
    )


def solution(mesh):
    placed = (
        P(("dp", "head", "rep"), None, None),
        P(("dp", "head", "rep"), None),
        P(("dp", "head", "rep"), None, None),
        P(("dp", "head"), None, None),
        P(("dp", "head"), None),
        P(("dp", "head"), None),
        P(("dp", "head"), "rep", None),
        P(("dp", "head"), "rep", None),
        P(("dp", "head"), None, None),
        P(("dp", "head"), None, None),
    )
    return jax.shard_map(
        per_device,
        mesh=mesh,
        in_specs=placed,
        out_specs=(
            P(("dp", "head"), None, None),
            P(("dp", "head"), None, None),
            P(("dp", "head"), "rep", None),
            P(("dp", "head"), "rep", None),
            P(("dp", "head"), None, None),
            P(("dp", "head"), None, None),
        ),
        check_vma=False,
    )
```

profile of v0, /device:TPU:0, one launch (start us, length us, event | category | flops | bytes accessed | tf_op | source)
XLA Modules:
  0.0 193.2 jit_solution(14907246978465760152)
XLA Ops:
  7.2 0.8 copy.39
  8.2 0.2 reduce_window_sum.11
  8.5 0.7 add_convert_fusion
  9.3 0.2 convolution_convert_fusion.1
  9.7 0.6 copy.42
  10.3 8.3 %all-to-all-start.1 = ((bf16[16,16,8]{1,2,0:T(8,128)(2,1)}), bf16[16,16,8]{1,2,0:T(8,128)(2,1)S(1)}, u32[]{:S(2)}, u32[]{:S(2)}) async-start(bf16[16,16,8]{1,2,0:T(8,128)(2,1)} %copy.42), calls=%async_computation.1 | async-start | bytes 65536 | tf_op jit(solution)/shard_map/all_to_all | solution.py:43
  18.8 1.5 copy.45
  20.3 0.7 multiply_add_fusion
  21.1 1.4 convolution_convert_fusion
  22.5 3.1 %copy.46 = bf16[32,8,8,1152]{3,2,1,0:T(8,128)(2,1)} copy(bf16[32,8,8,1152]{3,1,2,0:T(8,128)(2,1)S(1)} %bitcast.57) | data formatting | bytes 9437184
  25.6 0.5 all-to-all-done.1
  26.0 6.6 %all-to-all-start = ((bf16[16,16,8,1152]{3,2,1,0:T(8,128)(2,1)}), bf16[16,16,8,1152]{3,2,1,0:T(8,128)(2,1)}, u32[]{:S(2)}, u32[]{:S(2)}) async-start(bf16[16,16,8,1152]{3,2,1,0:T(8,128)(2,1)} %bitcast.56), calls=%async_computation | async-start | bytes 9437184 | tf_op jit(solution)/shard_map/all_to_all | solution.py:42
  33.3 87.4 %all-to-all-done = bf16[16,16,8,1152]{3,2,1,0:T(8,128)(2,1)} async-done(((bf16[16,16,8,1152]{3,2,1,0:T(8,128)(2,1)}), bf16[16,16,8,1152]{3,2,1,0:T(8,128)(2,1)}, u32[]{:S(2)}, u32[]{:S(2)}) %all-to-all-start) | async-done | bytes 4718624 | tf_op jit(solution)/shard_map/all_to_all | solution.py:42
  120.7 7.0 %multiply_reduce_fusion.1 = (f32[2048]{0:T(1024)S(1)}, f32[2048,768]{1,0:T(8,128)S(1)}) fusion(f32[768]{0:T(1024)S(1)} %get-tuple-element.16, f32[768]{0:T(1024)S(1)} %get-tuple-element.17, bf16[2048,1152]{1,0:T(8,128)(2,1)} %bitcast.2, bf16[1,1152,768]{2,1,0:T(8,128)(2,1)S(1)} %copy-done.3), kind=kOutput, calls=%fused_computation.3 | convolution fusion | flops 3634886656 | bytes 12793856 | tf_op jit(solution)/shard_map/dot_general | solution.py:51
  127.7 2.6 %copy-done = f32[2048,768]{1,0:T(8,128)} copy-done((f32[2048,768]{1,0:T(8,128)}, f32[2048,768]{1,0:T(8,128)S(1)}, u32[]{:S(2)}) %copy-start) | copy-done | bytes 6291480
  130.3 9.1 %fusion.1 = f32[1152,768]{1,0:T(8,128)} fusion(bf16[2048,1152]{1,0:T(8,128)(2,1)} %bitcast.2, f32[2048,768]{1,0:T(8,128)S(1)} %get-tuple-element.15, f32[2048]{0:T(1024)S(1)} %subtract_select_fusion, f32[768]{0:T(1024)S(1)} %get-tuple-element.16, f32[768]{0:T(1024)S(1)} %get-tuple-element.17), kind=kOutput, calls=%fused_computation.6 | convolution fusion | flops 3641180160 | bytes 14563328 | tf_op jit(solution)/shard_map/dot_general | solution.py:64
  139.4 0.2 all-gather.2.cloned.1.call-start
  139.7 27.5 %reduce-scatter.2.cloned.1.call-done = f32[576,768]{1,0:T(8,128)} async-done(((f32[1152,768]{1,0:T(8,128)}), f32[576,768]{1,0:T(8,128)}) %reduce-scatter.2.cloned.1.call-update) | async-done | bytes 1769488 | tf_op jit(solution)/shard_map/reduce_scatter | solution.py:63
  167.2 4.9 %fusion.8 = (f32[1,576,768]{2,1,0:T(8,128)}, bf16[576,768]{1,0:T(8,128)(2,1)}, f32[1,576,768]{2,1,0:T(8,128)}) fusion(f32[576,768]{1,0:T(8,128)} %reduce-scatter.2.cloned.1.call-done, f32[1,576,768]{2,1,0:T(8,128)S(1)} %copy-done.1, f32[1,576,768]{2,1,0:T(8,128)S(1)} %copy-done.2, bf16[1,1152,768]{2,1,0:T(8,128)(2,1)} %param.13, s32[]{:T(128)S(6)} %select_n.11), kind=kLoop, calls=%fused_computation.17 | loop fusion | flops 5750784 | bytes 10616836 | tf_op jit(solution)/shard_map/broadcast_in_dim | solution.py:89
  172.1 5.3 %fusion.16 = (f32[768]{0:T(1024)S(1)}, f32[768]{0:T(1024)S(1)}) fusion(f32[2048,768]{1,0:T(8,128)} %copy-done, f32[768]{0:T(1024)S(1)} %get-tuple-element.17, f32[768]{0:T(1024)S(1)} %get-tuple-element.16, f32[2048]{0:T(1024)S(1)} %subtract_select_fusion), kind=kLoop, calls=%fused_computation.42 | loop fusion | flops 22018560 | bytes 6311936 | tf_op jit(solution)/shard_map/reduce_sum | solution.py:60
  177.5 2.5 %psum.7 = f32[2,768]{1,0:T(2,128)S(1)} all-reduce(f32[2,768]{1,0:T(2,128)S(1)} %pad_maximum_fusion), channel_id=1, replica_groups=mesh['dp'=4,'head'=4,'rep'=2] {'rep'}, use_global_device_ids=true, to_apply=%region_7.8 | all-reduce | flops 1536 | bytes 12288 | tf_op jit(solution)/shard_map/psum | solution.py:71
  180.0 0.6 fusion.15
  180.6 2.9 %all-gather.2.cloned.1.call-done = bf16[1152,768]{1,0:T(8,128)(2,1)} async-done(((bf16[576,768]{1,0:T(8,128)(2,1)}), bf16[1152,768]{1,0:T(8,128)(2,1)}) %all-gather.2.cloned.1.call-update) | async-done | bytes 1769488 | tf_op jit(solution)/shard_map/all_gather | solution.py:78
  183.6 2.8 %copy.48 = bf16[1,1152,768]{2,1,0:T(8,128)(2,1)} copy(bf16[1,1152,768]{2,1,0:T(8,128)(2,1)} %bitcast.59) | data formatting | bytes 3538944
  (42 shorter events, 1.5 us)
Async XLA Ops:
  10.3 15.7 %all-to-all-start.1 = ((bf16[16,16,8]{1,2,0:T(8,128)(2,1)}), bf16[16,16,8]{1,2,0:T(8,128)(2,1)S(1)}, u32[]{:S(2)}, u32[]{:S(2)}) async-start(bf16[16,16,8]{1,2,0:T(8,128)(2,1)} %copy.42), calls=%async_computation.1 | async-start | bytes 65536 | tf_op jit(solution)/shard_map/all_to_all | solution.py:43
  26.0 6.7 %copy-start.4 = (bf16[1,768]{1,0:T(2,128)(2,1)S(1)}, bf16[1,768]{1,0:T(2,128)(2,1)}, u32[]{:S(2)}) copy-start(bf16[1,768]{1,0:T(2,128)(2,1)} %param.15) | copy-start | bytes 4612
  26.0 6.7 %copy-start.6 = (bf16[1,768]{1,0:T(2,128)(2,1)S(1)}, bf16[1,768]{1,0:T(2,128)(2,1)}, u32[]{:S(2)}) copy-start(bf16[1,768]{1,0:T(2,128)(2,1)} %param.14) | copy-start | bytes 4612
  26.0 94.6 %copy-start.3 = (bf16[1,1152,768]{2,1,0:T(8,128)(2,1)S(1)}, bf16[1,1152,768]{2,1,0:T(8,128)(2,1)}, u32[]{:S(2)}) copy-start(bf16[1,1152,768]{2,1,0:T(8,128)(2,1)} %param.13) | copy-start | bytes 5308420
  26.0 94.6 %all-to-all-start = ((bf16[16,16,8,1152]{3,2,1,0:T(8,128)(2,1)}), bf16[16,16,8,1152]{3,2,1,0:T(8,128)(2,1)}, u32[]{:S(2)}, u32[]{:S(2)}) async-start(bf16[16,16,8,1152]{3,2,1,0:T(8,128)(2,1)} %bitcast.56), calls=%async_computation | async-start | bytes 9437184 | tf_op jit(solution)/shard_map/all_to_all | solution.py:42
  32.7 134.5 %reduce-scatter.2.cloned.1.call-start = ((), (), s32[]{:S(2)}) async-start(), calls=%async_computation.3 | async-start | bytes 5308416 | tf_op jit(solution)/shard_map/reduce_scatter | solution.py:63
  127.7 2.7 %copy-start = (f32[2048,768]{1,0:T(8,128)}, f32[2048,768]{1,0:T(8,128)S(1)}, u32[]{:S(2)}) copy-start(f32[2048,768]{1,0:T(8,128)S(1)} %get-tuple-element.15) | copy-start | bytes 18874372
  139.4 27.8 %copy-start.1 = (f32[1,576,768]{2,1,0:T(8,128)S(1)}, f32[1,576,768]{2,1,0:T(8,128)}, u32[]{:S(2)}) copy-start(f32[1,576,768]{2,1,0:T(8,128)} %param.17) | copy-start | bytes 5308420
  139.4 27.8 %copy-start.2 = (f32[1,576,768]{2,1,0:T(8,128)S(1)}, f32[1,576,768]{2,1,0:T(8,128)}, u32[]{:S(2)}) copy-start(f32[1,576,768]{2,1,0:T(8,128)} %param.16) | copy-start | bytes 5308420
  139.4 44.1 %all-gather.2.cloned.1.call-start = ((), (), s32[]{:S(2)}) async-start(), calls=%async_computation.4 | async-start | bytes 2654208 | tf_op jit(solution)/shard_map/all_gather | solution.py:78
  172.1 7.9 %copy-start.5 = (bf16[1,768]{1,0:T(2,128)(2,1)S(1)}, bf16[1,768]{1,0:T(2,128)(2,1)}, u32[]{:S(2)}) copy-start(bf16[1,768]{1,0:T(2,128)(2,1)} %param.15) | copy-start | bytes 4612
  172.1 7.9 %copy-start.7 = (bf16[1,768]{1,0:T(2,128)(2,1)S(1)}, bf16[1,768]{1,0:T(2,128)(2,1)}, u32[]{:S(2)}) copy-start(bf16[1,768]{1,0:T(2,128)(2,1)} %param.14) | copy-start | bytes 4612
  172.1 7.9 %copy-start.8 = (f32[1,2,768]{2,1,0:T(2,128)S(1)}, f32[1,2,768]{2,1,0:T(2,128)}, u32[]{:S(2)}) copy-start(f32[1,2,768]{2,1,0:T(2,128)} %param.19) | copy-start | bytes 18436
  172.1 7.9 %copy-start.9 = (f32[1,2,768]{2,1,0:T(2,128)S(1)}, f32[1,2,768]{2,1,0:T(2,128)}, u32[]{:S(2)}) copy-start(f32[1,2,768]{2,1,0:T(2,128)} %param.18) | copy-start | bytes 18436
Sparse Core Ops, SparseCore 0:
  139.5 27.5 reduce-scatter.1
  172.3 11.2 all-gather.1
where the time goes:
time: 194 us; the launch traced here: 193 us
  waiting for transfers between devices  118 us (61%)
  matrix products  17.7 us (9%)
  starting transfers between devices  15.2 us (8%)
  between operations  14.3 us (7%)
  other arithmetic  12.8 us (7%)
  local copies, waits for them, and re-layouts  12.4 us (6%)
  blocking collectives  2.49 us (1%)
    all_to_all x1, waiting for transfers between devices, per_device(): lax.all_to_all(direct_rows, ('dp', 'head'), split_axis=0, concat_axis=0,...  87.4 us
    reduce_scatter x1, waiting for transfers between devices, per_device(): lax.psum_scatter(lax.dot_general(row_data, grad_low, (((0,), (0,)), ((),...  27.5 us
    unnamed x24, local copies, waits for them, and re-layouts  10.8 us
    dot_general x1, matrix products, per_device(): lax.dot_general(row_data, grad_low, (((0,), (0,)), ((), ())), preferred_e...  9.07 us
    all_to_all x1, starting transfers between devices, per_device(): lax.all_to_all(direct_marks, ('dp', 'head'), split_axis=0, concat_axis=0,...  8.31 us
    dot_general x1, matrix products, per_device(): jnp.dot(row_data, w_in[0], preferred_element_type=jnp.float32)  7 us
    all_to_all x1, starting transfers between devices, per_device(): lax.all_to_all(direct_rows, ('dp', 'head'), split_axis=0, concat_axis=0,...  6.64 us
    reduce_sum x1, other arithmetic, per_device(): jnp.sum(grad_pre, axis=0)  5.27 us
  transfers between devices with their start and end apart: 4, of which 4 were waited for; matrix products, arithmetic and copies ran while one was open for 7% of the time, Pallas kernels for 0%

commit v1 on v0

--- a/solution.py
+++ b/solution.py
@@ -7,6 +7,7 @@
 beta_two = 0.999
 learn_rate = 0.001
 epsilon = 1e-08
+swap = [(0, 1), (1, 0)]
 
 
 def per_device(
@@ -59,23 +60,27 @@
     grad_low = grad_pre.astype(jnp.bfloat16)
     vec_part = jnp.stack([jnp.sum(grad_pre, axis=0), jnp.sum(residual[:, None] * hidden, axis=0)])
     half_rows = feature // lax.axis_size("rep")
-    first_row = lax.axis_index("rep") * half_rows
-    grad_w = lax.psum_scatter(
-        lax.dot_general(
-            row_data, grad_low, (((0,), (0,)), ((), ())), preferred_element_type=jnp.float32
-        ),
-        "rep",
-        scatter_dimension=0,
-        tiled=True,
-    )
-    grad_vec = lax.psum(vec_part, "rep")
+    rep_at = lax.axis_index("rep")
+    first_row = rep_at * half_rows
+    grad_part = lax.dot_general(
+        row_data, grad_low, (((0,), (0,)), ((), ())), preferred_element_type=jnp.float32
+    ).reshape(2, half_rows, -1)
+    kept = jnp.where(rep_at == 0, grad_part[0], grad_part[1])
+    given = jnp.where(rep_at == 0, grad_part[1], grad_part[0])
+    grad_w = kept + lax.ppermute(given, "rep", swap)
+    grad_vec = vec_part + lax.ppermute(vec_part, "rep", swap)
     new_first_w = beta_one * first_w[0] + (1.0 - beta_one) * grad_w
     new_second_w = beta_two * second_w[0] + (1.0 - beta_two) * grad_w * grad_w
     old_rows = lax.dynamic_slice_in_dim(w_in[0], first_row, half_rows, 0).astype(jnp.float32)
     new_half = (old_rows - learn_rate * new_first_w / (jnp.sqrt(new_second_w) + epsilon)).astype(
         jnp.bfloat16
     )
-    new_w_in = lax.all_gather(new_half, "rep", axis=0, tiled=True)
+    other_half = lax.ppermute(new_half, "rep", swap)
+    new_w_in = jnp.where(
+        rep_at == 0,
+        jnp.concatenate([new_half, other_half]),
+        jnp.concatenate([other_half, new_half]),
+    )
     vector = jnp.stack([bias_in[0], w_out[0]]).astype(jnp.float32)
     new_first_vec = beta_one * first_vec[0] + (1.0 - beta_one) * grad_vec
     new_second_vec = beta_two * second_vec[0] + (1.0 - beta_two) * grad_vec * grad_vec

time: 194 us -> 167 us (0.86)
  the two profiles are of different devices: /device:TPU:0 before, /device:TPU:15 now
where the time goes in v1:
time: 167 us; the launch traced here: 166 us
  waiting for transfers between devices  109 us (65%)
  matrix products  18.1 us (11%)
  starting transfers between devices  15.4 us (9%)
  other arithmetic  15.3 us (9%)
  local copies, waits for them, and re-layouts  7.54 us (5%)
    all_to_all x1, waiting for transfers between devices, per_device(): lax.all_to_all(direct_rows, ('dp', 'head'), split_axis=0, concat_axis=0,...  105 us
    dot_general x1, matrix products, per_device(): lax.dot_general(row_data, grad_low, (((0,), (0,)), ((), ())), preferred_e...  9.46 us
    dot_general x1, matrix products, per_device(): jnp.dot(row_data, w_in[0], preferred_element_type=jnp.float32)  7 us
    all_to_all x1, starting transfers between devices, per_device(): lax.all_to_all(direct_marks, ('dp', 'head'), split_axis=0, concat_axis=0,...  6.58 us
    all_to_all x1, starting transfers between devices, per_device(): lax.all_to_all(direct_rows, ('dp', 'head'), split_axis=0, concat_axis=0,...  6.5 us
    unnamed x27, local copies, waits for them, and re-layouts  5.9 us
    broadcast_in_dim x1, other arithmetic, per_device(): new_second_w[None]  3.67 us
    ppermute x1, waiting for transfers between devices, per_device(): grad_w = kept + lax.ppermute(given, 'rep', swap)  3.65 us
  transfers between devices with their start and end apart: 5, of which 3 were waited for; matrix products, arithmetic and copies ran while one was open for 7% of the time, Pallas kernels for 0%

profile of v1, /device:TPU:15, one launch (start us, length us, event | category | flops | bytes accessed | tf_op | source)
XLA Modules:
  0.0 166.2 jit_solution(1372608765328573309)
XLA Ops:
  0.6 0.7 add_convert_fusion
  1.3 0.8 copy.39
  3.1 0.6 copy.42
  3.8 6.6 %all-to-all-start.1 = ((bf16[16,16,8]{1,2,0:T(8,128)(2,1)}), bf16[16,16,8]{1,2,0:T(8,128)(2,1)S(1)}, u32[]{:S(2)}, u32[]{:S(2)}) async-start(bf16[16,16,8]{1,2,0:T(8,128)(2,1)} %copy.42), calls=%async_computation.1 | async-start | bytes 65536 | tf_op jit(solution)/shard_map/all_to_all | solution.py:44
  10.5 0.7 multiply_add_fusion
  11.3 1.5 copy.45
  12.8 1.4 convolution_convert_fusion
  14.2 3.1 %copy.46 = bf16[32,8,8,1152]{3,2,1,0:T(8,128)(2,1)} copy(bf16[32,8,8,1152]{3,1,2,0:T(8,128)(2,1)S(1)} %bitcast.58) | data formatting | bytes 9437184
  17.3 6.5 %all-to-all-start = ((bf16[16,16,8,1152]{3,2,1,0:T(8,128)(2,1)}), bf16[16,16,8,1152]{3,2,1,0:T(8,128)(2,1)}, u32[]{:S(2)}, u32[]{:S(2)}) async-start(bf16[16,16,8,1152]{3,2,1,0:T(8,128)(2,1)} %bitcast.57), calls=%async_computation | async-start | bytes 9437184 | tf_op jit(solution)/shard_map/all_to_all | solution.py:43
  24.3 104.5 %all-to-all-done = bf16[16,16,8,1152]{3,2,1,0:T(8,128)(2,1)} async-done(((bf16[16,16,8,1152]{3,2,1,0:T(8,128)(2,1)}), bf16[16,16,8,1152]{3,2,1,0:T(8,128)(2,1)}, u32[]{:S(2)}, u32[]{:S(2)}) %all-to-all-start) | async-done | bytes 4718624 | tf_op jit(solution)/shard_map/all_to_all | solution.py:43
  128.8 7.0 %multiply_reduce_fusion.1 = (f32[2048]{0:T(1024)S(1)}, f32[2048,768]{1,0:T(8,128)S(1)}) fusion(f32[768]{0:T(1024)S(1)} %get-tuple-element.17, f32[768]{0:T(1024)S(1)} %get-tuple-element.18, bf16[2048,1152]{1,0:T(8,128)(2,1)} %bitcast.2, bf16[1,1152,768]{2,1,0:T(8,128)(2,1)S(1)} %copy-done.4), kind=kOutput, calls=%fused_computation.3 | convolution fusion | flops 3634886656 | bytes 12793856 | tf_op jit(solution)/shard_map/dot_general | solution.py:52
  135.9 9.5 %fusion.1 = f32[1152,768]{1,0:T(8,128)S(1)} fusion(bf16[2048,1152]{1,0:T(8,128)(2,1)} %bitcast.2, f32[2048,768]{1,0:T(8,128)S(1)} %get-tuple-element.16, f32[2048]{0:T(1024)S(1)} %subtract_select_fusion, f32[768]{0:T(1024)S(1)} %get-tuple-element.17, f32[768]{0:T(1024)S(1)} %get-tuple-element.18), kind=kOutput, calls=%fused_computation.6 | convolution fusion | flops 3641180160 | bytes 14563328 | tf_op jit(solution)/shard_map/dot_general | solution.py:65
  145.4 1.4 slice_select_fusion
  146.8 1.5 collective-permute-start
  148.3 3.7 %collective-permute-done = f32[576,768]{1,0:T(8,128)} collective-permute-done((f32[576,768]{1,0:T(8,128)}, f32[576,768]{1,0:T(8,128)}, u32[]{:S(2)}, u32[]{:S(2)}) %collective-permute-start) | collective-permute-done | bytes 1769504 | tf_op jit(solution)/shard_map/ppermute | solution.py:70
  151.9 3.7 %fusion.8 = (f32[1,576,768]{2,1,0:T(8,128)}, f32[576,768]{1,0:T(8,128)S(1)}) fusion(f32[1,576,768]{2,1,0:T(8,128)} %param.17, f32[576,768]{1,0:T(8,128)} %collective-permute-done, f32[1152,768]{1,0:T(8,128)S(1)} %fusion.1, pred[]{:T(512)S(6)} %eq.40), kind=kLoop, calls=%fused_computation.20 | loop fusion | flops 2654208 | bytes 10616833 | tf_op jit(solution)/shard_map/broadcast_in_dim | solution.py:94
  155.6 2.4 %fusion.7 = (f32[1,576,768]{2,1,0:T(8,128)}, bf16[576,768]{1,0:T(8,128)(2,1)S(1)}) fusion(f32[576,768]{1,0:T(8,128)S(1)} %get-tuple-element.9, f32[1,576,768]{2,1,0:T(8,128)S(1)} %copy-done.3, f32[1,576,768]{2,1,0:T(8,128)S(1)} %copy-done, bf16[1,1152,768]{2,1,0:T(8,128)(2,1)S(1)} %copy-done.5, s32[]{:T(128)S(6)} %select_n.39), kind=kLoop, calls=%fused_computation.19 | loop fusion | flops 5750784 | bytes 8847364 | tf_op jit(solution)/shard_map/broadcast_in_dim | solution.py:93
  158.0 0.4 collective-permute-start.1
  158.4 0.6 copy-done.2
  159.0 3.2 %fusion.16 = (f32[768]{0:T(1024)S(1)}, f32[768]{0:T(1024)S(1)}) fusion(f32[2048,768]{1,0:T(8,128)S(1)} %copy-done.2, f32[768]{0:T(1024)S(1)} %get-tuple-element.18, f32[768]{0:T(1024)S(1)} %get-tuple-element.17, f32[2048]{0:T(1024)S(1)} %subtract_select_fusion), kind=kLoop, calls=%fused_computation.45 | loop fusion | flops 22018560 | bytes 6311936 | tf_op jit(solution)/shard_map/reduce_sum | solution.py:61
  162.3 0.4 collective-permute-start.2
  162.7 0.8 collective-permute-done.2
  163.6 0.6 fusion.15
  164.2 2.0 %maximum_select_fusion = bf16[1,1152,768]{2,1,0:T(8,128)(2,1)} fusion(bf16[1,576,768]{2,1,0:T(8,128)(2,1)S(1)} %bitcast.62, bf16[1,576,768]{2,1,0:T(8,128)(2,1)S(1)} %bitcast.60, pred[]{:T(512)S(6)} %eq.40), kind=kLoop, calls=%fused_computation.10 | loop fusion | flops 7962624 | bytes 3538945 | tf_op jit(solution)/shard_map/jit(_where)/select_n | solution.py:79
  (47 shorter events, 1.8 us)
Async XLA Ops:
  3.8 13.5 %all-to-all-start.1 = ((bf16[16,16,8]{1,2,0:T(8,128)(2,1)}), bf16[16,16,8]{1,2,0:T(8,128)(2,1)S(1)}, u32[]{:S(2)}, u32[]{:S(2)}) async-start(bf16[16,16,8]{1,2,0:T(8,128)(2,1)} %copy.42), calls=%async_computation.1 | async-start | bytes 65536 | tf_op jit(solution)/shard_map/all_to_all | solution.py:44
  17.3 6.5 %copy-start.6 = (bf16[1,768]{1,0:T(2,128)(2,1)S(1)}, bf16[1,768]{1,0:T(2,128)(2,1)}, u32[]{:S(2)}) copy-start(bf16[1,768]{1,0:T(2,128)(2,1)} %param.15) | copy-start | bytes 4612
  17.3 6.5 %copy-start.8 = (bf16[1,768]{1,0:T(2,128)(2,1)S(1)}, bf16[1,768]{1,0:T(2,128)(2,1)}, u32[]{:S(2)}) copy-start(bf16[1,768]{1,0:T(2,128)(2,1)} %param.14) | copy-start | bytes 4612
  17.3 111.6 %copy-start.4 = (bf16[1,1152,768]{2,1,0:T(8,128)(2,1)S(1)}, bf16[1,1152,768]{2,1,0:T(8,128)(2,1)}, u32[]{:S(2)}) copy-start(bf16[1,1152,768]{2,1,0:T(8,128)(2,1)} %param.13) | copy-start | bytes 5308420
  17.3 111.5 %all-to-all-start = ((bf16[16,16,8,1152]{3,2,1,0:T(8,128)(2,1)}), bf16[16,16,8,1152]{3,2,1,0:T(8,128)(2,1)}, u32[]{:S(2)}, u32[]{:S(2)}) async-start(bf16[16,16,8,1152]{3,2,1,0:T(8,128)(2,1)} %bitcast.57), calls=%async_computation | async-start | bytes 9437184 | tf_op jit(solution)/shard_map/all_to_all | solution.py:43
  135.8 9.5 %copy-start.1 = (f32[2048,768]{1,0:T(8,128)}, f32[2048,768]{1,0:T(8,128)S(1)}, u32[]{:S(2)}) copy-start(f32[2048,768]{1,0:T(8,128)S(1)} %get-tuple-element.16) | copy-start | bytes 18874372
  146.8 5.1 %collective-permute-start = (f32[576,768]{1,0:T(8,128)}, f32[576,768]{1,0:T(8,128)}, u32[]{:S(2)}, u32[]{:S(2)}) collective-permute-start(f32[576,768]{1,0:T(8,128)} %slice_select_fusion), channel_id=1, source_target_pairs={{0,1},{1,0},{2,3},{3,2},{4,5},{5,4},{6,7},{7,6},{8,9},{9,8},{10,11... | collective-permute-start | bytes 5308424 | tf_op jit(solution)/shard_map/ppermute | solution.py:70
  148.3 7.3 %copy-start = (f32[1,576,768]{2,1,0:T(8,128)S(1)}, f32[1,576,768]{2,1,0:T(8,128)}, u32[]{:S(2)}) copy-start(f32[1,576,768]{2,1,0:T(8,128)} %param.17) | copy-start | bytes 5308420
  148.3 7.3 %copy-start.3 = (f32[1,576,768]{2,1,0:T(8,128)S(1)}, f32[1,576,768]{2,1,0:T(8,128)}, u32[]{:S(2)}) copy-start(f32[1,576,768]{2,1,0:T(8,128)} %param.16) | copy-start | bytes 5308420
  148.3 7.3 %copy-start.5 = (bf16[1,1152,768]{2,1,0:T(8,128)(2,1)S(1)}, bf16[1,1152,768]{2,1,0:T(8,128)(2,1)}, u32[]{:S(2)}) copy-start(bf16[1,1152,768]{2,1,0:T(8,128)(2,1)} %param.13) | copy-start | bytes 5308420
  155.6 3.4 %copy-start.2 = (f32[2048,768]{1,0:T(8,128)S(1)}, f32[2048,768]{1,0:T(8,128)}, u32[]{:S(2)}) copy-start(f32[2048,768]{1,0:T(8,128)} %copy-done.1) | copy-start | bytes 18874372
  158.0 5.6 %copy-start.7 = (bf16[1,768]{1,0:T(2,128)(2,1)S(1)}, bf16[1,768]{1,0:T(2,128)(2,1)}, u32[]{:S(2)}) copy-start(bf16[1,768]{1,0:T(2,128)(2,1)} %param.15) | copy-start | bytes 4612
  158.0 5.6 %copy-start.9 = (bf16[1,768]{1,0:T(2,128)(2,1)S(1)}, bf16[1,768]{1,0:T(2,128)(2,1)}, u32[]{:S(2)}) copy-start(bf16[1,768]{1,0:T(2,128)(2,1)} %param.14) | copy-start | bytes 4612
  158.0 5.6 %copy-start.10 = (f32[1,2,768]{2,1,0:T(2,128)S(1)}, f32[1,2,768]{2,1,0:T(2,128)}, u32[]{:S(2)}) copy-start(f32[1,2,768]{2,1,0:T(2,128)} %param.19) | copy-start | bytes 18436
  158.0 5.6 %copy-start.11 = (f32[1,2,768]{2,1,0:T(2,128)S(1)}, f32[1,2,768]{2,1,0:T(2,128)}, u32[]{:S(2)}) copy-start(f32[1,2,768]{2,1,0:T(2,128)} %param.18) | copy-start | bytes 18436
  158.0 6.2 %collective-permute-start.1 = (bf16[576,768]{1,0:T(8,128)(2,1)S(1)}, bf16[576,768]{1,0:T(8,128)(2,1)S(1)}, u32[]{:S(2)}, u32[]{:S(2)}) collective-permute-start(bf16[576,768]{1,0:T(8,128)(2,1)S(1)} %get-tuple-element.11), channel_id=1, source_target_pairs={{0,1},{1,0},{2,3},{3,2},{4,5},{5,4},{6,7},{7,6},{8,9},{9,8},{10,11... | collective-permute-start | bytes 2654216 | tf_op jit(solution)/shard_map/ppermute | solution.py:78
  162.3 1.3 collective-permute-start.2

commit v2 on v1

--- a/solution.py
+++ b/solution.py
@@ -1,6 +1,10 @@
+import functools
+
 import jax
 import jax.numpy as jnp
 from jax import lax
+from jax.experimental import pallas as pl
+from jax.experimental.pallas import tpu as pltpu
 from jax.sharding import PartitionSpec as P
 
 beta_one = 0.9
@@ -8,9 +12,516 @@
 learn_rate = 0.001
 epsilon = 1e-08
 swap = [(0, 1), (1, 0)]
-
-
-def per_device(
+MIB = 1024 * 1024
+ANY = pl.BlockSpec(memory_space=pl.ANY)
+VMEM = pl.BlockSpec(memory_space=pltpu.VMEM)
+SMEM = pl.BlockSpec(memory_space=pltpu.SMEM)
+f32 = jnp.float32
+bf16 = jnp.bfloat16
+
+
+def params(mib):
+    return pltpu.CompilerParams(vmem_limit_bytes=mib * MIB)
+
+
+def sds(shape, dtype):
+    return jax.ShapeDtypeStruct(shape, dtype)
+
+
+def half_sigmoid(x):
+    return 0.5 * jnp.tanh(0.5 * x) + 0.5
+
+
+def marks_kernel(owners, unit, cov_ref, lab_ref, out_ref):
+    per_block, blocks = cov_ref.shape
+    rows_block = lab_ref.shape[1]
+    rows = blocks * rows_block
+    cov = cov_ref[...]
+    heads_at = lax.broadcasted_iota(jnp.int32, (owners, blocks), 0)
+    named = (cov[0:1] == heads_at).astype(f32)
+    for t in range(1, per_block):
+        named = named + (cov[t : t + 1] == heads_at).astype(f32)
+    block_of = lax.broadcasted_iota(jnp.int32, (blocks, rows), 1) // rows_block
+    block_at = lax.broadcasted_iota(jnp.int32, (blocks, rows), 0)
+    same = (block_of == block_at).astype(bf16)
+    before = (block_at < block_of).astype(bf16)
+    rank = jnp.dot(named.astype(bf16), before, preferred_element_type=f32)
+    cov_rows = jnp.dot(cov.astype(f32).astype(bf16), same, preferred_element_type=f32)
+    row_in = lax.broadcasted_iota(jnp.int32, (rows_block, rows), 1) % rows_block
+    row_at = lax.broadcasted_iota(jnp.int32, (rows_block, rows), 0)
+    head_rows = lax.broadcasted_iota(jnp.int32, (owners, rows), 0).astype(f32)
+    for t in range(per_block):
+        mine = cov_rows[t : t + 1]
+        own_rank = jnp.sum(jnp.where(mine == head_rows, rank, 0.0), axis=0, keepdims=True)
+        out_ref[t : t + 1, :] = (
+            mine * unit + own_rank * rows_block + row_in[0:1].astype(f32)
+        )
+        spread = jnp.dot(lab_ref[t].astype(f32).astype(bf16), same, preferred_element_type=f32)
+        out_ref[per_block + t : per_block + t + 1, :] = 1.0 + jnp.sum(
+            jnp.where(row_in == row_at, spread, 0.0), axis=0, keepdims=True
+        )
+
+
+def make_marks(coverage, labels, owners, unit):
+    blocks, per_block = coverage.shape
+    rows = blocks * labels.shape[2]
+    return pl.pallas_call(
+        functools.partial(marks_kernel, owners, unit),
+        out_shape=sds((2 * per_block, rows), f32),
+        in_specs=[VMEM, VMEM],
+        out_specs=VMEM,
+        compiler_params=params(8),
+        name="marks",
+    )(coverage.T, labels.transpose(1, 2, 0))
+
+
+def pick_rows(marks, shard, first_code, unit, per_block):
+    rows = marks.shape[1]
+    slot = lax.broadcasted_iota(jnp.int32, (unit, rows), 0).astype(f32) + first_code
+    chosen = marks[0:1] == slot
+    for t in range(1, per_block):
+        chosen = chosen | (marks[t : t + 1] == slot)
+    return jnp.dot(
+        jnp.where(chosen, 1.0, 0.0).astype(bf16), shard, preferred_element_type=f32
+    ).astype(bf16)
+
+
+def pick_kernel(plan, unit, per_block, n_shards, n_marks, at_ref, *refs):
+    shards, refs = refs[:n_shards], refs[n_shards:]
+    marks, refs = refs[:n_marks], refs[n_marks:]
+    n_heads = len(plan[0][2])
+    n_out = len(plan) * n_heads
+    outs, (held, sems) = refs[:-2], refs[-2:]
+    loads = []
+    for i in range(n_shards):
+        load = pltpu.make_async_copy(shards[i], held.at[i], sems.at[i])
+        load.start()
+        loads.append(load)
+    done = set()
+    for shard_at, mark_at, places in plan:
+        if shard_at not in done:
+            loads[shard_at].wait()
+            done.add(shard_at)
+        for slot, (out_at, row_at) in enumerate(places):
+            first_code = at_ref[mark_at * n_heads + slot].astype(f32)
+            outs[out_at][row_at : row_at + unit, :] = pick_rows(
+                marks[mark_at][...], held[shard_at], first_code, unit, per_block
+            )
+
+
+def pick_either_kernel(unit, per_block, n_heads, at_ref, left_ref, right_ref, marks_ref, *refs):
+    outs, (held, sem) = refs[:-2], refs[-2:]
+    use_left = at_ref[n_heads] > 0
+
+    @pl.when(use_left)
+    def _():
+        load = pltpu.make_async_copy(left_ref, held, sem)
+        load.start()
+        load.wait()
+
+    @pl.when(jnp.logical_not(use_left))
+    def _():
+        load = pltpu.make_async_copy(right_ref, held, sem)
+        load.start()
+        load.wait()
+
+    for slot in range(n_heads):
+        outs[slot][...] = pick_rows(
+            marks_ref[...], held[...], at_ref[slot].astype(f32), unit, per_block
+        )
+
+
+def learn_kernel(
+    unit, per_block, n_units, n_parts, last, with_total, half_rows,
+    at_ref, *refs
+):
+    parts, refs = refs[:n_parts], refs[n_parts:]
+    marks_ref, w_ref, bias_ref, out_ref, refs = refs[0], refs[1], refs[2], refs[3], refs[4:]
+    if with_total:
+        total_ref, vec_ref, refs = refs[0], refs[1], refs[2:]
+    if last:
+        kept_ref, given_ref, refs = refs[0], refs[1], refs[2:]
+    else:
+        new_total_ref, new_vec_ref, refs = refs[0], refs[1], refs[2:]
+    rows_ref, low_ref, target_ref, sems = refs
+    rows_all, feature = rows_ref.shape
+    loads = []
+    at = 0
+    for i in range(n_parts):
+        size = parts[i].shape[0]
+        load = pltpu.make_async_copy(parts[i], rows_ref.at[pl.ds(at, size)], sems.at[i])
+        load.start()
+        loads.append(load)
+        at += size
+    first_code = at_ref[0].astype(f32)
+    for u in range(n_units):
+        source = at_ref[1 + u]
+        real = at_ref[1 + n_units + u].astype(f32)
+        marks = marks_ref[source]
+        slot = lax.broadcasted_iota(jnp.int32, (unit, marks.shape[1]), 0).astype(f32) + first_code
+        found = jnp.zeros(slot.shape, f32)
+        for t in range(per_block):
+            found = found + jnp.where(
+                marks[t : t + 1] == slot, marks[per_block + t : per_block + t + 1], 0.0
+            )
+        target_ref[u * unit : (u + 1) * unit, :] = jnp.sum(found, axis=1, keepdims=True) * real
+    for load in loads:
+        load.wait()
+    bias = bias_ref[...].astype(f32)
+    out_weight = out_ref[...].astype(f32)
+    step = 2 * unit
+    hid = w_ref.shape[1]
+
+    def forward(i, carry):
+        span = pl.ds(pl.multiple_of(i * step, step), step)
+        pre = jnp.dot(rows_ref[span, :], w_ref[...], preferred_element_type=f32) + bias
+        gate = half_sigmoid(pre)
+        hidden = pre * gate
+        logit = jnp.sum(hidden * out_weight, axis=1, keepdims=True)
+        mark = target_ref[span, :]
+        residual = jnp.where(mark > 0.5, half_sigmoid(logit) - (mark - 1.0), 0.0)
+        grad_pre = residual * out_weight * gate * (1.0 + pre * (1.0 - gate))
+        low_ref[span, :] = grad_pre.astype(bf16)
+        return (
+            carry[0] + jnp.sum(grad_pre, axis=0, keepdims=True),
+            carry[1] + jnp.sum(residual * hidden, axis=0, keepdims=True),
+        )
+
+    if with_total:
+        start = (vec_ref[0:1, :], vec_ref[1:2, :])
+    else:
+        start = (jnp.zeros((1, hid), f32), jnp.zeros((1, hid), f32))
+    grad_bias, grad_out = lax.fori_loop(0, rows_all // step, forward, start)
+
+    def product(first, size):
+        piece = lax.dot_general(
+            rows_ref[:, first : first + size],
+            low_ref[...],
+            (((0,), (0,)), ((), ())),
+            preferred_element_type=f32,
+        )
+        if with_total:
+            piece = piece + total_ref[first : first + size, :]
+        return piece
+
+    tile = 128 * max(n for n in range(1, 5) if feature % (128 * n) == 0)
+    if not last:
+        for first in range(0, feature, tile):
+            new_total_ref[first : first + tile, :] = product(first, tile)
+        new_vec_ref[0:1, :] = grad_bias
+        new_vec_ref[1:2, :] = grad_out
+        return
+    rep = at_ref[1 + 2 * n_units]
+    given_ref[half_rows : half_rows + 8, :] = jnp.zeros((8, hid), f32)
+    kept_ref[half_rows : half_rows + 8, :] = jnp.zeros((8, hid), f32)
+    for ref in (given_ref, kept_ref):
+        ref[half_rows : half_rows + 1, :] = grad_bias
+        ref[half_rows + 1 : half_rows + 2, :] = grad_out
+    for first in range(0, feature, tile):
+        piece = product(first, tile)
+        cut = min(max(half_rows - first, 0), tile)
+
+        @pl.when(rep == 0)
+        def _():
+            if cut > 0:
+                kept_ref[first : first + cut, :] = piece[:cut]
+            if cut < tile:
+                given_ref[first + cut - half_rows : first + tile - half_rows, :] = piece[cut:]
+
+        @pl.when(rep != 0)
+        def _():
+            if cut > 0:
+                given_ref[first : first + cut, :] = piece[:cut]
+            if cut < tile:
+                kept_ref[first + cut - half_rows : first + tile - half_rows, :] = piece[cut:]
+
+
+def learn(unit, per_block, n_units, parts, at, marks, w, bias, out, total, last):
+    feature, hid = w.shape
+    rows_all = sum(p.shape[0] for p in parts)
+    half = feature // 2
+    if last:
+        outs = (sds((half + 8, hid), f32), sds((half + 8, hid), f32))
+    else:
+        outs = (sds((feature, hid), f32), sds((2, hid), f32))
+    extra = () if total is None else total
+    kernel = functools.partial(
+        learn_kernel, unit, per_block, n_units, len(parts), last, total is not None, half
+    )
+    return pl.pallas_call(
+        kernel,
+        out_shape=outs,
+        in_specs=[SMEM] + [ANY] * len(parts) + [VMEM] * (4 + len(extra)),
+        out_specs=(VMEM, VMEM),
+        scratch_shapes=[
+            pltpu.VMEM((rows_all, feature), bf16),
+            pltpu.VMEM((rows_all, hid), bf16),
+            pltpu.VMEM((rows_all, 1), f32),
+            pltpu.SemaphoreType.DMA((len(parts),)),
+        ],
+        compiler_params=params(32),
+        cost_estimate=pl.CostEstimate(
+            flops=4 * rows_all * feature * hid,
+            bytes_accessed=4 * rows_all * feature + 10 * feature * hid,
+            transcendentals=rows_all * hid,
+        ),
+        name="learn",
+    )(at, *parts, marks, w, bias, out, *extra)
+
+
+def adam(old, grad, first, second):
+    new_first = beta_one * first + (1.0 - beta_one) * grad
+    new_second = beta_two * second + (1.0 - beta_two) * grad * grad
+    new = old - learn_rate * new_first / (jnp.sqrt(new_second) + epsilon)
+    return new.astype(bf16), new_first, new_second
+
+
+def step_kernel(
+    at_ref, kept, got, kept_vec, got_vec, w, first_w, second_w, vec_old, first_vec, second_vec,
+    new_half, new_full, new_vec, new_first_w, new_second_w, new_first_vec, new_second_vec,
+):
+    new, new_first, new_second = adam(
+        w[...].astype(f32), kept[...] + got[...], first_w[0], second_w[0]
+    )
+    new_half[...] = new
+    new_full[0] = new
+    new_first_w[0] = new_first
+    new_second_w[0] = new_second
+
+    @pl.when(pl.program_id(0) == 0)
+    def _():
+        grad = kept_vec[0:2, :] + got_vec[0:2, :]
+        fresh, fresh_first, fresh_second = adam(
+            vec_old[...].astype(f32), grad, first_vec[0], second_vec[0]
+        )
+        new_vec[0] = fresh
+        new_first_vec[0] = fresh_first
+        new_second_vec[0] = fresh_second
+
+
+def take_step(rep, kept, got, w_in, vec_old, first_w, second_w, first_vec, second_vec):
+    feature, hid = w_in.shape
+    half = feature // 2
+    tiles = max(n for n in range(1, 5) if half % (16 * n) == 0)
+    tile = half // tiles
+    here = pl.BlockSpec((tile, hid), lambda i, at: (i, 0))
+    there = pl.BlockSpec((tile, hid), lambda i, at: (at[0] * tiles + i, 0))
+    tail = pl.BlockSpec((8, hid), lambda i, at: (half // 8, 0))
+    moment = pl.BlockSpec((1, tile, hid), lambda i, at: (0, i, 0))
+    pair = pl.BlockSpec((2, hid), lambda i, at: (0, 0))
+    pairs = pl.BlockSpec((1, 2, hid), lambda i, at: (0, 0, 0))
+    full = pl.BlockSpec((1, tile, hid), lambda i, at: (0, at[0] * tiles + i, 0))
+    return pl.pallas_call(
+        step_kernel,
+        grid_spec=pltpu.PrefetchScalarGridSpec(
+            num_scalar_prefetch=1,
+            grid=(tiles,),
+            in_specs=[here, here, tail, tail, there, moment, moment, pair, pairs, pairs],
+            out_specs=[here, full, pairs, moment, moment, pairs, pairs],
+        ),
+        out_shape=(
+            sds((half, hid), bf16),
+            sds((1, feature, hid), bf16),
+            sds((1, 2, hid), bf16),
+            sds((1, half, hid), f32),
+            sds((1, half, hid), f32),
+            sds((1, 2, hid), f32),
+            sds((1, 2, hid), f32),
+        ),
+        compiler_params=params(24),
+        name="step",
+    )(rep, kept, got, kept, got, w_in, first_w, second_w, vec_old, first_vec, second_vec)
+
+
+def join_kernel(at_ref, other_ref, full_ref, out_ref, sem):
+    half = other_ref.shape[0]
+    start = pl.multiple_of((1 - at_ref[0]) * half, half)
+    load = pltpu.make_async_copy(other_ref, out_ref.at[0, pl.ds(start, half)], sem)
+    load.start()
+    load.wait()
+
+
+def join(rep, other, full):
+    return pl.pallas_call(
+        join_kernel,
+        out_shape=sds(full.shape, full.dtype),
+        in_specs=[SMEM, ANY, ANY],
+        out_specs=ANY,
+        scratch_shapes=[pltpu.SemaphoreType.DMA(())],
+        input_output_aliases={2: 0},
+        compiler_params=params(8),
+        name="join",
+    )(rep, other, full)
+
+
+def gathered(
+    embeddings, coverage, labels, w_in, bias_in, w_out, first_w, second_w, first_vec, second_vec
+):
+    planes = lax.axis_size("dp")
+    heads = lax.axis_size("head")
+    owners = planes * heads
+    z = lax.axis_index("dp")
+    q = lax.axis_index("head")
+    rep = lax.axis_index("rep").reshape(1)
+    blocks, rows_block, feature = embeddings.shape
+    per_block = coverage.shape[1]
+    slots = 2 * blocks * per_block // owners
+    unit = slots * rows_block
+    rows = blocks * rows_block
+    hid = w_in.shape[2]
+    i32 = jnp.int32
+
+    def right_pairs(hop):
+        return [(i, i + 1) for i in range(hop - 1, planes - 1)]
+
+    def left_pairs(hop):
+        return [(i + 1, i) for i in range(planes - hop)]
+
+    head_pairs = [[(i, i ^ k) for i in range(heads)] for k in range(heads)]
+
+    def pair_up(k, ends):
+        wanted = (0, planes - 1) if ends else range(planes)
+        return [(p * heads + i, p * heads + (i ^ k)) for p in wanted for i in range(heads)]
+
+    def exchange(units, ends=False):
+        return [units[0]] + [
+            lax.ppermute(units[k], ("dp", "head"), pair_up(k, ends)) for k in range(1, heads)
+        ]
+
+    def codes(plane):
+        return [(plane * heads + (q ^ k)) * unit for k in range(heads)]
+
+    own = embeddings.reshape(rows, feature)
+    marks_own = make_marks(coverage, labels, owners, unit)
+
+    hops_right, hops_left = [own], [own]
+    for hop in range(1, planes - 1):
+        hops_right.append(lax.ppermute(hops_right[-1], "dp", right_pairs(hop)))
+        hops_left.append(lax.ppermute(hops_left[-1], "dp", left_pairs(hop)))
+
+    marks_z = [marks_own] + [
+        lax.ppermute(marks_own, "dp", [(i, (i + s) % planes) for i in range(planes)])
+        for s in range(1, planes)
+    ]
+    marks_plane = jnp.stack(marks_z)
+    marks_all = jnp.stack(
+        [marks_plane]
+        + [lax.ppermute(marks_plane, "head", head_pairs[k]) for k in range(1, heads)]
+    ).reshape(heads * planes, 2 * per_block, rows)
+
+    def pick(shards, marks, plan, scalars, out_rows):
+        kernel = functools.partial(
+            pick_kernel, plan, unit, per_block, len(shards), len(marks)
+        )
+        return pl.pallas_call(
+            kernel,
+            out_shape=[sds((r, feature), bf16) for r in out_rows],
+            in_specs=[SMEM] + [ANY] * len(shards) + [VMEM] * len(marks),
+            out_specs=[VMEM] * len(out_rows),
+            scratch_shapes=[
+                pltpu.VMEM((len(shards), rows, feature), bf16),
+                pltpu.SemaphoreType.DMA((len(shards),)),
+            ],
+            compiler_params=params(32),
+            cost_estimate=pl.CostEstimate(
+                flops=2 * sum(out_rows) * rows * feature,
+                bytes_accessed=2 * feature * (sum(out_rows) + rows * len(shards)),
+                transcendentals=0,
+            ),
+            name="pick",
+        )(jnp.stack(scalars).astype(i32), *shards, *marks)
+
+    far = planes - 1 - z
+    plan = [
+        (0, 1, [(heads + k, 0) for k in range(heads)]),
+        (0, 0, [(k, 0) for k in range(heads)]),
+    ]
+    picked = pick(
+        [own], [marks_own, marks_own], plan, codes(z) + codes(far), [unit] * (2 * heads)
+    )
+    far_units = exchange(picked[heads:], ends=True)
+    own_units = exchange(picked[:heads])
+    far_sent = jnp.concatenate(far_units)
+    far_got = lax.ppermute(far_sent, "dp", [(0, planes - 1), (planes - 1, 0)])
+
+    one = jnp.ones((), i32)
+    groups = [(own_units, [(k, jnp.zeros((), i32), one) for k in range(heads)])]
+    for hop in range(1, planes - 1):
+        from_left = (z >= hop).astype(i32)
+        from_right = (z + hop < planes).astype(i32)
+        if 2 * hop < planes:
+            plan = [
+                (0, 0, [(k, 0) for k in range(heads)]),
+                (1, 1, [(k, unit) for k in range(heads)]),
+            ]
+            absent = -2 * unit * jnp.ones((), i32)
+            scalars = [jnp.where(from_left > 0, c, absent) for c in codes(z)]
+            scalars += [jnp.where(from_right > 0, c, absent) for c in codes(z)]
+            got = exchange(
+                pick(
+                    [hops_right[hop], hops_left[hop]],
+                    [marks_z[hop], marks_z[planes - hop]],
+                    plan,
+                    scalars,
+                    [2 * unit] * heads,
+                )
+            )
+            sources = []
+            for k in range(heads):
+                sources.append((k, jnp.full((), hop, i32), from_left))
+                sources.append((k, jnp.full((), planes - hop, i32), from_right))
+        else:
+            use_left = from_right
+            back = jnp.where(use_left > 0, planes - hop, hop).astype(i32)
+            marks_hop = jnp.where(use_left > 0, marks_z[planes - hop], marks_z[hop])
+            scalars = jnp.stack(codes(z) + [use_left]).astype(i32)
+            got = exchange(
+                pl.pallas_call(
+                    functools.partial(pick_either_kernel, unit, per_block, heads),
+                    out_shape=[sds((unit, feature), bf16)] * heads,
+                    in_specs=[SMEM, ANY, ANY, VMEM],
+                    out_specs=[VMEM] * heads,
+                    scratch_shapes=[
+                        pltpu.VMEM((rows, feature), bf16),
+                        pltpu.SemaphoreType.DMA(()),
+                    ],
+                    compiler_params=params(32),
+                    cost_estimate=pl.CostEstimate(
+                        flops=2 * heads * unit * rows * feature,
+                        bytes_accessed=2 * feature * (heads * unit + rows),
+                        transcendentals=0,
+                    ),
+                    name="pick",
+                )(scalars, hops_left[hop], hops_right[hop], marks_hop)
+            )
+            sources = [(k, back, from_left | from_right) for k in range(heads)]
+        groups.append((got, sources))
+    at_end = ((z == 0) | (z == planes - 1)).astype(i32)
+    far_back = jnp.where(z == 0, 1, planes - 1).astype(i32)
+    groups.append(([far_got], [(k, far_back, at_end) for k in range(heads)]))
+
+    total = None
+    my_code = (z * heads + q) * unit
+    for at, (parts, sources) in enumerate(groups):
+        scalars = [my_code]
+        scalars += [k * planes + back for k, back, _ in sources]
+        scalars += [real for _, _, real in sources]
+        scalars += [rep[0]]
+        total = learn(
+            unit, per_block, len(sources), parts, jnp.stack(scalars).astype(i32), marks_all,
+            w_in[0], bias_in, w_out, total, at == len(groups) - 1,
+        )
+    kept, given = total
+    got = lax.ppermute(given, "rep", swap)
+    vec_old = jnp.concatenate([bias_in, w_out])
+    new_half, new_full, new_vec, nfw, nsw, nfv, nsv = take_step(
+        rep, kept, got, w_in[0], vec_old, first_w, second_w, first_vec, second_vec
+    )
+    new_w_in = join(rep, lax.ppermute(new_half, "rep", swap), new_full)
+    return new_w_in, new_vec, nfw, nsw, nfv, nsv
+
+
+def routed(
     embeddings, coverage, labels, w_in, bias_in, w_out, first_w, second_w, first_vec, second_vec
 ):
     dp_count = lax.axis_size("dp")
@@ -110,8 +621,10 @@
         P(("dp", "head"), None, None),
         P(("dp", "head"), None, None),
     )
+    planes, heads, reps = mesh.shape["dp"], mesh.shape["head"], mesh.shape["rep"]
+    short = 2 < planes <= heads and heads & (heads - 1) == 0 and reps == 2
     return jax.shard_map(
-        per_device,
+        gathered if short else routed,
         mesh=mesh,
         in_specs=placed,
         out_specs=(

time: 167 us -> 167 us (level)
  the two profiles are of different devices: /device:TPU:15 before, /device:TPU:0 now
where the time goes in v2:
time: 167 us; the launch traced here: 166 us
  waiting for transfers between devices  72.9 us (44%)
  starting transfers between devices  43.1 us (26%)
  Pallas kernels  37.5 us (22%)
  local copies, waits for them, and re-layouts  9.18 us (5%)
  other arithmetic  2.21 us (1%)
    pallas_call x4, Pallas kernels, learn(): pl.pallas_call(kernel, out_shape=outs, in_specs=[SMEM] + [ANY] * len(part...  23.8 us
    ppermute x2, waiting for transfers between devices, gathered(): hops_left.append(lax.ppermute(hops_left[-1], 'dp', left_pairs(hop)))  23.3 us
    ppermute x3, waiting for transfers between devices, gathered(): lax.ppermute(marks_own, 'dp', [(i, (i + s) % planes) for i in range(plane...  21.9 us
    ppermute x12, waiting for transfers between devices, exchange(): lax.ppermute(units[k], ('dp', 'head'), pair_up(k, ends))  21.7 us
    ppermute x12, starting transfers between devices, exchange(): lax.ppermute(units[k], ('dp', 'head'), pair_up(k, ends))  20.5 us
    unnamed x36, local copies, waits for them, and re-layouts  8.57 us
    ppermute x2, starting transfers between devices, gathered(): hops_right.append(lax.ppermute(hops_right[-1], 'dp', right_pairs(hop)))  8.34 us
    pallas_call x2, Pallas kernels, pick(): pl.pallas_call(kernel, out_shape=[sds((r, feature), bf16) for r in out_ro...  7.47 us
  transfers between devices with their start and end apart: 25, of which 11 were waited for; matrix products, arithmetic and copies ran while one was open for 2% of the time, Pallas kernels for 16%

profile of v2, /device:TPU:0, one launch (start us, length us, event | category | flops | bytes accessed | tf_op | source)
XLA Modules:
  0.0 166.0 jit_solution(12377455202115765622)
XLA Ops:
  1.9 6.6 %collective-permute-start.12 = (bf16[512,1152]{1,0:T(8,128)(2,1)}, bf16[512,1152]{1,0:T(8,128)(2,1)}, u32[]{:S(2)}, u32[]{:S(2)}) collective-permute-start(bf16[512,1152]{1,0:T(8,128)(2,1)} %bitcast.56), channel_id=1, source_target_pairs={{0,8},{8,16},{16,24},{1,9},{9,17},{17,25},{2,10},{10,18},{18,26},{... | collective-permute-start | bytes 3538952 | tf_op jit(solution)/shard_map/ppermute | solution.py:399
  8.6 23.3 %collective-permute-done.10.refs_1_ = bf16[512,1152]{1,0:T(8,128)(2,1)} collective-permute-done((bf16[512,1152]{1,0:T(8,128)(2,1)}, bf16[512,1152]{1,0:T(8,128)(2,1)}, u32[]{:S(2)}, u32[]{:S(2)}) %collective-permute-start.10) | collective-permute-done | bytes 1179680 | tf_op jit(solution)/shard_map/ppermute | solution.py:400
  35.9 2.9 %collective-permute-start.5 = (f32[4,512]{1,0:T(4,128)S(1)}, f32[4,512]{1,0:T(4,128)S(1)}, u32[]{:S(2)}, u32[]{:S(2)}) collective-permute-start(f32[4,512]{1,0:T(4,128)S(1)} %marks.1.refs_1_.refs_2_), channel_id=1, source_target_pairs={{0,16},{8,24},{16,0},{24,8},{1,17},{9,25},{17,1},{25,9},{2,18},{10... | collective-permute-start | bytes 24584 | tf_op jit(solution)/shard_map/ppermute | solution.py:403
  40.7 20.8 %collective-permute-done.6.refs_3_ = f32[4,512]{1,0:T(4,128)S(1)} collective-permute-done((f32[4,512]{1,0:T(4,128)S(1)}, f32[4,512]{1,0:T(4,128)S(1)}, u32[]{:S(2)}, u32[]{:S(2)}) %collective-permute-start.6) | collective-permute-done | bytes 8224 | tf_op jit(solution)/shard_map/ppermute | solution.py:403
  62.7 2.5 %collective-permute-start.9 = (f32[4,4,512]{2,1,0:T(4,128)S(1)}, f32[4,4,512]{2,1,0:T(4,128)S(1)}, u32[]{:S(2)}, u32[]{:S(2)}) collective-permute-start(f32[4,4,512]{2,1,0:T(4,128)S(1)} %get-tuple-element.69), channel_id=1, source_target_pairs={{0,6},{2,4},{4,2},{6,0},{1,7},{3,5},{5,3},{7,1},{8,14},{10,12},{12... | collective-permute-start | bytes 98312 | tf_op jit(solution)/shard_map/ppermute | solution.py:409
  67.5 3.0 %pick.3 = (bf16[128,1152]{1,0:T(8,128)(2,1)S(1)}, bf16[128,1152]{1,0:T(8,128)(2,1)}, bf16[128,1152]{1,0:T(8,128)(2,1)}, bf16[128,1152]{1,0:T(8,128)(2,1)}, bf16[...) custom-call(s32[8]{0:T(128)S(1)} %stack.168.at_ref, ...), custom_call_target="tpu_custom_call" | custom-call | flops 1207959552 | bytes 3538944 | tf_op jit(solution)/shard_map/pick/pallas_call | solution.py:416
  71.3 4.3 %collective-permute-start.2 = (bf16[128,1152]{1,0:T(8,128)(2,1)S(1)}, bf16[128,1152]{1,0:T(8,128)(2,1)S(1)}, u32[]{:S(2)}, u32[]{:S(2)}) collective-permute-start(bf16[128,1152]{1,0:T(8,128)(2,1)S(1)} %get-tuple-element.40), channel_id=1, source_target_pairs={{0,6},{2,4},{4,2},{6,0},{24,30},{26,28},{28,26},{30,24},{1,7},{3,5... | collective-permute-start | bytes 884744 | tf_op jit(solution)/shard_map/ppermute | solution.py:388
  75.6 2.4 %collective-permute-start.1 = (bf16[128,1152]{1,0:T(8,128)(2,1)S(1)}, bf16[128,1152]{1,0:T(8,128)(2,1)}, u32[]{:S(2)}, u32[]{:S(2)}) collective-permute-start(bf16[128,1152]{1,0:T(8,128)(2,1)S(1)} %get-tuple-element.39), channel_id=1, source_target_pairs={{0,4},{2,6},{4,0},{6,2},{24,28},{26,30},{28,24},{30,26},{1,5},{3,7... | collective-permute-start | bytes 884744 | tf_op jit(solution)/shard_map/ppermute | solution.py:388
  78.0 2.4 %collective-permute-start = (bf16[128,1152]{1,0:T(8,128)(2,1)S(1)}, bf16[128,1152]{1,0:T(8,128)(2,1)}, u32[]{:S(2)}, u32[]{:S(2)}) collective-permute-start(bf16[128,1152]{1,0:T(8,128)(2,1)S(1)} %get-tuple-element.38), channel_id=1, source_target_pairs={{0,2},{2,0},{4,6},{6,4},{24,26},{26,24},{28,30},{30,28},{1,3},{3,1... | collective-permute-start | bytes 884744 | tf_op jit(solution)/shard_map/ppermute | solution.py:388
  84.3 2.1 %collective-permute-done.1 = bf16[128,1152]{1,0:T(8,128)(2,1)} collective-permute-done((bf16[128,1152]{1,0:T(8,128)(2,1)S(1)}, bf16[128,1152]{1,0:T(8,128)(2,1)}, u32[]{:S(2)}, u32[]{:S(2)}) %collective-permute-start.1) | collective-permute-done | bytes 294944 | tf_op jit(solution)/shard_map/ppermute | solution.py:388
  87.8 2.2 %collective-permute-done = bf16[128,1152]{1,0:T(8,128)(2,1)} collective-permute-done((bf16[128,1152]{1,0:T(8,128)(2,1)S(1)}, bf16[128,1152]{1,0:T(8,128)(2,1)}, u32[]{:S(2)}, u32[]{:S(2)}) %collective-permute-start) | collective-permute-done | bytes 294944 | tf_op jit(solution)/shard_map/ppermute | solution.py:388
  91.5 2.2 %pad_maximum_fusion = bf16[512,1152]{1,0:T(8,128)(2,1)} fusion(bf16[128,1152]{1,0:T(8,128)(2,1)S(1)} %collective-permute-done.2, bf16[128,1152]{1,0:T(8,128)(2,1)} %collective-permute-done.1, bf16[128,1152]{1,0:T(8,128)(2,1)} %collective-permute-done, bf16[128,1152]{1,0:T(8,128)(2,1)S(1)} %get-tuple-element.37), kind=kLoop, calls=%fused_computation | loop fusion | flops 4718592 | bytes 2359296 | tf_op jit(solution)/shard_map/concatenate | solution.py:444
  93.6 2.6 %collective-permute-done.20.refs_1_ = bf16[128,1152]{1,0:T(8,128)(2,1)S(1)} collective-permute-done((bf16[128,1152]{1,0:T(8,128)(2,1)}, bf16[128,1152]{1,0:T(8,128)(2,1)S(1)}, u32[]{:S(2)}, u32[]{:S(2)}) %collective-permute-start.20) | collective-permute-done | bytes 294944 | tf_op jit(solution)/shard_map/ppermute | solution.py:388
  96.2 1.9 %collective-permute-start.3 = (bf16[512,1152]{1,0:T(8,128)(2,1)}, bf16[512,1152]{1,0:T(8,128)(2,1)}, u32[]{:S(2)}, u32[]{:S(2)}) collective-permute-start(bf16[512,1152]{1,0:T(8,128)(2,1)} %pad_maximum_fusion), channel_id=1, source_target_pairs={{0,24},{24,0},{1,25},{25,1},{2,26},{26,2},{3,27},{27,3},{4,28},{28... | collective-permute-start | bytes 3538952 | tf_op jit(solution)/shard_map/ppermute | solution.py:445
  98.1 4.4 %pick.5 = (bf16[256,1152]{1,0:T(8,128)(2,1)S(1)}, bf16[256,1152]{1,0:T(8,128)(2,1)}, bf16[256,1152]{1,0:T(8,128)(2,1)}, bf16[256,1152]{1,0:T(8,128)(2,1)}) custom-call(s32[8]{0:T(128)S(1)} %stack.194.at_ref, bf16[512,1152]{1,0:T(8,128)(2,1)} %collective-permute-done.12.refs_0_, bf16[512,1152]{1,0:T(8,128)(2,1)} %collective-permute-done.10.refs_1_, ...), custom_call_target="tpu_custom_call" | custom-call | flops 1207959552 | bytes 4718592 | tf_op jit(solution)/shard_map/pick/pallas_call | solution.py:416
  111.8 4.4 %learn.4 = (f32[1152,768]{1,0:T(8,128)S(1)}, f32[2,768]{1,0:T(2,128)S(1)}) custom-call(s32[10]{0:T(128)S(1)} %stack.195.at_ref, bf16[128,1152]{1,0:T(8,128)(2,1)S(1)} %copy-done.17, bf16[128,1152]{1,0:T(8,128)(2,1)S(1)} %collective-permute-done.20.refs_1_, bf16[128,1152]{1,0:T(8,128)(2,1)S(1)} %copy-done.11, bf16[128,1152]{1,0:T(8,128)(2,1)S(1)} %copy-done.13, ...), custom_call_target="tpu_custom_call" | custom-call | flops 1811939328 | bytes 11206656 | tf_op jit(solution)/shard_map/learn/pallas_call | solution.py:251
  116.2 1.8 %pick.4 = (bf16[128,1152]{1,0:T(8,128)(2,1)S(1)}, bf16[128,1152]{1,0:T(8,128)(2,1)S(1)}, bf16[128,1152]{1,0:T(8,128)(2,1)S(1)}, bf16[128,1152]{1,0:T(8,128)(2,1)S(1)}) custom-call(s32[5]{0:T(128)S(1)} %stack.182.at_ref, bf16[512,1152]{1,0:T(8,128)(2,1)S(1)} %collective-permute-done.11.left_ref, bf16[512,1152]{1,0:T(8,128)(2,1)} %collective-permute-done.13.right_ref, ...), custom_call_target="tpu_custom_call" | custom-call | flops 603979776 | bytes 2359296 | tf_op jit(solution)/shard_map/pick/pallas_call | solution.py:479
  121.7 13.4 %collective-permute-done.18.refs_2_ = bf16[256,1152]{1,0:T(8,128)(2,1)} collective-permute-done((bf16[256,1152]{1,0:T(8,128)(2,1)}, bf16[256,1152]{1,0:T(8,128)(2,1)}, u32[]{:S(2)}, u32[]{:S(2)}) %collective-permute-start.18) | collective-permute-done | bytes 589856 | tf_op jit(solution)/shard_map/ppermute | solution.py:388
  135.8 8.7 %learn.5 = (f32[1152,768]{1,0:T(8,128)S(1)}, f32[2,768]{1,0:T(2,128)S(1)}) custom-call(s32[18]{0:T(128)S(1)} %stack.185.at_ref, bf16[256,1152]{1,0:T(8,128)(2,1)S(1)} %copy-done.15, bf16[256,1152]{1,0:T(8,128)(2,1)} %collective-permute-done.17.refs_1_, bf16[256,1152]{1,0:T(8,128)(2,1)} %collective-permute-done.18.refs_2_, ...), custom_call_target="tpu_custom_call" | custom-call | flops 3623878656 | bytes 13565952 | tf_op jit(solution)/shard_map/learn/pallas_call | solution.py:251
  144.6 4.5 %learn.6 = (f32[1152,768]{1,0:T(8,128)S(1)}, f32[2,768]{1,0:T(2,128)S(1)}) custom-call(s32[10]{0:T(128)S(1)} %stack.180.at_ref, bf16[128,1152]{1,0:T(8,128)(2,1)S(1)} %get-tuple-element.41.refs_0_, bf16[128,1152]{1,0:T(8,128)(2,1)S(1)} %collective-permute-done.14.refs_1_, bf16[128,1152]{1,0:T(8,128)(2,1)S(1)} %collective-permute-done.15.refs_2_, ...), custom_call_target="tpu_custom_call" | custom-call | flops 1811939328 | bytes 11206656 | tf_op jit(solution)/shard_map/learn/pallas_call | solution.py:251
  149.1 6.2 %learn.7 = (f32[584,768]{1,0:T(8,128)S(1)}, f32[584,768]{1,0:T(8,128)S(1)}) custom-call(s32[10]{0:T(128)S(1)} %stack.160.at_ref, bf16[512,1152]{1,0:T(8,128)(2,1)} %collective-permute-done.3.refs_0_, f32[16,4,512]{2,1,0:T(4,128)S(1)} %bitcast.48, bf16[1152,768]{1,0:T(8,128)(2,1)S(1)} %bitcast.43, bf16[1,768]{1,0:T(2,128)(2,1)S(1)} %copy-done.6, ...), custom_call_target="tpu_custom_call" | custom-call | flops 1811939328 | bytes 11206656 | tf_op jit(solution)/shard_map/learn/pallas_call | solution.py:251
  155.4 3.7 %collective-permute-done.23.got.got_vec = f32[584,768]{1,0:T(8,128)S(1)} collective-permute-done((f32[584,768]{1,0:T(8,128)S(1)}, f32[584,768]{1,0:T(8,128)S(1)}, u32[]{:S(2)}, u32[]{:S(2)}) %collective-permute-start.23) | collective-permute-done | bytes 1794080 | tf_op jit(solution)/shard_map/ppermute | solution.py:515
  159.2 3.3 %step.1 = (bf16[576,768]{1,0:T(8,128)(2,1)S(1)}, bf16[1,1152,768]{2,1,0:T(8,128)(2,1)}, bf16[1,2,768]{2,1,0:T(2,128)(2,1)}, f32[1,576,768]{2,1,0:T(8,128)}, f32[...) custom-call(s32[1]{0:T(128)} %bitcast.at_ref, f32[584,768]{1,0:T(8,128)S(1)} %get-tuple-element.59.kept.kept_vec, ...), custom_call_target="tpu_custom_call" | custom-call | tf_op jit(solution)/shard_map/step/pallas_call | solution.py:314
  162.6 2.3 %collective-permute-done.24.other_ref = bf16[576,768]{1,0:T(8,128)(2,1)S(1)} collective-permute-done((bf16[576,768]{1,0:T(8,128)(2,1)S(1)}, bf16[576,768]{1,0:T(8,128)(2,1)S(1)}, u32[]{:S(2)}, u32[]{:S(2)}) %collective-permute-start.24) | collective-permute-done | bytes 884768 | tf_op jit(solution)/shard_map/ppermute | solution.py:520
  (84 shorter events, 32.8 us)
Async XLA Ops:
  0.6 31.2 %collective-permute-start.10 = (bf16[512,1152]{1,0:T(8,128)(2,1)}, bf16[512,1152]{1,0:T(8,128)(2,1)}, u32[]{:S(2)}, u32[]{:S(2)}) collective-permute-start(bf16[512,1152]{1,0:T(8,128)(2,1)} %bitcast.55), channel_id=1, source_target_pairs={{8,0},{16,8},{24,16},{9,1},{17,9},{25,17},{10,2},{18,10},{26,18},{... | collective-permute-start | bytes 3538952 | tf_op jit(solution)/shard_map/ppermute | solution.py:400
  1.9 78.6 %collective-permute-start.12 = (bf16[512,1152]{1,0:T(8,128)(2,1)}, bf16[512,1152]{1,0:T(8,128)(2,1)}, u32[]{:S(2)}, u32[]{:S(2)}) collective-permute-start(bf16[512,1152]{1,0:T(8,128)(2,1)} %bitcast.56), channel_id=1, source_target_pairs={{0,8},{8,16},{16,24},{1,9},{9,17},{17,25},{2,10},{10,18},{18,26},{... | collective-permute-start | bytes 3538952 | tf_op jit(solution)/shard_map/ppermute | solution.py:399
  31.8 75.1 %collective-permute-start.11 = (bf16[512,1152]{1,0:T(8,128)(2,1)}, bf16[512,1152]{1,0:T(8,128)(2,1)S(1)}, u32[]{:S(2)}, u32[]{:S(2)}) collective-permute-start(bf16[512,1152]{1,0:T(8,128)(2,1)} %collective-permute-done.10.refs_1_), channel_id=1, source_target_pairs={{8,0},{16,8},{9,1},{17,9},{10,2},{18,10},{11,3},{19,11},{12,4},{20... | collective-permute-start | bytes 3538952 | tf_op jit(solution)/shard_map/ppermute | solution.py:400
  34.7 26.8 %collective-permute-start.6 = (f32[4,512]{1,0:T(4,128)S(1)}, f32[4,512]{1,0:T(4,128)S(1)}, u32[]{:S(2)}, u32[]{:S(2)}) collective-permute-start(f32[4,512]{1,0:T(4,128)S(1)} %marks.1.refs_1_.refs_2_), channel_id=1, source_target_pairs={{0,24},{8,0},{16,8},{24,16},{1,25},{9,1},{17,9},{25,17},{2,26},{10... | collective-permute-start | bytes 24584 | tf_op jit(solution)/shard_map/ppermute | solution.py:403
  35.9 26.7 %collective-permute-start.5 = (f32[4,512]{1,0:T(4,128)S(1)}, f32[4,512]{1,0:T(4,128)S(1)}, u32[]{:S(2)}, u32[]{:S(2)}) collective-permute-start(f32[4,512]{1,0:T(4,128)S(1)} %marks.1.refs_1_.refs_2_), channel_id=1, source_target_pairs={{0,16},{8,24},{16,0},{24,8},{1,17},{9,25},{17,1},{25,9},{2,18},{10... | collective-permute-start | bytes 24584 | tf_op jit(solution)/shard_map/ppermute | solution.py:403
  38.8 23.8 %collective-permute-start.4 = (f32[4,512]{1,0:T(4,128)S(1)}, f32[4,512]{1,0:T(4,128)S(1)}, u32[]{:S(2)}, u32[]{:S(2)}) collective-permute-start(f32[4,512]{1,0:T(4,128)S(1)} %marks.1.refs_1_.refs_2_), channel_id=1, source_target_pairs={{0,8},{8,16},{16,24},{24,0},{1,9},{9,17},{17,25},{25,1},{2,10},{10... | collective-permute-start | bytes 24584 | tf_op jit(solution)/shard_map/ppermute | solution.py:403
  62.7 8.6 %collective-permute-start.9 = (f32[4,4,512]{2,1,0:T(4,128)S(1)}, f32[4,4,512]{2,1,0:T(4,128)S(1)}, u32[]{:S(2)}, u32[]{:S(2)}) collective-permute-start(f32[4,4,512]{2,1,0:T(4,128)S(1)} %get-tuple-element.69), channel_id=1, source_target_pairs={{0,6},{2,4},{4,2},{6,0},{1,7},{3,5},{5,3},{7,1},{8,14},{10,12},{12... | collective-permute-start | bytes 98312 | tf_op jit(solution)/shard_map/ppermute | solution.py:409
  65.2 10.4 %collective-permute-start.8 = (f32[4,4,512]{2,1,0:T(4,128)S(1)}, f32[4,4,512]{2,1,0:T(4,128)S(1)}, u32[]{:S(2)}, u32[]{:S(2)}) collective-permute-start(f32[4,4,512]{2,1,0:T(4,128)S(1)} %get-tuple-element.69), channel_id=1, source_target_pairs={{0,4},{2,6},{4,0},{6,2},{1,5},{3,7},{5,1},{7,3},{8,12},{10,14},{12... | collective-permute-start | bytes 98312 | tf_op jit(solution)/shard_map/ppermute | solution.py:409
  65.7 12.4 %collective-permute-start.7 = (f32[4,4,512]{2,1,0:T(4,128)S(1)}, f32[4,4,512]{2,1,0:T(4,128)S(1)}, u32[]{:S(2)}, u32[]{:S(2)}) collective-permute-start(f32[4,4,512]{2,1,0:T(4,128)S(1)} %get-tuple-element.69), channel_id=1, source_target_pairs={{0,2},{2,0},{4,6},{6,4},{1,3},{3,1},{5,7},{7,5},{8,10},{10,8},{12,... | collective-permute-start | bytes 98312 | tf_op jit(solution)/shard_map/ppermute | solution.py:409
  71.3 11.5 %collective-permute-start.2 = (bf16[128,1152]{1,0:T(8,128)(2,1)S(1)}, bf16[128,1152]{1,0:T(8,128)(2,1)S(1)}, u32[]{:S(2)}, u32[]{:S(2)}) collective-permute-start(bf16[128,1152]{1,0:T(8,128)(2,1)S(1)} %get-tuple-element.40), channel_id=1, source_target_pairs={{0,6},{2,4},{4,2},{6,0},{24,30},{26,28},{28,26},{30,24},{1,7},{3,5... | collective-permute-start | bytes 884744 | tf_op jit(solution)/shard_map/ppermute | solution.py:388
  75.6 10.7 %collective-permute-start.1 = (bf16[128,1152]{1,0:T(8,128)(2,1)S(1)}, bf16[128,1152]{1,0:T(8,128)(2,1)}, u32[]{:S(2)}, u32[]{:S(2)}) collective-permute-start(bf16[128,1152]{1,0:T(8,128)(2,1)S(1)} %get-tuple-element.39), channel_id=1, source_target_pairs={{0,4},{2,6},{4,0},{6,2},{24,28},{26,30},{28,24},{30,26},{1,5},{3,7... | collective-permute-start | bytes 884744 | tf_op jit(solution)/shard_map/ppermute | solution.py:388
  78.0 11.9 %collective-permute-start = (bf16[128,1152]{1,0:T(8,128)(2,1)S(1)}, bf16[128,1152]{1,0:T(8,128)(2,1)}, u32[]{:S(2)}, u32[]{:S(2)}) collective-permute-start(bf16[128,1152]{1,0:T(8,128)(2,1)S(1)} %get-tuple-element.38), channel_id=1, source_target_pairs={{0,2},{2,0},{4,6},{6,4},{24,26},{26,24},{28,30},{30,28},{1,3},{3,1... | collective-permute-start | bytes 884744 | tf_op jit(solution)/shard_map/ppermute | solution.py:388
  80.5 35.7 %collective-permute-start.13 = (bf16[512,1152]{1,0:T(8,128)(2,1)}, bf16[512,1152]{1,0:T(8,128)(2,1)}, u32[]{:S(2)}, u32[]{:S(2)}) collective-permute-start(bf16[512,1152]{1,0:T(8,128)(2,1)} %collective-permute-done.12.refs_0_), channel_id=1, source_target_pairs={{8,16},{16,24},{9,17},{17,25},{10,18},{18,26},{11,19},{19,27},{12,... | collective-permute-start | bytes 3538952 | tf_op jit(solution)/shard_map/ppermute | solution.py:399
  82.7 13.5 %collective-permute-start.20 = (bf16[128,1152]{1,0:T(8,128)(2,1)}, bf16[128,1152]{1,0:T(8,128)(2,1)S(1)}, u32[]{:S(2)}, u32[]{:S(2)}) collective-permute-start(bf16[128,1152]{1,0:T(8,128)(2,1)} %get-tuple-element.50), channel_id=1, source_target_pairs={{0,2},{2,0},{4,6},{6,4},{8,10},{10,8},{12,14},{14,12},{16,18},{18,... | collective-permute-start | bytes 884744 | tf_op jit(solution)/shard_map/ppermute | solution.py:388
  86.3 17.1 %collective-permute-start.21 = (bf16[128,1152]{1,0:T(8,128)(2,1)}, bf16[128,1152]{1,0:T(8,128)(2,1)S(1)}, u32[]{:S(2)}, u32[]{:S(2)}) collective-permute-start(bf16[128,1152]{1,0:T(8,128)(2,1)} %get-tuple-element.51), channel_id=1, source_target_pairs={{0,4},{2,6},{4,0},{6,2},{8,12},{10,14},{12,8},{14,10},{16,20},{18,... | collective-permute-start | bytes 884744 | tf_op jit(solution)/shard_map/ppermute | solution.py:388
  90.0 15.8 %collective-permute-start.22 = (bf16[128,1152]{1,0:T(8,128)(2,1)}, bf16[128,1152]{1,0:T(8,128)(2,1)S(1)}, u32[]{:S(2)}, u32[]{:S(2)}) collective-permute-start(bf16[128,1152]{1,0:T(8,128)(2,1)} %get-tuple-element.52), channel_id=1, source_target_pairs={{0,6},{2,4},{4,2},{6,0},{8,14},{10,12},{12,10},{14,8},{16,22},{18,... | collective-permute-start | bytes 884744 | tf_op jit(solution)/shard_map/ppermute | solution.py:388
  96.2 52.9 %collective-permute-start.3 = (bf16[512,1152]{1,0:T(8,128)(2,1)}, bf16[512,1152]{1,0:T(8,128)(2,1)}, u32[]{:S(2)}, u32[]{:S(2)}) collective-permute-start(bf16[512,1152]{1,0:T(8,128)(2,1)} %pad_maximum_fusion), channel_id=1, source_target_pairs={{0,24},{24,0},{1,25},{25,1},{2,26},{26,2},{3,27},{27,3},{4,28},{28... | collective-permute-start | bytes 3538952 | tf_op jit(solution)/shard_map/ppermute | solution.py:445
  104.1 16.6 %collective-permute-start.17 = (bf16[256,1152]{1,0:T(8,128)(2,1)}, bf16[256,1152]{1,0:T(8,128)(2,1)}, u32[]{:S(2)}, u32[]{:S(2)}) collective-permute-start(bf16[256,1152]{1,0:T(8,128)(2,1)} %get-tuple-element.46), channel_id=1, source_target_pairs={{0,2},{2,0},{4,6},{6,4},{8,10},{10,8},{12,14},{14,12},{16,18},{18,... | collective-permute-start | bytes 1769480 | tf_op jit(solution)/shard_map/ppermute | solution.py:388
  106.5 28.6 %collective-permute-start.18 = (bf16[256,1152]{1,0:T(8,128)(2,1)}, bf16[256,1152]{1,0:T(8,128)(2,1)}, u32[]{:S(2)}, u32[]{:S(2)}) collective-permute-start(bf16[256,1152]{1,0:T(8,128)(2,1)} %get-tuple-element.47), channel_id=1, source_target_pairs={{0,4},{2,6},{4,0},{6,2},{8,12},{10,14},{12,8},{14,10},{16,20},{18,... | collective-permute-start | bytes 1769480 | tf_op jit(solution)/shard_map/ppermute | solution.py:388
  107.0 28.9 %collective-permute-start.19 = (bf16[256,1152]{1,0:T(8,128)(2,1)}, bf16[256,1152]{1,0:T(8,128)(2,1)}, u32[]{:S(2)}, u32[]{:S(2)}) collective-permute-start(bf16[256,1152]{1,0:T(8,128)(2,1)} %get-tuple-element.48), channel_id=1, source_target_pairs={{0,6},{2,4},{4,2},{6,0},{8,14},{10,12},{12,10},{14,8},{16,22},{18,... | collective-permute-start | bytes 1769480 | tf_op jit(solution)/shard_map/ppermute | solution.py:388
  118.1 26.5 %collective-permute-start.14 = (bf16[128,1152]{1,0:T(8,128)(2,1)S(1)}, bf16[128,1152]{1,0:T(8,128)(2,1)S(1)}, u32[]{:S(2)}, u32[]{:S(2)}) collective-permute-start(bf16[128,1152]{1,0:T(8,128)(2,1)S(1)} %get-tuple-element.42), channel_id=1, source_target_pairs={{0,2},{2,0},{4,6},{6,4},{8,10},{10,8},{12,14},{14,12},{16,18},{18,... | collective-permute-start | bytes 884744 | tf_op jit(solution)/shard_map/ppermute | solution.py:388
  120.7 23.9 %collective-permute-start.15 = (bf16[128,1152]{1,0:T(8,128)(2,1)S(1)}, bf16[128,1152]{1,0:T(8,128)(2,1)S(1)}, u32[]{:S(2)}, u32[]{:S(2)}) collective-permute-start(bf16[128,1152]{1,0:T(8,128)(2,1)S(1)} %get-tuple-element.43), channel_id=1, source_target_pairs={{0,4},{2,6},{4,0},{6,2},{8,12},{10,14},{12,8},{14,10},{16,20},{18,... | collective-permute-start | bytes 884744 | tf_op jit(solution)/shard_map/ppermute | solution.py:388
  135.1 9.5 %collective-permute-start.16 = (bf16[128,1152]{1,0:T(8,128)(2,1)S(1)}, bf16[128,1152]{1,0:T(8,128)(2,1)S(1)}, u32[]{:S(2)}, u32[]{:S(2)}) collective-permute-start(bf16[128,1152]{1,0:T(8,128)(2,1)S(1)} %get-tuple-element.44), channel_id=1, source_target_pairs={{0,6},{2,4},{4,2},{6,0},{8,14},{10,12},{12,10},{14,8},{16,22},{18,... | collective-permute-start | bytes 884744 | tf_op jit(solution)/shard_map/ppermute | solution.py:388
  155.3 3.8 %collective-permute-start.23 = (f32[584,768]{1,0:T(8,128)S(1)}, f32[584,768]{1,0:T(8,128)S(1)}, u32[]{:S(2)}, u32[]{:S(2)}) collective-permute-start(f32[584,768]{1,0:T(8,128)S(1)} %get-tuple-element.60), channel_id=1, source_target_pairs={{0,1},{1,0},{2,3},{3,2},{4,5},{5,4},{6,7},{7,6},{8,9},{9,8},{10,11... | collective-permute-start | bytes 5382152 | tf_op jit(solution)/shard_map/ppermute | solution.py:515
  (19 other events, 116.6 us)

commit v3 on v2

--- a/solution.py
+++ b/solution.py
@@ -12,12 +12,18 @@
 learn_rate = 0.001
 epsilon = 1e-08
 swap = [(0, 1), (1, 0)]
+PB, PC, LA, LB, LC, LF = (0, 10, 0, 40, 20, 0)
+bf16 = jnp.bfloat16
 MIB = 1024 * 1024
 ANY = pl.BlockSpec(memory_space=pl.ANY)
 VMEM = pl.BlockSpec(memory_space=pltpu.VMEM)
+HBM = pl.BlockSpec(memory_space=pltpu.HBM)
 SMEM = pl.BlockSpec(memory_space=pltpu.SMEM)
 f32 = jnp.float32
-bf16 = jnp.bfloat16
+
+
+def spent(us):
+    return pl.CostEstimate(flops=int(us * 1150000000) + 1, bytes_accessed=1, transcendentals=0)
 
 
 def params(mib):
@@ -32,10 +38,12 @@
     return 0.5 * jnp.tanh(0.5 * x) + 0.5
 
 
-def marks_kernel(owners, unit, cov_ref, lab_ref, out_ref):
+def shard_kernel(owners, cov_ref, lab_ref, own_ref, out_ref, mark_ref, sems):
     per_block, blocks = cov_ref.shape
     rows_block = lab_ref.shape[1]
     rows = blocks * rows_block
+    load = pltpu.make_async_copy(own_ref, out_ref.at[pl.ds(0, rows)], sems.at[0])
+    load.start()
     cov = cov_ref[...]
     heads_at = lax.broadcasted_iota(jnp.int32, (owners, blocks), 0)
     named = (cov[0:1] == heads_at).astype(f32)
@@ -50,123 +58,209 @@
     row_in = lax.broadcasted_iota(jnp.int32, (rows_block, rows), 1) % rows_block
     row_at = lax.broadcasted_iota(jnp.int32, (rows_block, rows), 0)
     head_rows = lax.broadcasted_iota(jnp.int32, (owners, rows), 0).astype(f32)
+    at_mark = lax.broadcasted_iota(jnp.int32, (16, rows), 0)
+    mark_rows = jnp.zeros((16, rows), f32)
     for t in range(per_block):
         mine = cov_rows[t : t + 1]
         own_rank = jnp.sum(jnp.where(mine == head_rows, rank, 0.0), axis=0, keepdims=True)
-        out_ref[t : t + 1, :] = (
-            mine * unit + own_rank * rows_block + row_in[0:1].astype(f32)
+        place = own_rank * rows_block + row_in[0:1].astype(f32)
+        spread = jnp.dot(lab_ref[t].astype(f32).astype(bf16), same, preferred_element_type=f32)
+        label = 1.0 + jnp.sum(jnp.where(row_in == row_at, spread, 0.0), axis=0, keepdims=True)
+        mark_rows = jnp.where(at_mark == t, mine, mark_rows)
+        mark_rows = jnp.where(at_mark == per_block + t, place, mark_rows)
+        mark_rows = jnp.where(at_mark == 2 * per_block + t, label, mark_rows)
+    mark_ref[...] = jnp.zeros(mark_ref.shape, bf16)
+    mark_ref[:, 0:rows] = mark_rows.astype(bf16)
+    store = pltpu.make_async_copy(mark_ref, out_ref.at[pl.ds(rows, 16)], sems.at[1])
+    store.start()
+    load.wait()
+    store.wait()
+
+
+def make_shard(own, coverage, labels, owners):
+    rows, feature = own.shape
+    return pl.pallas_call(
+        functools.partial(shard_kernel, owners),
+        out_shape=sds((rows + 16, feature), bf16),
+        in_specs=[VMEM, VMEM, HBM],
+        out_specs=HBM,
+        scratch_shapes=[pltpu.VMEM((16, feature), bf16), pltpu.SemaphoreType.DMA((2,))],
+        compiler_params=params(8),
+        name="shard",
+    )(coverage.T, labels.transpose(1, 2, 0), own)
+
+
+def pick_rows(marks, shard, heads, unit, per_block):
+    rows = marks.shape[1]
+    slot = lax.broadcasted_iota(jnp.int32, (unit, rows), 0).astype(f32)
+    at_head = lax.broadcasted_iota(jnp.int32, (8, rows), 0)
+    chosen = []
+    labels = jnp.zeros((8, rows), f32)
+    for k, head in enumerate(heads):
+        place = jnp.full((1, rows), -1.0, f32)
+        label = jnp.zeros((1, rows), f32)
+        for t in range(per_block):
+            mine = marks[t : t + 1] == head
+            place = jnp.where(mine, marks[per_block + t : per_block + t + 1], place)
+            label = jnp.where(mine, marks[2 * per_block + t : 2 * per_block + t + 1], label)
+        chosen.append(jnp.where(place == slot, 1.0, 0.0).astype(bf16))
+        labels = jnp.where(at_head == k, label, labels)
+    chosen = jnp.concatenate(chosen, axis=0)
+    picked = jnp.dot(chosen, shard, preferred_element_type=f32).astype(bf16)
+    mark = lax.dot_general(
+        labels.astype(bf16), chosen, (((1,), (1,)), ((), ())), preferred_element_type=f32
+    )
+    return picked, mark
+
+
+def pick_kernel(unit, per_block, plan, n_shards, n_heads, at_ref, *refs):
+    shards, refs = refs[:n_shards], refs[n_shards:]
+    outs, refs = refs[:n_heads], refs[n_heads:]
+    held, ready, in_sems, out_sems = refs
+    units = len(plan)
+    rows = held.shape[1] - 16
+
+    for g, (yes, no) in enumerate(plan):
+        if yes == no:
+            pltpu.make_async_copy(shards[yes], held.at[g], in_sems.at[g]).start()
+        else:
+            flag = at_ref[units * n_heads + g] > 0
+
+            @pl.when(flag)
+            def _():
+                pltpu.make_async_copy(shards[yes], held.at[g], in_sems.at[g]).start()
+
+            @pl.when(jnp.logical_not(flag))
+            def _():
+                pltpu.make_async_copy(shards[no], held.at[g], in_sems.at[g]).start()
+
+    at_mark = lax.broadcasted_iota(jnp.int32, (16, unit), 0)
+    mark_rows = [jnp.zeros((16, unit), f32)] * n_heads
+    for g, (yes, _) in enumerate(plan):
+        pltpu.make_async_copy(shards[yes], held.at[g], in_sems.at[g]).wait()
+        marks = held[g, rows:, 0:rows].astype(f32)
+        wanted = [at_ref[g * n_heads + k].astype(f32) for k in range(n_heads)]
+        picked, mark = pick_rows(marks, held[g, 0:rows], wanted, unit, per_block)
+        for k in range(n_heads):
+            ready[k, g * unit : (g + 1) * unit, :] = picked[k * unit : (k + 1) * unit]
+            own_mark = mark[k : k + 1, k * unit : (k + 1) * unit]
+            mark_rows[k] = jnp.where(at_mark == g, own_mark, mark_rows[k])
+    for k in range(n_heads):
+        ready[k, units * unit :, :] = jnp.zeros((16, ready.shape[2]), bf16)
+        ready[k, units * unit :, 0:unit] = mark_rows[k].astype(bf16)
+        pltpu.make_async_copy(ready.at[k], outs[k], out_sems.at[k]).start()
+    for k in range(n_heads):
+        pltpu.make_async_copy(ready.at[k], outs[k], out_sems.at[k]).wait()
+
+
+def pick(unit, per_block, shards, plan, heads_at, flags, cost):
+    rows, feature = shards[0].shape
+    units = len(plan)
+    n_heads = len(heads_at) // units
+    size = units * unit + 16
+    return pl.pallas_call(
+        functools.partial(pick_kernel, unit, per_block, plan, len(shards), n_heads),
+        out_shape=[sds((size, feature), bf16)] * n_heads,
+        in_specs=[SMEM] + [HBM] * len(shards),
+        out_specs=[HBM] * n_heads,
+        scratch_shapes=[
+            pltpu.VMEM((units, rows, feature), bf16),
+            pltpu.VMEM((n_heads, size, feature), bf16),
+            pltpu.SemaphoreType.DMA((units,)),
+            pltpu.SemaphoreType.DMA((n_heads,)),
+        ],
+        compiler_params=params(16),
+        cost_estimate=spent(cost),
+        name="pick",
+    )(jnp.stack(heads_at + flags).astype(jnp.int32), *shards)
+
+
+def pack_kernel(unit, n, *refs):
+    parts, out_ref, mark_ref, all_ref, sems = refs[:n], *refs[n:]
+    loads = []
+    for k in range(n):
+        loads.append(
+            pltpu.make_async_copy(
+                parts[k].at[pl.ds(0, unit)], out_ref.at[pl.ds(k * unit, unit)], sems.at[0, k]
+            )
         )
-        spread = jnp.dot(lab_ref[t].astype(f32).astype(bf16), same, preferred_element_type=f32)
-        out_ref[per_block + t : per_block + t + 1, :] = 1.0 + jnp.sum(
-            jnp.where(row_in == row_at, spread, 0.0), axis=0, keepdims=True
+        loads.append(
+            pltpu.make_async_copy(
+                parts[k].at[pl.ds(unit, 16)], mark_ref.at[k], sems.at[1, k]
+            )
         )
-
-
-def make_marks(coverage, labels, owners, unit):
-    blocks, per_block = coverage.shape
-    rows = blocks * labels.shape[2]
+    for load in loads:
+        load.start()
+    for load in loads:
+        load.wait()
+    at_mark = lax.broadcasted_iota(jnp.int32, (16, unit), 0)
+    mark_rows = jnp.zeros((16, unit), f32)
+    for k in range(n):
+        marks = mark_ref[k, :, 0:unit].astype(f32)
+        mark_rows = jnp.where(at_mark == k, marks[0:1], mark_rows)
+    all_ref[...] = jnp.zeros(all_ref.shape, bf16)
+    all_ref[:, 0:unit] = mark_rows.astype(bf16)
+    store = pltpu.make_async_copy(all_ref, out_ref.at[pl.ds(n * unit, 16)], sems.at[0, n])
+    store.start()
+    store.wait()
+
+
+def pack(unit, parts):
+    feature = parts[0].shape[1]
+    n = len(parts)
     return pl.pallas_call(
-        functools.partial(marks_kernel, owners, unit),
-        out_shape=sds((2 * per_block, rows), f32),
-        in_specs=[VMEM, VMEM],
-        out_specs=VMEM,
+        functools.partial(pack_kernel, unit, n),
+        out_shape=sds((n * unit + 16, feature), bf16),
+        in_specs=[HBM] * n,
+        out_specs=HBM,
+        scratch_shapes=[
+            pltpu.VMEM((n, 16, feature), bf16),
+            pltpu.VMEM((16, feature), bf16),
+            pltpu.SemaphoreType.DMA((2, n + 1)),
+        ],
         compiler_params=params(8),
-        name="marks",
-    )(coverage.T, labels.transpose(1, 2, 0))
-
-
-def pick_rows(marks, shard, first_code, unit, per_block):
-    rows = marks.shape[1]
-    slot = lax.broadcasted_iota(jnp.int32, (unit, rows), 0).astype(f32) + first_code
-    chosen = marks[0:1] == slot
-    for t in range(1, per_block):
-        chosen = chosen | (marks[t : t + 1] == slot)
-    return jnp.dot(
-        jnp.where(chosen, 1.0, 0.0).astype(bf16), shard, preferred_element_type=f32
-    ).astype(bf16)
-
-
-def pick_kernel(plan, unit, per_block, n_shards, n_marks, at_ref, *refs):
-    shards, refs = refs[:n_shards], refs[n_shards:]
-    marks, refs = refs[:n_marks], refs[n_marks:]
-    n_heads = len(plan[0][2])
-    n_out = len(plan) * n_heads
-    outs, (held, sems) = refs[:-2], refs[-2:]
-    loads = []
-    for i in range(n_shards):
-        load = pltpu.make_async_copy(shards[i], held.at[i], sems.at[i])
-        load.start()
-        loads.append(load)
-    done = set()
-    for shard_at, mark_at, places in plan:
-        if shard_at not in done:
-            loads[shard_at].wait()
-            done.add(shard_at)
-        for slot, (out_at, row_at) in enumerate(places):
-            first_code = at_ref[mark_at * n_heads + slot].astype(f32)
-            outs[out_at][row_at : row_at + unit, :] = pick_rows(
-                marks[mark_at][...], held[shard_at], first_code, unit, per_block
-            )
-
-
-def pick_either_kernel(unit, per_block, n_heads, at_ref, left_ref, right_ref, marks_ref, *refs):
-    outs, (held, sem) = refs[:-2], refs[-2:]
-    use_left = at_ref[n_heads] > 0
-
-    @pl.when(use_left)
-    def _():
-        load = pltpu.make_async_copy(left_ref, held, sem)
-        load.start()
-        load.wait()
-
-    @pl.when(jnp.logical_not(use_left))
-    def _():
-        load = pltpu.make_async_copy(right_ref, held, sem)
-        load.start()
-        load.wait()
-
-    for slot in range(n_heads):
-        outs[slot][...] = pick_rows(
-            marks_ref[...], held[...], at_ref[slot].astype(f32), unit, per_block
-        )
-
-
-def learn_kernel(
-    unit, per_block, n_units, n_parts, last, with_total, half_rows,
-    at_ref, *refs
-):
+        name="pack",
+    )(*parts)
+
+
+def learn_kernel(unit, spots, n_parts, last, with_total, half_rows, at_ref, *refs):
     parts, refs = refs[:n_parts], refs[n_parts:]
-    marks_ref, w_ref, bias_ref, out_ref, refs = refs[0], refs[1], refs[2], refs[3], refs[4:]
+    w_ref, bias_ref, out_ref, refs = refs[0], refs[1], refs[2], refs[3:]
     if with_total:
         total_ref, vec_ref, refs = refs[0], refs[1], refs[2:]
     if last:
         kept_ref, given_ref, refs = refs[0], refs[1], refs[2:]
     else:
         new_total_ref, new_vec_ref, refs = refs[0], refs[1], refs[2:]
-    rows_ref, low_ref, target_ref, sems = refs
+    rows_ref, low_ref, mark_ref, target_ref, sems = refs
     rows_all, feature = rows_ref.shape
     loads = []
-    at = 0
     for i in range(n_parts):
-        size = parts[i].shape[0]
-        load = pltpu.make_async_copy(parts[i], rows_ref.at[pl.ds(at, size)], sems.at[i])
+        loads.append(
+            pltpu.make_async_copy(
+                parts[i].at[pl.ds(parts[i].shape[0] - 16, 16)], mark_ref.at[i], sems.at[0, i]
+            )
+        )
+    for u, (part, at, _) in enumerate(spots):
+        loads.append(
+            pltpu.make_async_copy(
+                parts[part].at[pl.ds(at, unit)],
+                rows_ref.at[pl.ds(u * unit, unit)],
+                sems.at[1, u],
+            )
+        )
+    for load in loads:
         load.start()
-        loads.append(load)
-        at += size
-    first_code = at_ref[0].astype(f32)
-    for u in range(n_units):
-        source = at_ref[1 + u]
-        real = at_ref[1 + n_units + u].astype(f32)
-        marks = marks_ref[source]
-        slot = lax.broadcasted_iota(jnp.int32, (unit, marks.shape[1]), 0).astype(f32) + first_code
-        found = jnp.zeros(slot.shape, f32)
-        for t in range(per_block):
-            found = found + jnp.where(
-                marks[t : t + 1] == slot, marks[per_block + t : per_block + t + 1], 0.0
-            )
-        target_ref[u * unit : (u + 1) * unit, :] = jnp.sum(found, axis=1, keepdims=True) * real
     for load in loads:
         load.wait()
+    eye = lax.broadcasted_iota(jnp.int32, (unit, unit), 0) == lax.broadcasted_iota(
+        jnp.int32, (unit, unit), 1
+    )
+    for u, (part, _, mark_at) in enumerate(spots):
+        marks = mark_ref[part, :, 0:unit].astype(f32)[mark_at : mark_at + 1]
+        target_ref[u * unit : (u + 1) * unit, :] = jnp.sum(
+            jnp.where(eye, marks, 0.0), axis=1, keepdims=True
+        ) * at_ref[1].astype(f32)
     bias = bias_ref[...].astype(f32)
     out_weight = out_ref[...].astype(f32)
     step = 2 * unit
@@ -211,7 +305,7 @@
         new_vec_ref[0:1, :] = grad_bias
         new_vec_ref[1:2, :] = grad_out
         return
-    rep = at_ref[1 + 2 * n_units]
+    rep = at_ref[0]
     given_ref[half_rows : half_rows + 8, :] = jnp.zeros((8, hid), f32)
     kept_ref[half_rows : half_rows + 8, :] = jnp.zeros((8, hid), f32)
     for ref in (given_ref, kept_ref):
@@ -236,9 +330,9 @@
                 kept_ref[first + cut - half_rows : first + tile - half_rows, :] = piece[cut:]
 
 
-def learn(unit, per_block, n_units, parts, at, marks, w, bias, out, total, last):
+def learn(unit, spots, parts, at, w, bias, out, total, cost, last):
     feature, hid = w.shape
-    rows_all = sum(p.shape[0] for p in parts)
+    rows_all = len(spots) * unit
     half = feature // 2
     if last:
         outs = (sds((half + 8, hid), f32), sds((half + 8, hid), f32))
@@ -246,27 +340,24 @@
         outs = (sds((feature, hid), f32), sds((2, hid), f32))
     extra = () if total is None else total
     kernel = functools.partial(
-        learn_kernel, unit, per_block, n_units, len(parts), last, total is not None, half
+        learn_kernel, unit, spots, len(parts), last, total is not None, half
     )
     return pl.pallas_call(
         kernel,
         out_shape=outs,
-        in_specs=[SMEM] + [ANY] * len(parts) + [VMEM] * (4 + len(extra)),
+        in_specs=[SMEM] + [HBM] * len(parts) + [VMEM] * (3 + len(extra)),
         out_specs=(VMEM, VMEM),
         scratch_shapes=[
             pltpu.VMEM((rows_all, feature), bf16),
             pltpu.VMEM((rows_all, hid), bf16),
+            pltpu.VMEM((len(parts), 16, feature), bf16),
             pltpu.VMEM((rows_all, 1), f32),
-            pltpu.SemaphoreType.DMA((len(parts),)),
+            pltpu.SemaphoreType.DMA((2, max(len(parts), len(spots)))),
         ],
-        compiler_params=params(32),
-        cost_estimate=pl.CostEstimate(
-            flops=4 * rows_all * feature * hid,
-            bytes_accessed=4 * rows_all * feature + 10 * feature * hid,
-            transcendentals=rows_all * hid,
-        ),
+        compiler_params=params(24),
+        cost_estimate=spent(cost),
         name="learn",
-    )(at, *parts, marks, w, bias, out, *extra)
+    )(at, *parts, w, bias, out, *extra)
 
 
 def adam(old, grad, first, second):
@@ -328,7 +419,7 @@
             sds((1, 2, hid), f32),
             sds((1, 2, hid), f32),
         ),
-        compiler_params=params(24),
+        compiler_params=params(16),
         name="step",
     )(rep, kept, got, kept, got, w_in, first_w, second_w, vec_old, first_vec, second_vec)
 
@@ -368,149 +459,89 @@
     slots = 2 * blocks * per_block // owners
     unit = slots * rows_block
     rows = blocks * rows_block
-    hid = w_in.shape[2]
-    i32 = jnp.int32
-
     def right_pairs(hop):
         return [(i, i + 1) for i in range(hop - 1, planes - 1)]
 
     def left_pairs(hop):
         return [(i + 1, i) for i in range(planes - hop)]
 
-    head_pairs = [[(i, i ^ k) for i in range(heads)] for k in range(heads)]
-
-    def pair_up(k, ends):
-        wanted = (0, planes - 1) if ends else range(planes)
-        return [(p * heads + i, p * heads + (i ^ k)) for p in wanted for i in range(heads)]
-
-    def exchange(units, ends=False):
+    def exchange(units):
         return [units[0]] + [
-            lax.ppermute(units[k], ("dp", "head"), pair_up(k, ends)) for k in range(1, heads)
+            lax.ppermute(units[k], "head", [(i, i ^ k) for i in range(heads)])
+            for k in range(1, heads)
         ]
 
-    def codes(plane):
-        return [(plane * heads + (q ^ k)) * unit for k in range(heads)]
-
-    own = embeddings.reshape(rows, feature)
-    marks_own = make_marks(coverage, labels, owners, unit)
-
-    hops_right, hops_left = [own], [own]
+    def plane_heads(plane, real=None):
+        found = [plane * heads + (q ^ k) for k in range(heads)]
+        return found if real is None else [jnp.where(real, h, -1) for h in found]
+
+    own = make_shard(embeddings.reshape(rows, feature), coverage, labels, owners)
+    right = lax.ppermute(own, "dp", right_pairs(1))
+    left = lax.ppermute(own, "dp", left_pairs(1))
+    always = jnp.ones((), jnp.bool_)
+    at_end = (z == 0) | (z == planes - 1)
+
+    def add(total, parts, spots, real, cost, last=False):
+        scalars = jnp.stack([rep[0], real]).astype(jnp.int32)
+        return learn(unit, spots, parts, scalars, w_in[0], bias_in, w_out, total, cost, last)
+
+    first_heads = plane_heads(jnp.where(at_end, planes - 1 - z, z))
+    first_units = exchange(pick(unit, per_block, [own], [(0, 0)], first_heads, [always], 0))
+    far_sent = pack(unit, first_units)
+    one = jnp.ones((), jnp.int32)
+    first_spots = [(k, 0, 0) for k in range(heads)]
+    middle = 1 - at_end.astype(jnp.int32)
+    rest = []
     for hop in range(1, planes - 1):
-        hops_right.append(lax.ppermute(hops_right[-1], "dp", right_pairs(hop)))
-        hops_left.append(lax.ppermute(hops_left[-1], "dp", left_pairs(hop)))
-
-    marks_z = [marks_own] + [
-        lax.ppermute(marks_own, "dp", [(i, (i + s) % planes) for i in range(planes)])
-        for s in range(1, planes)
-    ]
-    marks_plane = jnp.stack(marks_z)
-    marks_all = jnp.stack(
-        [marks_plane]
-        + [lax.ppermute(marks_plane, "head", head_pairs[k]) for k in range(1, heads)]
-    ).reshape(heads * planes, 2 * per_block, rows)
-
-    def pick(shards, marks, plan, scalars, out_rows):
-        kernel = functools.partial(
-            pick_kernel, plan, unit, per_block, len(shards), len(marks)
-        )
-        return pl.pallas_call(
-            kernel,
-            out_shape=[sds((r, feature), bf16) for r in out_rows],
-            in_specs=[SMEM] + [ANY] * len(shards) + [VMEM] * len(marks),
-            out_specs=[VMEM] * len(out_rows),
-            scratch_shapes=[
-                pltpu.VMEM((len(shards), rows, feature), bf16),
-                pltpu.SemaphoreType.DMA((len(shards),)),
-            ],
-            compiler_params=params(32),
-            cost_estimate=pl.CostEstimate(
-                flops=2 * sum(out_rows) * rows * feature,
-                bytes_accessed=2 * feature * (sum(out_rows) + rows * len(shards)),
-                transcendentals=0,
-            ),
-            name="pick",
-        )(jnp.stack(scalars).astype(i32), *shards, *marks)
-
-    far = planes - 1 - z
-    plan = [
-        (0, 1, [(heads + k, 0) for k in range(heads)]),
-        (0, 0, [(k, 0) for k in range(heads)]),
-    ]
-    picked = pick(
-        [own], [marks_own, marks_own], plan, codes(z) + codes(far), [unit] * (2 * heads)
-    )
-    far_units = exchange(picked[heads:], ends=True)
-    own_units = exchange(picked[:heads])
-    far_sent = jnp.concatenate(far_units)
-    far_got = lax.ppermute(far_sent, "dp", [(0, planes - 1), (planes - 1, 0)])
-
-    one = jnp.ones((), i32)
-    groups = [(own_units, [(k, jnp.zeros((), i32), one) for k in range(heads)])]
-    for hop in range(1, planes - 1):
-        from_left = (z >= hop).astype(i32)
-        from_right = (z + hop < planes).astype(i32)
+        from_left = z >= hop
+        from_right = z + hop < planes
+        if hop + 1 < planes - 1:
+            right, left, far_sent = lax.optimization_barrier((right, left, far_sent))
+            next_right = lax.ppermute(right, "dp", right_pairs(hop + 1))
+            next_left = lax.ppermute(left, "dp", left_pairs(hop + 1))
+        else:
+            next_right, next_left = None, None
+        if hop == planes - 2 and hop > 1:
+            far_sent, right, left, *total = lax.optimization_barrier(
+                (far_sent, right, left, *total)
+            )
+            far_got = lax.ppermute(far_sent, "dp", [(0, planes - 1), (planes - 1, 0)])
         if 2 * hop < planes:
-            plan = [
-                (0, 0, [(k, 0) for k in range(heads)]),
-                (1, 1, [(k, unit) for k in range(heads)]),
-            ]
-            absent = -2 * unit * jnp.ones((), i32)
-            scalars = [jnp.where(from_left > 0, c, absent) for c in codes(z)]
-            scalars += [jnp.where(from_right > 0, c, absent) for c in codes(z)]
-            got = exchange(
-                pick(
-                    [hops_right[hop], hops_left[hop]],
-                    [marks_z[hop], marks_z[planes - hop]],
-                    plan,
-                    scalars,
-                    [2 * unit] * heads,
-                )
+            fill = hop == 1
+            messages = pick(
+                unit,
+                per_block,
+                [right, left, own],
+                [(0, 2), (1, 2)],
+                plane_heads(z, from_left | fill) + plane_heads(z, from_right | fill),
+                [from_left, from_right],
+                PB,
             )
-            sources = []
-            for k in range(heads):
-                sources.append((k, jnp.full((), hop, i32), from_left))
-                sources.append((k, jnp.full((), planes - hop, i32), from_right))
+            units = 2
         else:
-            use_left = from_right
-            back = jnp.where(use_left > 0, planes - hop, hop).astype(i32)
-            marks_hop = jnp.where(use_left > 0, marks_z[planes - hop], marks_z[hop])
-            scalars = jnp.stack(codes(z) + [use_left]).astype(i32)
-            got = exchange(
-                pl.pallas_call(
-                    functools.partial(pick_either_kernel, unit, per_block, heads),
-                    out_shape=[sds((unit, feature), bf16)] * heads,
-                    in_specs=[SMEM, ANY, ANY, VMEM],
-                    out_specs=[VMEM] * heads,
-                    scratch_shapes=[
-                        pltpu.VMEM((rows, feature), bf16),
-                        pltpu.SemaphoreType.DMA(()),
-                    ],
-                    compiler_params=params(32),
-                    cost_estimate=pl.CostEstimate(
-                        flops=2 * heads * unit * rows * feature,
-                        bytes_accessed=2 * feature * (heads * unit + rows),
-                        transcendentals=0,
-                    ),
-                    name="pick",
-                )(scalars, hops_left[hop], hops_right[hop], marks_hop)
+            messages = pick(
+                unit,
+                per_block,
+                [left, right],
+                [(0, 1)],
+                plane_heads(z, from_left | from_right),
+                [from_right],
+                PC,
             )
-            sources = [(k, back, from_left | from_right) for k in range(heads)]
-        groups.append((got, sources))
-    at_end = ((z == 0) | (z == planes - 1)).astype(i32)
-    far_back = jnp.where(z == 0, 1, planes - 1).astype(i32)
-    groups.append(([far_got], [(k, far_back, at_end) for k in range(heads)]))
-
-    total = None
-    my_code = (z * heads + q) * unit
-    for at, (parts, sources) in enumerate(groups):
-        scalars = [my_code]
-        scalars += [k * planes + back for k, back, _ in sources]
-        scalars += [real for _, _, real in sources]
-        scalars += [rep[0]]
-        total = learn(
-            unit, per_block, len(sources), parts, jnp.stack(scalars).astype(i32), marks_all,
-            w_in[0], bias_in, w_out, total, at == len(groups) - 1,
-        )
+            units = 1
+        where = [(k, g * unit, g) for k in range(heads) for g in range(units)]
+        if hop == 1:
+            first_units = lax.optimization_barrier((*first_units, *messages))[:heads]
+            total = add(None, first_units, first_spots, middle, LA)
+        else:
+            messages = lax.optimization_barrier((*messages, *rest[-1][0]))[:heads]
+        rest.append((exchange(messages), where))
+        right, left = next_right, next_left
+    rest.append(([far_got], [(0, k * unit, k) for k in range(heads)]))
+
+    for at, (parts, spots) in enumerate(rest):
+        cost = (LB, LC, LF)[min(at, 2)]
+        total = add(total, parts, spots, one, cost, at == len(rest) - 1)
     kept, given = total
     got = lax.ppermute(given, "rep", swap)
     vec_old = jnp.concatenate([bias_in, w_out])

time: 167 us -> 119 us (0.71)
  waiting for transfers between devices: 72.9 us -> 53 us
  starting transfers between devices: 43.1 us -> 23.2 us
  local copies, waits for them, and re-layouts: 9.18 us -> 3.95 us
  other arithmetic: 2.21 us -> 0.16 us
    ppermute x22 -> x13, waiting for transfers between devices: 66.9 us -> 42.7 us  [the longest x9 18.3 us: exchange(): lax.ppermute(units[k], 'head', [(i, i ^ k) for i in range(heads)])]
    ppermute x22 -> x13, starting transfers between devices: 41 us -> 20.9 us  [the longest x9 10.7 us: exchange(): lax.ppermute(units[k], 'head', [(i, i ^ k) for i in range(heads)])]
    unnamed x36 -> x24, local copies, waits for them, and re-layouts: 8.57 us -> 3.69 us
    ppermute x1, waiting for transfers between devices: 0.01 us -> 4.27 us  [gathered(): far_got = lax.ppermute(far_sent, 'dp', [(0, planes - 1), (planes - 1, 0)])]
    concatenate x1 -> x0, other arithmetic: 2.15 us -> none  [gathered(): far_sent = jnp.concatenate(far_units)]
    pallas_call x8 -> x9, Pallas kernels: 33.3 us -> 32.8 us  [the longest x4 22.3 us: learn(): pl.pallas_call(kernel, out_shape=outs, in_specs=[SMEM] + [HBM] * len(part...]
  transfers between devices with their start and end apart: 25 -> 16, of which waited for: 11 -> 9; matrix products, arithmetic and copies ran while one was open for 2% -> 0% of each run, Pallas kernels for 16% -> 23%
where the time goes in v3:
time: 119 us; the launch traced here: 118 us
  waiting for transfers between devices  53 us (45%)
  Pallas kernels  37 us (31%)
  starting transfers between devices  23.2 us (19%)
  local copies, waits for them, and re-layouts  3.95 us (3%)
    pallas_call x4, Pallas kernels, learn(): pl.pallas_call(kernel, out_shape=outs, in_specs=[SMEM] + [HBM] * len(part...  22.3 us
    ppermute x9, waiting for transfers between devices, exchange(): lax.ppermute(units[k], 'head', [(i, i ^ k) for i in range(heads)])  18.3 us
    ppermute x1, waiting for transfers between devices, gathered(): next_left = lax.ppermute(left, 'dp', left_pairs(hop + 1))  17.2 us
    ppermute x9, starting transfers between devices, exchange(): lax.ppermute(units[k], 'head', [(i, i ^ k) for i in range(heads)])  10.7 us
    pallas_call x3, Pallas kernels, pick(): pl.pallas_call(functools.partial(pick_kernel, unit, per_block, plan, len(...  9.48 us
    ppermute x1, starting transfers between devices, gathered(): right = lax.ppermute(own, 'dp', right_pairs(1))  5.98 us
    ppermute x1, waiting for transfers between devices, gathered(): left = lax.ppermute(own, 'dp', left_pairs(1))  5.25 us
    ppermute x1, waiting for transfers between devices, gathered(): far_got = lax.ppermute(far_sent, 'dp', [(0, planes - 1), (planes - 1, 0)])  4.27 us
  transfers between devices with their start and end apart: 16, of which 9 were waited for; matrix products, arithmetic and copies ran while one was open for 0% of the time, Pallas kernels for 23%

profile of v3, /device:TPU:0, one launch (start us, length us, event | category | flops | bytes accessed | tf_op | source)
XLA Modules:
  0.0 118.4 jit_solution(10290398697789588147)
XLA Ops:
  3.8 6.0 %collective-permute-start = (bf16[528,1152]{1,0:T(8,128)(2,1)S(1)}, bf16[528,1152]{1,0:T(8,128)(2,1)}, u32[]{:S(2)}, u32[]{:S(2)}) collective-permute-start(bf16[528,1152]{1,0:T(8,128)(2,1)S(1)} %shard.1.refs_0_.refs_2_), channel_id=1, source_target_pairs={{0,8},{8,16},{16,24},{1,9},{9,17},{17,25},{2,10},{10,18},{18,26},{... | collective-permute-start | bytes 3649544 | tf_op jit(solution)/shard_map/ppermute | solution.py:479
  11.1 2.3 %pick.3 = (bf16[144,1152]{1,0:T(8,128)(2,1)S(1)}, bf16[144,1152]{1,0:T(8,128)(2,1)S(1)}, bf16[144,1152]{1,0:T(8,128)(2,1)S(1)}, bf16[144,1152]{1,0:T(8,128)(2,1)S(1)}) custom-call(s32[5]{0:T(128)S(1)} %stack.83.at_ref, bf16[528,1152]{1,0:T(8,128)(2,1)S(1)} %shard.1.refs_0_.refs_2_), custom_call_target="tpu_custom_call" | custom-call | flops 1 | bytes 1 | tf_op jit(solution)/shard_map/pick/pallas_call | solution.py:161
  13.4 1.6 %collective-permute-start.2 = (bf16[144,1152]{1,0:T(8,128)(2,1)S(1)}, bf16[144,1152]{1,0:T(8,128)(2,1)S(1)}, u32[]{:S(2)}, u32[]{:S(2)}) collective-permute-start(bf16[144,1152]{1,0:T(8,128)(2,1)S(1)} %get-tuple-element.50), channel_id=1, source_target_pairs={{0,2},{2,0},{4,6},{6,4},{1,3},{3,1},{5,7},{7,5},{8,10},{10,8},{12,... | collective-permute-start | bytes 995336 | tf_op jit(solution)/shard_map/ppermute | solution.py:470
  15.0 1.5 %collective-permute-start.3 = (bf16[144,1152]{1,0:T(8,128)(2,1)S(1)}, bf16[144,1152]{1,0:T(8,128)(2,1)S(1)}, u32[]{:S(2)}, u32[]{:S(2)}) collective-permute-start(bf16[144,1152]{1,0:T(8,128)(2,1)S(1)} %get-tuple-element.51), channel_id=1, source_target_pairs={{0,4},{2,6},{4,0},{6,2},{1,5},{3,7},{5,1},{7,3},{8,12},{10,14},{12... | collective-permute-start | bytes 995336 | tf_op jit(solution)/shard_map/ppermute | solution.py:470
  17.0 7.2 %collective-permute-done.2.refs_1_ = bf16[144,1152]{1,0:T(8,128)(2,1)S(1)} collective-permute-done((bf16[144,1152]{1,0:T(8,128)(2,1)S(1)}, bf16[144,1152]{1,0:T(8,128)(2,1)S(1)}, u32[]{:S(2)}, u32[]{:S(2)}) %collective-permute-start.2) | collective-permute-done | bytes 331808 | tf_op jit(solution)/shard_map/ppermute | solution.py:470
  24.2 6.9 %collective-permute-done.3.refs_2_ = bf16[144,1152]{1,0:T(8,128)(2,1)S(1)} collective-permute-done((bf16[144,1152]{1,0:T(8,128)(2,1)S(1)}, bf16[144,1152]{1,0:T(8,128)(2,1)S(1)}, u32[]{:S(2)}, u32[]{:S(2)}) %collective-permute-start.3) | collective-permute-done | bytes 331808 | tf_op jit(solution)/shard_map/ppermute | solution.py:470
  32.7 2.0 %collective-permute-done.refs_0_ = bf16[528,1152]{1,0:T(8,128)(2,1)} collective-permute-done((bf16[528,1152]{1,0:T(8,128)(2,1)S(1)}, bf16[528,1152]{1,0:T(8,128)(2,1)}, u32[]{:S(2)}, u32[]{:S(2)}) %collective-permute-start) | collective-permute-done | bytes 1216544 | tf_op jit(solution)/shard_map/ppermute | solution.py:479
  34.7 5.2 %collective-permute-done.1.refs_1_ = bf16[528,1152]{1,0:T(8,128)(2,1)} collective-permute-done((bf16[528,1152]{1,0:T(8,128)(2,1)S(1)}, bf16[528,1152]{1,0:T(8,128)(2,1)}, u32[]{:S(2)}, u32[]{:S(2)}) %collective-permute-start.1) | collective-permute-done | bytes 1216544 | tf_op jit(solution)/shard_map/ppermute | solution.py:480
  39.9 1.7 %collective-permute-start.5 = (bf16[528,1152]{1,0:T(8,128)(2,1)}, bf16[528,1152]{1,0:T(8,128)(2,1)}, u32[]{:S(2)}, u32[]{:S(2)}) collective-permute-start(bf16[528,1152]{1,0:T(8,128)(2,1)} %collective-permute-done.refs_0_), channel_id=1, source_target_pairs={{8,16},{16,24},{9,17},{17,25},{10,18},{18,26},{11,19},{19,27},{12,... | collective-permute-start | bytes 3649544 | tf_op jit(solution)/shard_map/ppermute | solution.py:500
  43.3 3.9 %pick.4 = (bf16[272,1152]{1,0:T(8,128)(2,1)S(1)}, bf16[272,1152]{1,0:T(8,128)(2,1)S(1)}, bf16[272,1152]{1,0:T(8,128)(2,1)S(1)}, bf16[272,1152]{1,0:T(8,128)(2,1)S(1)}) custom-call(s32[10]{0:T(128)S(1)} %stack.94.at_ref, bf16[528,1152]{1,0:T(8,128)(2,1)} %collective-permute-done.refs_0_, bf16[528,1152]{1,0:T(8,128)(2,1)} %collective-permute-done.1.refs_1_, ...), custom_call_target="tpu_custom_call" | custom-call | flops 1 | bytes 1 | tf_op jit(solution)/shard_map/pick/pallas_call | solution.py:161
  47.2 1.6 %collective-permute-start.8 = (bf16[272,1152]{1,0:T(8,128)(2,1)S(1)}, bf16[272,1152]{1,0:T(8,128)(2,1)S(1)}, u32[]{:S(2)}, u32[]{:S(2)}) collective-permute-start(bf16[272,1152]{1,0:T(8,128)(2,1)S(1)} %get-tuple-element.57), channel_id=1, source_target_pairs={{0,2},{2,0},{4,6},{6,4},{1,3},{3,1},{5,7},{7,5},{8,10},{10,8},{12,... | collective-permute-start | bytes 1880072 | tf_op jit(solution)/shard_map/ppermute | solution.py:470
  50.7 4.5 %learn.4 = (f32[1152,768]{1,0:T(8,128)S(1)}, f32[2,768]{1,0:T(2,128)S(1)}) custom-call(s32[2]{0:T(128)S(1)} %pad_add_fusion.1.at_ref, bf16[144,1152]{1,0:T(8,128)(2,1)S(1)} %get-tuple-element.60.refs_0_, bf16[144,1152]{1,0:T(8,128)(2,1)S(1)} %collective-permute-done.2.refs_1_, bf16[144,1152]{1,0:T(8,128)(2,1)S(1)} %collective-permute-done.3.refs_2_, ...), custom_call_target="tpu_custom_call" | custom-call | flops 1 | bytes 1 | tf_op jit(solution)/shard_map/learn/pallas_call | solution.py:345
  55.3 17.2 %collective-permute-done.6.refs_0_ = bf16[528,1152]{1,0:T(8,128)(2,1)} collective-permute-done((bf16[528,1152]{1,0:T(8,128)(2,1)}, bf16[528,1152]{1,0:T(8,128)(2,1)}, u32[]{:S(2)}, u32[]{:S(2)}) %collective-permute-start.6) | collective-permute-done | bytes 1216544 | tf_op jit(solution)/shard_map/ppermute | solution.py:501
  72.5 2.1 %collective-permute-start.7 = (bf16[528,1152]{1,0:T(8,128)(2,1)S(1)}, bf16[528,1152]{1,0:T(8,128)(2,1)S(1)}, u32[]{:S(2)}, u32[]{:S(2)}) collective-permute-start(bf16[528,1152]{1,0:T(8,128)(2,1)S(1)} %copy-done.4), channel_id=1, source_target_pairs={{0,24},{24,0},{1,25},{25,1},{2,26},{26,2},{3,27},{27,3},{4,28},{28... | collective-permute-start | bytes 3649544 | tf_op jit(solution)/shard_map/ppermute | solution.py:508
  74.6 3.3 %pick.5 = (bf16[144,1152]{1,0:T(8,128)(2,1)S(1)}, bf16[144,1152]{1,0:T(8,128)(2,1)S(1)}, bf16[144,1152]{1,0:T(8,128)(2,1)S(1)}, bf16[144,1152]{1,0:T(8,128)(2,1)S(1)}) custom-call(s32[5]{0:T(128)S(1)} %stack.101.at_ref, bf16[528,1152]{1,0:T(8,128)(2,1)} %collective-permute-done.6.refs_0_, bf16[528,1152]{1,0:T(8,128)(2,1)} %collective-permute-done.5.refs_1_), custom_call_target="tpu_custom_call" | custom-call | flops 11500000256 | bytes 1 | tf_op jit(solution)/shard_map/pick/pallas_call | solution.py:161
  77.9 1.6 %collective-permute-start.11 = (bf16[144,1152]{1,0:T(8,128)(2,1)S(1)}, bf16[144,1152]{1,0:T(8,128)(2,1)S(1)}, u32[]{:S(2)}, u32[]{:S(2)}) collective-permute-start(bf16[144,1152]{1,0:T(8,128)(2,1)S(1)} %get-tuple-element.74), channel_id=1, source_target_pairs={{0,2},{2,0},{4,6},{6,4},{1,3},{3,1},{5,7},{7,5},{8,10},{10,8},{12,... | collective-permute-start | bytes 995336 | tf_op jit(solution)/shard_map/ppermute | solution.py:470
  81.5 8.1 %learn.5 = (f32[1152,768]{1,0:T(8,128)S(1)}, f32[2,768]{1,0:T(2,128)S(1)}) custom-call(s32[2]{0:T(128)S(1)} %pad_add_fusion.at_ref, bf16[272,1152]{1,0:T(8,128)(2,1)S(1)} %get-tuple-element.56.refs_0_, bf16[272,1152]{1,0:T(8,128)(2,1)S(1)} %collective-permute-done.8.refs_1_, bf16[272,1152]{1,0:T(8,128)(2,1)S(1)} %collective-permute-done.9.refs_2_, ...), custom_call_target="tpu_custom_call" | custom-call | flops 46000001024 | bytes 1 | tf_op jit(solution)/shard_map/learn/pallas_call | solution.py:345
  89.6 4.2 %collective-permute-done.12.refs_2_ = bf16[144,1152]{1,0:T(8,128)(2,1)S(1)} collective-permute-done((bf16[144,1152]{1,0:T(8,128)(2,1)S(1)}, bf16[144,1152]{1,0:T(8,128)(2,1)S(1)}, u32[]{:S(2)}, u32[]{:S(2)}) %collective-permute-start.12) | collective-permute-done | bytes 331808 | tf_op jit(solution)/shard_map/ppermute | solution.py:470
  93.7 4.5 %learn.6 = (f32[1152,768]{1,0:T(8,128)S(1)}, f32[2,768]{1,0:T(2,128)S(1)}) custom-call(s32[2]{0:T(128)S(1)} %pad_add_fusion.at_ref, bf16[144,1152]{1,0:T(8,128)(2,1)S(1)} %get-tuple-element.73.refs_0_, bf16[144,1152]{1,0:T(8,128)(2,1)S(1)} %collective-permute-done.11.refs_1_, bf16[144,1152]{1,0:T(8,128)(2,1)S(1)} %collective-permute-done.12.refs_2_, ...), custom_call_target="tpu_custom_call" | custom-call | flops 23000000512 | bytes 1 | tf_op jit(solution)/shard_map/learn/pallas_call | solution.py:345
  98.3 4.3 %collective-permute-done.7.refs_0_ = bf16[528,1152]{1,0:T(8,128)(2,1)S(1)} collective-permute-done((bf16[528,1152]{1,0:T(8,128)(2,1)S(1)}, bf16[528,1152]{1,0:T(8,128)(2,1)S(1)}, u32[]{:S(2)}, u32[]{:S(2)}) %collective-permute-start.7) | collective-permute-done | bytes 1216544 | tf_op jit(solution)/shard_map/ppermute | solution.py:508
  102.6 5.1 %learn.7 = (f32[584,768]{1,0:T(8,128)S(1)}, f32[584,768]{1,0:T(8,128)S(1)}) custom-call(s32[2]{0:T(128)S(1)} %pad_add_fusion.at_ref, bf16[528,1152]{1,0:T(8,128)(2,1)S(1)} %collective-permute-done.7.refs_0_, bf16[1152,768]{1,0:T(8,128)(2,1)S(1)} %bitcast.24, bf16[1,768]{1,0:T(2,128)(2,1)S(1)} %copy-done.6, bf16[1,768]{1,0:T(2,128)(2,1)S(1)} %copy-done.7, ...), custom_call_target="tpu_custom_call" | custom-call | flops 1 | bytes 1 | tf_op jit(solution)/shard_map/learn/pallas_call | solution.py:345
  107.8 3.7 %collective-permute-done.14.got.got_vec = f32[584,768]{1,0:T(8,128)S(1)} collective-permute-done((f32[584,768]{1,0:T(8,128)S(1)}, f32[584,768]{1,0:T(8,128)S(1)}, u32[]{:S(2)}, u32[]{:S(2)}) %collective-permute-start.14) | collective-permute-done | bytes 1794080 | tf_op jit(solution)/shard_map/ppermute | solution.py:546
  111.5 3.3 %step.1 = (bf16[576,768]{1,0:T(8,128)(2,1)S(1)}, bf16[1,1152,768]{2,1,0:T(8,128)(2,1)}, bf16[1,2,768]{2,1,0:T(2,128)(2,1)}, f32[1,576,768]{2,1,0:T(8,128)}, f32[...) custom-call(s32[1]{0:T(128)} %bitcast.at_ref, f32[584,768]{1,0:T(8,128)S(1)} %get-tuple-element.83.kept.kept_vec, ...), custom_call_target="tpu_custom_call" | custom-call | tf_op jit(solution)/shard_map/step/pallas_call | solution.py:405
  115.0 2.3 %collective-permute-done.15.other_ref = bf16[576,768]{1,0:T(8,128)(2,1)S(1)} collective-permute-done((bf16[576,768]{1,0:T(8,128)(2,1)S(1)}, bf16[576,768]{1,0:T(8,128)(2,1)S(1)}, u32[]{:S(2)}, u32[]{:S(2)}) %collective-permute-start.15) | collective-permute-done | bytes 884768 | tf_op jit(solution)/shard_map/ppermute | solution.py:551
  (49 shorter events, 13.4 us)
Async XLA Ops:
  3.8 30.9 %collective-permute-start = (bf16[528,1152]{1,0:T(8,128)(2,1)S(1)}, bf16[528,1152]{1,0:T(8,128)(2,1)}, u32[]{:S(2)}, u32[]{:S(2)}) collective-permute-start(bf16[528,1152]{1,0:T(8,128)(2,1)S(1)} %shard.1.refs_0_.refs_2_), channel_id=1, source_target_pairs={{0,8},{8,16},{16,24},{1,9},{9,17},{17,25},{2,10},{10,18},{18,26},{... | collective-permute-start | bytes 3649544 | tf_op jit(solution)/shard_map/ppermute | solution.py:479
  9.7 30.2 %collective-permute-start.1 = (bf16[528,1152]{1,0:T(8,128)(2,1)S(1)}, bf16[528,1152]{1,0:T(8,128)(2,1)}, u32[]{:S(2)}, u32[]{:S(2)}) collective-permute-start(bf16[528,1152]{1,0:T(8,128)(2,1)S(1)} %shard.1.refs_0_.refs_2_), channel_id=1, source_target_pairs={{8,0},{16,8},{24,16},{9,1},{17,9},{25,17},{10,2},{18,10},{26,18},{... | collective-permute-start | bytes 3649544 | tf_op jit(solution)/shard_map/ppermute | solution.py:480
  13.4 10.8 %collective-permute-start.2 = (bf16[144,1152]{1,0:T(8,128)(2,1)S(1)}, bf16[144,1152]{1,0:T(8,128)(2,1)S(1)}, u32[]{:S(2)}, u32[]{:S(2)}) collective-permute-start(bf16[144,1152]{1,0:T(8,128)(2,1)S(1)} %get-tuple-element.50), channel_id=1, source_target_pairs={{0,2},{2,0},{4,6},{6,4},{1,3},{3,1},{5,7},{7,5},{8,10},{10,8},{12,... | collective-permute-start | bytes 995336 | tf_op jit(solution)/shard_map/ppermute | solution.py:470
  15.0 16.1 %collective-permute-start.3 = (bf16[144,1152]{1,0:T(8,128)(2,1)S(1)}, bf16[144,1152]{1,0:T(8,128)(2,1)S(1)}, u32[]{:S(2)}, u32[]{:S(2)}) collective-permute-start(bf16[144,1152]{1,0:T(8,128)(2,1)S(1)} %get-tuple-element.51), channel_id=1, source_target_pairs={{0,4},{2,6},{4,0},{6,2},{1,5},{3,7},{5,1},{7,3},{8,12},{10,14},{12... | collective-permute-start | bytes 995336 | tf_op jit(solution)/shard_map/ppermute | solution.py:470
  16.5 14.6 %collective-permute-start.4 = (bf16[144,1152]{1,0:T(8,128)(2,1)S(1)}, bf16[144,1152]{1,0:T(8,128)(2,1)S(1)}, u32[]{:S(2)}, u32[]{:S(2)}) collective-permute-start(bf16[144,1152]{1,0:T(8,128)(2,1)S(1)} %get-tuple-element.52), channel_id=1, source_target_pairs={{0,6},{2,4},{4,2},{6,0},{1,7},{3,5},{5,3},{7,1},{8,14},{10,12},{12... | collective-permute-start | bytes 995336 | tf_op jit(solution)/shard_map/ppermute | solution.py:470
  39.9 15.3 %collective-permute-start.5 = (bf16[528,1152]{1,0:T(8,128)(2,1)}, bf16[528,1152]{1,0:T(8,128)(2,1)}, u32[]{:S(2)}, u32[]{:S(2)}) collective-permute-start(bf16[528,1152]{1,0:T(8,128)(2,1)} %collective-permute-done.refs_0_), channel_id=1, source_target_pairs={{8,16},{16,24},{9,17},{17,25},{10,18},{18,26},{11,19},{19,27},{12,... | collective-permute-start | bytes 3649544 | tf_op jit(solution)/shard_map/ppermute | solution.py:500
  41.6 30.9 %collective-permute-start.6 = (bf16[528,1152]{1,0:T(8,128)(2,1)}, bf16[528,1152]{1,0:T(8,128)(2,1)}, u32[]{:S(2)}, u32[]{:S(2)}) collective-permute-start(bf16[528,1152]{1,0:T(8,128)(2,1)} %collective-permute-done.1.refs_1_), channel_id=1, source_target_pairs={{8,0},{16,8},{9,1},{17,9},{10,2},{18,10},{11,3},{19,11},{12,4},{20... | collective-permute-start | bytes 3649544 | tf_op jit(solution)/shard_map/ppermute | solution.py:501
  43.3 7.4 %copy-start = (bf16[1,1152,768]{2,1,0:T(8,128)(2,1)S(1)}, bf16[1,1152,768]{2,1,0:T(8,128)(2,1)}, u32[]{:S(2)}) copy-start(bf16[1,1152,768]{2,1,0:T(8,128)(2,1)} %param.13) | copy-start | bytes 5308420
  43.3 7.5 %copy-start.6 = (bf16[1,768]{1,0:T(2,128)(2,1)S(1)}, bf16[1,768]{1,0:T(2,128)(2,1)}, u32[]{:S(2)}) copy-start(bf16[1,768]{1,0:T(2,128)(2,1)} %refs_2_.1) | copy-start | bytes 4612
  43.3 7.5 %copy-start.7 = (bf16[1,768]{1,0:T(2,128)(2,1)S(1)}, bf16[1,768]{1,0:T(2,128)(2,1)}, u32[]{:S(2)}) copy-start(bf16[1,768]{1,0:T(2,128)(2,1)} %refs_3_.1) | copy-start | bytes 4612
  47.2 25.3 %copy-start.4 = (bf16[528,1152]{1,0:T(8,128)(2,1)S(1)}, bf16[528,1152]{1,0:T(8,128)(2,1)}, u32[]{:S(2)}) copy-start(bf16[528,1152]{1,0:T(8,128)(2,1)} %copy-done.3) | copy-start | bytes 3649540
  47.2 30.7 %collective-permute-start.8 = (bf16[272,1152]{1,0:T(8,128)(2,1)S(1)}, bf16[272,1152]{1,0:T(8,128)(2,1)S(1)}, u32[]{:S(2)}, u32[]{:S(2)}) collective-permute-start(bf16[272,1152]{1,0:T(8,128)(2,1)S(1)} %get-tuple-element.57), channel_id=1, source_target_pairs={{0,2},{2,0},{4,6},{6,4},{1,3},{3,1},{5,7},{7,5},{8,10},{10,8},{12,... | collective-permute-start | bytes 1880072 | tf_op jit(solution)/shard_map/ppermute | solution.py:470
  48.7 29.2 %collective-permute-start.9 = (bf16[272,1152]{1,0:T(8,128)(2,1)S(1)}, bf16[272,1152]{1,0:T(8,128)(2,1)S(1)}, u32[]{:S(2)}, u32[]{:S(2)}) collective-permute-start(bf16[272,1152]{1,0:T(8,128)(2,1)S(1)} %get-tuple-element.58), channel_id=1, source_target_pairs={{0,4},{2,6},{4,0},{6,2},{1,5},{3,7},{5,1},{7,3},{8,12},{10,14},{12... | collective-permute-start | bytes 1880072 | tf_op jit(solution)/shard_map/ppermute | solution.py:470
  50.2 27.7 %collective-permute-start.10 = (bf16[272,1152]{1,0:T(8,128)(2,1)S(1)}, bf16[272,1152]{1,0:T(8,128)(2,1)S(1)}, u32[]{:S(2)}, u32[]{:S(2)}) collective-permute-start(bf16[272,1152]{1,0:T(8,128)(2,1)S(1)} %get-tuple-element.59), channel_id=1, source_target_pairs={{0,6},{2,4},{4,2},{6,0},{1,7},{3,5},{5,3},{7,1},{8,14},{10,12},{12... | collective-permute-start | bytes 1880072 | tf_op jit(solution)/shard_map/ppermute | solution.py:470
  72.5 30.1 %collective-permute-start.7 = (bf16[528,1152]{1,0:T(8,128)(2,1)S(1)}, bf16[528,1152]{1,0:T(8,128)(2,1)S(1)}, u32[]{:S(2)}, u32[]{:S(2)}) collective-permute-start(bf16[528,1152]{1,0:T(8,128)(2,1)S(1)} %copy-done.4), channel_id=1, source_target_pairs={{0,24},{24,0},{1,25},{25,1},{2,26},{26,2},{3,27},{27,3},{4,28},{28... | collective-permute-start | bytes 3649544 | tf_op jit(solution)/shard_map/ppermute | solution.py:508
  77.9 11.6 %collective-permute-start.11 = (bf16[144,1152]{1,0:T(8,128)(2,1)S(1)}, bf16[144,1152]{1,0:T(8,128)(2,1)S(1)}, u32[]{:S(2)}, u32[]{:S(2)}) collective-permute-start(bf16[144,1152]{1,0:T(8,128)(2,1)S(1)} %get-tuple-element.74), channel_id=1, source_target_pairs={{0,2},{2,0},{4,6},{6,4},{1,3},{3,1},{5,7},{7,5},{8,10},{10,8},{12,... | collective-permute-start | bytes 995336 | tf_op jit(solution)/shard_map/ppermute | solution.py:470
  79.5 14.3 %collective-permute-start.12 = (bf16[144,1152]{1,0:T(8,128)(2,1)S(1)}, bf16[144,1152]{1,0:T(8,128)(2,1)S(1)}, u32[]{:S(2)}, u32[]{:S(2)}) collective-permute-start(bf16[144,1152]{1,0:T(8,128)(2,1)S(1)} %get-tuple-element.75), channel_id=1, source_target_pairs={{0,4},{2,6},{4,0},{6,2},{1,5},{3,7},{5,1},{7,3},{8,12},{10,14},{12... | collective-permute-start | bytes 995336 | tf_op jit(solution)/shard_map/ppermute | solution.py:470
  81.0 12.7 %collective-permute-start.13 = (bf16[144,1152]{1,0:T(8,128)(2,1)S(1)}, bf16[144,1152]{1,0:T(8,128)(2,1)S(1)}, u32[]{:S(2)}, u32[]{:S(2)}) collective-permute-start(bf16[144,1152]{1,0:T(8,128)(2,1)S(1)} %get-tuple-element.76), channel_id=1, source_target_pairs={{0,6},{2,4},{4,2},{6,0},{1,7},{3,5},{5,3},{7,1},{8,14},{10,12},{12... | collective-permute-start | bytes 995336 | tf_op jit(solution)/shard_map/ppermute | solution.py:470
  102.6 9.0 %copy-start.1 = (f32[1,576,768]{2,1,0:T(8,128)S(1)}, f32[1,576,768]{2,1,0:T(8,128)}, u32[]{:S(2)}) copy-start(f32[1,576,768]{2,1,0:T(8,128)} %first_w.1) | copy-start | bytes 5308420
  102.6 9.0 %copy-start.2 = (f32[1,576,768]{2,1,0:T(8,128)S(1)}, f32[1,576,768]{2,1,0:T(8,128)}, u32[]{:S(2)}) copy-start(f32[1,576,768]{2,1,0:T(8,128)} %second_w.1) | copy-start | bytes 5308420
  102.6 9.0 %copy-start.9 = (f32[1,2,768]{2,1,0:T(2,128)S(1)}, f32[1,2,768]{2,1,0:T(2,128)}, u32[]{:S(2)}) copy-start(f32[1,2,768]{2,1,0:T(2,128)} %first_vec.1) | copy-start | bytes 18436
  102.6 9.0 %copy-start.10 = (f32[1,2,768]{2,1,0:T(2,128)S(1)}, f32[1,2,768]{2,1,0:T(2,128)}, u32[]{:S(2)}) copy-start(f32[1,2,768]{2,1,0:T(2,128)} %second_vec.1) | copy-start | bytes 18436
  107.7 3.8 %collective-permute-start.14 = (f32[584,768]{1,0:T(8,128)S(1)}, f32[584,768]{1,0:T(8,128)S(1)}, u32[]{:S(2)}, u32[]{:S(2)}) collective-permute-start(f32[584,768]{1,0:T(8,128)S(1)} %get-tuple-element.84), channel_id=1, source_target_pairs={{0,1},{1,0},{2,3},{3,2},{4,5},{5,4},{6,7},{7,6},{8,9},{9,8},{10,11... | collective-permute-start | bytes 5382152 | tf_op jit(solution)/shard_map/ppermute | solution.py:546
  114.8 2.5 %collective-permute-start.15 = (bf16[576,768]{1,0:T(8,128)(2,1)S(1)}, bf16[576,768]{1,0:T(8,128)(2,1)S(1)}, u32[]{:S(2)}, u32[]{:S(2)}) collective-permute-start(bf16[576,768]{1,0:T(8,128)(2,1)S(1)} %get-tuple-element.85), channel_id=1, source_target_pairs={{0,1},{1,0},{2,3},{3,2},{4,5},{5,4},{6,7},{7,6},{8,9},{9,8},{10,11... | collective-permute-start | bytes 2654216 | tf_op jit(solution)/shard_map/ppermute | solution.py:551
  (4 other events, 3.7 us)

commit v4 on v3

--- a/solution.py
+++ b/solution.py
@@ -15,6 +15,7 @@
 PB, PC, LA, LB, LC, LF = (0, 10, 0, 40, 20, 0)
 bf16 = jnp.bfloat16
 MIB = 1024 * 1024
+ROOM = 60
 ANY = pl.BlockSpec(memory_space=pl.ANY)
 VMEM = pl.BlockSpec(memory_space=pltpu.VMEM)
 HBM = pl.BlockSpec(memory_space=pltpu.HBM)
@@ -38,12 +39,28 @@
     return 0.5 * jnp.tanh(0.5 * x) + 0.5
 
 
-def shard_kernel(owners, cov_ref, lab_ref, own_ref, out_ref, mark_ref, sems):
+def shard_kernel(owners, cov_hbm, lab_hbm, own_ref, out_ref, cov_ref, lab_ref, held_ref, sems):
     per_block, blocks = cov_ref.shape
     rows_block = lab_ref.shape[1]
     rows = blocks * rows_block
-    load = pltpu.make_async_copy(own_ref, out_ref.at[pl.ds(0, rows)], sems.at[0])
-    load.start()
+    load_cov = pltpu.make_async_copy(cov_hbm, cov_ref, sems.at[0])
+    load_lab = pltpu.make_async_copy(lab_hbm, lab_ref, sems.at[1])
+    half = rows // 2
+    loads = []
+    stores = []
+    for i in range(2):
+        part = pl.ds(i * half, half)
+        loads.append(pltpu.make_async_copy(own_ref.at[part], held_ref.at[part], sems.at[2 + i]))
+        stores.append(pltpu.make_async_copy(held_ref.at[part], out_ref.at[part], sems.at[4 + i]))
+    load_cov.start()
+    load_lab.start()
+    for load in loads:
+        load.start()
+    for load, store in zip(loads, stores):
+        load.wait()
+        store.start()
+    load_cov.wait()
+    load_lab.wait()
     cov = cov_ref[...]
     heads_at = lax.broadcasted_iota(jnp.int32, (owners, blocks), 0)
     named = (cov[0:1] == heads_at).astype(f32)
@@ -69,12 +86,13 @@
         mark_rows = jnp.where(at_mark == t, mine, mark_rows)
         mark_rows = jnp.where(at_mark == per_block + t, place, mark_rows)
         mark_rows = jnp.where(at_mark == 2 * per_block + t, label, mark_rows)
-    mark_ref[...] = jnp.zeros(mark_ref.shape, bf16)
-    mark_ref[:, 0:rows] = mark_rows.astype(bf16)
-    store = pltpu.make_async_copy(mark_ref, out_ref.at[pl.ds(rows, 16)], sems.at[1])
-    store.start()
-    load.wait()
-    store.wait()
+    held_ref[rows:, :] = jnp.zeros((16, held_ref.shape[1]), bf16)
+    held_ref[rows:, 0:rows] = mark_rows.astype(bf16)
+    last = pl.ds(rows, 16)
+    stores.append(pltpu.make_async_copy(held_ref.at[last], out_ref.at[last], sems.at[6]))
+    stores[-1].start()
+    for store in stores:
+        store.wait()
 
 
 def make_shard(own, coverage, labels, owners):
@@ -82,10 +100,15 @@
     return pl.pallas_call(
         functools.partial(shard_kernel, owners),
         out_shape=sds((rows + 16, feature), bf16),
-        in_specs=[VMEM, VMEM, HBM],
+        in_specs=[HBM, HBM, HBM],
         out_specs=HBM,
-        scratch_shapes=[pltpu.VMEM((16, feature), bf16), pltpu.SemaphoreType.DMA((2,))],
-        compiler_params=params(8),
+        scratch_shapes=[
+            pltpu.VMEM((coverage.shape[1], coverage.shape[0]), jnp.int32),
+            pltpu.VMEM((labels.shape[1], labels.shape[2], labels.shape[0]), jnp.int32),
+            pltpu.VMEM((rows + 16, feature), bf16),
+            pltpu.SemaphoreType.DMA((7,)),
+        ],
+        compiler_params=params(ROOM),
         name="shard",
     )(coverage.T, labels.transpose(1, 2, 0), own)
 
@@ -229,10 +252,12 @@
     if with_total:
         total_ref, vec_ref, refs = refs[0], refs[1], refs[2:]
     if last:
-        kept_ref, given_ref, refs = refs[0], refs[1], refs[2:]
+        given_ref, new_vec_ref, low_ref, refs = refs[0], refs[1], refs[2], refs[3:]
+        rows_ref, wide_ref, mark_ref, target_ref, sems = refs
     else:
         new_total_ref, new_vec_ref, refs = refs[0], refs[1], refs[2:]
-    rows_ref, low_ref, mark_ref, target_ref, sems = refs
+        rows_ref, low_ref, mark_ref, target_ref, sems = refs
+    low_cut = half_rows // 128 * 128
     rows_all, feature = rows_ref.shape
     loads = []
     for i in range(n_parts):
@@ -305,29 +330,69 @@
         new_vec_ref[0:1, :] = grad_bias
         new_vec_ref[1:2, :] = grad_out
         return
-    rep = at_ref[0]
+    first = pl.multiple_of((1 - at_ref[0]) * low_cut, 128)
+    skip = pl.multiple_of((1 - at_ref[0]) * (half_rows - low_cut), 8)
+    wide_ref[...] = lax.dot_general(
+        rows_ref[:, pl.ds(first, feature - low_cut)],
+        low_ref[...],
+        (((0,), (0,)), ((), ())),
+        preferred_element_type=f32,
+    )
+    other = pl.multiple_of((1 - at_ref[0]) * half_rows, 8)
+    given_ref[0:half_rows, :] = (
+        wide_ref[pl.ds(skip, half_rows), :] + total_ref[pl.ds(other, half_rows), :]
+    )
     given_ref[half_rows : half_rows + 8, :] = jnp.zeros((8, hid), f32)
-    kept_ref[half_rows : half_rows + 8, :] = jnp.zeros((8, hid), f32)
-    for ref in (given_ref, kept_ref):
-        ref[half_rows : half_rows + 1, :] = grad_bias
-        ref[half_rows + 1 : half_rows + 2, :] = grad_out
-    for first in range(0, feature, tile):
-        piece = product(first, tile)
-        cut = min(max(half_rows - first, 0), tile)
-
-        @pl.when(rep == 0)
-        def _():
-            if cut > 0:
-                kept_ref[first : first + cut, :] = piece[:cut]
-            if cut < tile:
-                given_ref[first + cut - half_rows : first + tile - half_rows, :] = piece[cut:]
-
-        @pl.when(rep != 0)
-        def _():
-            if cut > 0:
-                given_ref[first : first + cut, :] = piece[:cut]
-            if cut < tile:
-                kept_ref[first + cut - half_rows : first + tile - half_rows, :] = piece[cut:]
+    given_ref[half_rows : half_rows + 1, :] = grad_bias
+    given_ref[half_rows + 1 : half_rows + 2, :] = grad_out
+    new_vec_ref[0:1, :] = grad_bias
+    new_vec_ref[1:2, :] = grad_out
+
+
+def keep_kernel(half_rows, low_cut, unit, spots, n_parts, at_ref, *refs):
+    parts, (low_ref, total_ref, out_ref, rows_ref, wide_ref, sems) = refs[:n_parts], refs[n_parts:]
+    feature = rows_ref.shape[1]
+    loads = []
+    for u, (part, at, _) in enumerate(spots):
+        loads.append(
+            pltpu.make_async_copy(
+                parts[part].at[pl.ds(at, unit)], rows_ref.at[pl.ds(u * unit, unit)], sems.at[u]
+            )
+        )
+    for load in loads:
+        load.start()
+    for load in loads:
+        load.wait()
+    first = pl.multiple_of(at_ref[0] * low_cut, 128)
+    skip = pl.multiple_of(at_ref[0] * (half_rows - low_cut), 8)
+    wide_ref[...] = lax.dot_general(
+        rows_ref[:, pl.ds(first, feature - low_cut)],
+        low_ref[...],
+        (((0,), (0,)), ((), ())),
+        preferred_element_type=f32,
+    )
+    own = pl.multiple_of(at_ref[0] * half_rows, 8)
+    out_ref[...] = wide_ref[pl.ds(skip, half_rows), :] + total_ref[pl.ds(own, half_rows), :]
+
+
+def keep(unit, spots, parts, at, low, total):
+    feature, hid = total.shape
+    half = feature // 2
+    low_cut = half // 128 * 128
+    return pl.pallas_call(
+        functools.partial(keep_kernel, half, low_cut, unit, spots, len(parts)),
+        out_shape=sds((half, hid), f32),
+        in_specs=[SMEM] + [HBM] * len(parts) + [VMEM, VMEM],
+        out_specs=VMEM,
+        scratch_shapes=[
+            pltpu.VMEM((low.shape[0], feature), bf16),
+            pltpu.VMEM((feature - low_cut, hid), f32),
+            pltpu.SemaphoreType.DMA((len(spots),)),
+        ],
+        compiler_params=params(16),
+        cost_estimate=spent(2),
+        name="keep",
+    )(at, *parts, low, total)
 
 
 def learn(unit, spots, parts, at, w, bias, out, total, cost, last):
@@ -335,9 +400,11 @@
     rows_all = len(spots) * unit
     half = feature // 2
     if last:
-        outs = (sds((half + 8, hid), f32), sds((half + 8, hid), f32))
+        outs = (sds((half + 8, hid), f32), sds((2, hid), f32), sds((rows_all, hid), bf16))
+        work = pltpu.VMEM((feature - half // 128 * 128, hid), f32)
     else:
         outs = (sds((feature, hid), f32), sds((2, hid), f32))
+        work = pltpu.VMEM((rows_all, hid), bf16)
     extra = () if total is None else total
     kernel = functools.partial(
         learn_kernel, unit, spots, len(parts), last, total is not None, half
@@ -346,10 +413,10 @@
         kernel,
         out_shape=outs,
         in_specs=[SMEM] + [HBM] * len(parts) + [VMEM] * (3 + len(extra)),
-        out_specs=(VMEM, VMEM),
+        out_specs=(VMEM,) * len(outs),
         scratch_shapes=[
             pltpu.VMEM((rows_all, feature), bf16),
-            pltpu.VMEM((rows_all, hid), bf16),
+            work,
             pltpu.VMEM((len(parts), 16, feature), bf16),
             pltpu.VMEM((rows_all, 1), f32),
             pltpu.SemaphoreType.DMA((2, max(len(parts), len(spots)))),
@@ -381,7 +448,7 @@
 
     @pl.when(pl.program_id(0) == 0)
     def _():
-        grad = kept_vec[0:2, :] + got_vec[0:2, :]
+        grad = kept_vec[...] + got_vec[0:2, :]
         fresh, fresh_first, fresh_second = adam(
             vec_old[...].astype(f32), grad, first_vec[0], second_vec[0]
         )
@@ -390,7 +457,7 @@
         new_second_vec[0] = fresh_second
 
 
-def take_step(rep, kept, got, w_in, vec_old, first_w, second_w, first_vec, second_vec):
+def take_step(rep, kept, kept_vec, got, w_in, vec_old, first_w, second_w, first_vec, second_vec):
     feature, hid = w_in.shape
     half = feature // 2
     tiles = max(n for n in range(1, 5) if half % (16 * n) == 0)
@@ -407,7 +474,7 @@
         grid_spec=pltpu.PrefetchScalarGridSpec(
             num_scalar_prefetch=1,
             grid=(tiles,),
-            in_specs=[here, here, tail, tail, there, moment, moment, pair, pairs, pairs],
+            in_specs=[here, here, pair, tail, there, moment, moment, pair, pairs, pairs],
             out_specs=[here, full, pairs, moment, moment, pairs, pairs],
         ),
         out_shape=(
@@ -421,7 +488,7 @@
         ),
         compiler_params=params(16),
         name="step",
-    )(rep, kept, got, kept, got, w_in, first_w, second_w, vec_old, first_vec, second_vec)
+    )(rep, kept, got, kept_vec, got, w_in, first_w, second_w, vec_old, first_vec, second_vec)
 
 
 def join_kernel(at_ref, other_ref, full_ref, out_ref, sem):
@@ -502,10 +569,12 @@
         else:
             next_right, next_left = None, None
         if hop == planes - 2 and hop > 1:
-            far_sent, right, left, *total = lax.optimization_barrier(
+            far_sent, right, left, grad, vec = lax.optimization_barrier(
                 (far_sent, right, left, *total)
             )
-            far_got = lax.ppermute(far_sent, "dp", [(0, planes - 1), (planes - 1, 0)])
+            total = (grad, vec)
+            ends = [(0, planes - 1), (planes - 1, 0)]
+            far_got = lax.ppermute(far_sent, "dp", ends)
         if 2 * hop < planes:
             fill = hop == 1
             messages = pick(
@@ -541,12 +610,14 @@
 
     for at, (parts, spots) in enumerate(rest):
         cost = (LB, LC, LF)[min(at, 2)]
-        total = add(total, parts, spots, one, cost, at == len(rest) - 1)
-    kept, given = total
+        last = at == len(rest) - 1
+        done, total = total, add(total, parts, spots, one, cost, last)
+    given, kept_vec, low = total
     got = lax.ppermute(given, "rep", swap)
+    kept = keep(unit, spots, parts, rep, low, done[0])
     vec_old = jnp.concatenate([bias_in, w_out])
     new_half, new_full, new_vec, nfw, nsw, nfv, nsv = take_step(
-        rep, kept, got, w_in[0], vec_old, first_w, second_w, first_vec, second_vec
+        rep, kept, kept_vec, got, w_in[0], vec_old, first_w, second_w, first_vec, second_vec
     )
     new_w_in = join(rep, lax.ppermute(new_half, "rep", swap), new_full)
     return new_w_in, new_vec, nfw, nsw, nfv, nsv
@@ -653,7 +724,7 @@
         P(("dp", "head"), None, None),
     )
     planes, heads, reps = mesh.shape["dp"], mesh.shape["head"], mesh.shape["rep"]
-    short = 2 < planes <= heads and heads & (heads - 1) == 0 and reps == 2
+    short = 3 < planes <= heads and heads & (heads - 1) == 0 and reps == 2
     return jax.shard_map(
         gathered if short else routed,
         mesh=mesh,

time: 119 us -> 117 us (0.983)
  waiting for transfers between devices: 53 us -> 50.7 us
  Pallas kernels: 37 us -> 38.7 us
  local copies, waits for them, and re-layouts: 3.95 us -> 2.61 us
    pallas_call x1, Pallas kernels: 0.46 us -> 2.17 us  [make_shard(): pl.pallas_call(functools.partial(shard_kernel, owners), out_shape=sds((ro...]
    unnamed x24 -> x22, local copies, waits for them, and re-layouts: 3.69 us -> 2.35 us
    ppermute x1, waiting for transfers between devices: 3.69 us -> 2.44 us  [gathered(): got = lax.ppermute(given, 'rep', swap)]
    pallas_call x0 -> x1, Pallas kernels: none -> 1.19 us  [keep(): pl.pallas_call(functools.partial(keep_kernel, half, low_cut, unit, spots,...]
  transfers between devices with their start and end apart: 16 -> 16, of which waited for: 9 -> 9; matrix products, arithmetic and copies ran while one was open for 0% -> 0% of each run, Pallas kernels for 23% -> 24%
where the time goes in v4:
time: 117 us
  waiting for transfers between devices  50.7 us (43%)
  Pallas kernels  38.7 us (33%)
  starting transfers between devices  23.2 us (20%)
  local copies, waits for them, and re-layouts  2.61 us (2%)
    pallas_call x4, Pallas kernels, learn(): pl.pallas_call(kernel, out_shape=outs, in_specs=[SMEM] + [HBM] * len(part...  21.1 us
    ppermute x9, waiting for transfers between devices, exchange(): lax.ppermute(units[k], 'head', [(i, i ^ k) for i in range(heads)])  18.4 us
    ppermute x1, waiting for transfers between devices, gathered(): next_left = lax.ppermute(left, 'dp', left_pairs(hop + 1))  17.2 us
    ppermute x9, starting transfers between devices, exchange(): lax.ppermute(units[k], 'head', [(i, i ^ k) for i in range(heads)])  10.7 us
    pallas_call x3, Pallas kernels, pick(): pl.pallas_call(functools.partial(pick_kernel, unit, per_block, plan, len(...  9.48 us
    ppermute x1, starting transfers between devices, gathered(): right = lax.ppermute(own, 'dp', right_pairs(1))  5.98 us
    ppermute x1, waiting for transfers between devices, gathered(): left = lax.ppermute(own, 'dp', left_pairs(1))  5.15 us
    ppermute x1, waiting for transfers between devices, gathered(): far_got = lax.ppermute(far_sent, 'dp', ends)  4.28 us
  transfers between devices with their start and end apart: 16, of which 9 were waited for; matrix products, arithmetic and copies ran while one was open for 0% of the time, Pallas kernels for 24%

profile of v4, /device:TPU:0, one launch (start us, length us, event | category | flops | bytes accessed | tf_op | source)
XLA Modules:
  0.0 116.6 jit_solution(11144033614569749813)
XLA Ops:
  0.6 2.2 %shard.1.refs_0_.refs_2_ = bf16[528,1152]{1,0:T(8,128)(2,1)} custom-call(s32[2,64]{1,0:T(2,128)} %bitcast.28, s32[2,8,64]{2,1,0:T(8,128)} %bitcast.27, bf16[512,1152]{1,0:T(8,128)(2,1)} %bitcast.26), custom_call_target="tpu_custom_call" | custom-call | tf_op jit(solution)/shard_map/shard/pallas_call | solution.py:100
  2.8 6.0 %collective-permute-start = (bf16[528,1152]{1,0:T(8,128)(2,1)}, bf16[528,1152]{1,0:T(8,128)(2,1)}, u32[]{:S(2)}, u32[]{:S(2)}) collective-permute-start(bf16[528,1152]{1,0:T(8,128)(2,1)} %shard.1.refs_0_.refs_2_), channel_id=1, source_target_pairs={{0,8},{8,16},{16,24},{1,9},{9,17},{17,25},{2,10},{10,18},{18,26},{... | collective-permute-start | bytes 3649544 | tf_op jit(solution)/shard_map/ppermute | solution.py:546
  11.5 2.3 %pick.3 = (bf16[144,1152]{1,0:T(8,128)(2,1)S(1)}, bf16[144,1152]{1,0:T(8,128)(2,1)S(1)}, bf16[144,1152]{1,0:T(8,128)(2,1)S(1)}, bf16[144,1152]{1,0:T(8,128)(2,1)S(1)}) custom-call(s32[5]{0:T(128)S(1)} %stack.82.at_ref, bf16[528,1152]{1,0:T(8,128)(2,1)S(1)} %copy-done.1), custom_call_target="tpu_custom_call" | custom-call | flops 1 | bytes 1 | tf_op jit(solution)/shard_map/pick/pallas_call | solution.py:184
  13.8 1.6 %collective-permute-start.2 = (bf16[144,1152]{1,0:T(8,128)(2,1)S(1)}, bf16[144,1152]{1,0:T(8,128)(2,1)S(1)}, u32[]{:S(2)}, u32[]{:S(2)}) collective-permute-start(bf16[144,1152]{1,0:T(8,128)(2,1)S(1)} %get-tuple-element.51), channel_id=1, source_target_pairs={{0,2},{2,0},{4,6},{6,4},{1,3},{3,1},{5,7},{7,5},{8,10},{10,8},{12,... | collective-permute-start | bytes 995336 | tf_op jit(solution)/shard_map/ppermute | solution.py:537
  15.3 1.5 %collective-permute-start.3 = (bf16[144,1152]{1,0:T(8,128)(2,1)S(1)}, bf16[144,1152]{1,0:T(8,128)(2,1)S(1)}, u32[]{:S(2)}, u32[]{:S(2)}) collective-permute-start(bf16[144,1152]{1,0:T(8,128)(2,1)S(1)} %get-tuple-element.52), channel_id=1, source_target_pairs={{0,4},{2,6},{4,0},{6,2},{1,5},{3,7},{5,1},{7,3},{8,12},{10,14},{12... | collective-permute-start | bytes 995336 | tf_op jit(solution)/shard_map/ppermute | solution.py:537
  17.3 7.2 %collective-permute-done.2.refs_1_ = bf16[144,1152]{1,0:T(8,128)(2,1)S(1)} collective-permute-done((bf16[144,1152]{1,0:T(8,128)(2,1)S(1)}, bf16[144,1152]{1,0:T(8,128)(2,1)S(1)}, u32[]{:S(2)}, u32[]{:S(2)}) %collective-permute-start.2) | collective-permute-done | bytes 331808 | tf_op jit(solution)/shard_map/ppermute | solution.py:537
  24.6 6.9 %collective-permute-done.3.refs_2_ = bf16[144,1152]{1,0:T(8,128)(2,1)S(1)} collective-permute-done((bf16[144,1152]{1,0:T(8,128)(2,1)S(1)}, bf16[144,1152]{1,0:T(8,128)(2,1)S(1)}, u32[]{:S(2)}, u32[]{:S(2)}) %collective-permute-start.3) | collective-permute-done | bytes 331808 | tf_op jit(solution)/shard_map/ppermute | solution.py:537
  34.1 5.1 %collective-permute-done.1.refs_1_ = bf16[528,1152]{1,0:T(8,128)(2,1)} collective-permute-done((bf16[528,1152]{1,0:T(8,128)(2,1)}, bf16[528,1152]{1,0:T(8,128)(2,1)}, u32[]{:S(2)}, u32[]{:S(2)}) %collective-permute-start.1) | collective-permute-done | bytes 1216544 | tf_op jit(solution)/shard_map/ppermute | solution.py:547
  39.2 1.7 %collective-permute-start.5 = (bf16[528,1152]{1,0:T(8,128)(2,1)}, bf16[528,1152]{1,0:T(8,128)(2,1)}, u32[]{:S(2)}, u32[]{:S(2)}) collective-permute-start(bf16[528,1152]{1,0:T(8,128)(2,1)} %collective-permute-done.refs_0_), channel_id=1, source_target_pairs={{8,16},{16,24},{9,17},{17,25},{10,18},{18,26},{11,19},{19,27},{12,... | collective-permute-start | bytes 3649544 | tf_op jit(solution)/shard_map/ppermute | solution.py:567
  42.6 3.9 %pick.4 = (bf16[272,1152]{1,0:T(8,128)(2,1)S(1)}, bf16[272,1152]{1,0:T(8,128)(2,1)S(1)}, bf16[272,1152]{1,0:T(8,128)(2,1)S(1)}, bf16[272,1152]{1,0:T(8,128)(2,1)S(1)}) custom-call(s32[10]{0:T(128)S(1)} %stack.93.at_ref, bf16[528,1152]{1,0:T(8,128)(2,1)} %collective-permute-done.refs_0_, bf16[528,1152]{1,0:T(8,128)(2,1)} %collective-permute-done.1.refs_1_, ...), custom_call_target="tpu_custom_call" | custom-call | flops 1 | bytes 1 | tf_op jit(solution)/shard_map/pick/pallas_call | solution.py:184
  46.5 1.6 %collective-permute-start.8 = (bf16[272,1152]{1,0:T(8,128)(2,1)S(1)}, bf16[272,1152]{1,0:T(8,128)(2,1)S(1)}, u32[]{:S(2)}, u32[]{:S(2)}) collective-permute-start(bf16[272,1152]{1,0:T(8,128)(2,1)S(1)} %get-tuple-element.58), channel_id=1, source_target_pairs={{0,2},{2,0},{4,6},{6,4},{1,3},{3,1},{5,7},{7,5},{8,10},{10,8},{12,... | collective-permute-start | bytes 1880072 | tf_op jit(solution)/shard_map/ppermute | solution.py:537
  50.0 4.5 %learn.4 = (f32[1152,768]{1,0:T(8,128)S(1)}, f32[2,768]{1,0:T(2,128)S(1)}) custom-call(s32[2]{0:T(128)S(1)} %pad_add_fusion.at_ref, bf16[144,1152]{1,0:T(8,128)(2,1)S(1)} %get-tuple-element.61.refs_0_, bf16[144,1152]{1,0:T(8,128)(2,1)S(1)} %collective-permute-done.2.refs_1_, bf16[144,1152]{1,0:T(8,128)(2,1)S(1)} %collective-permute-done.3.refs_2_, ...), custom_call_target="tpu_custom_call" | custom-call | flops 1 | bytes 1 | tf_op jit(solution)/shard_map/learn/pallas_call | solution.py:412
  54.5 17.2 %collective-permute-done.6.refs_0_ = bf16[528,1152]{1,0:T(8,128)(2,1)} collective-permute-done((bf16[528,1152]{1,0:T(8,128)(2,1)}, bf16[528,1152]{1,0:T(8,128)(2,1)}, u32[]{:S(2)}, u32[]{:S(2)}) %collective-permute-start.6) | collective-permute-done | bytes 1216544 | tf_op jit(solution)/shard_map/ppermute | solution.py:568
  71.8 2.1 %collective-permute-start.7 = (bf16[528,1152]{1,0:T(8,128)(2,1)S(1)}, bf16[528,1152]{1,0:T(8,128)(2,1)S(1)}, u32[]{:S(2)}, u32[]{:S(2)}) collective-permute-start(bf16[528,1152]{1,0:T(8,128)(2,1)S(1)} %copy-done.6), channel_id=1, source_target_pairs={{0,24},{24,0},{1,25},{25,1},{2,26},{26,2},{3,27},{27,3},{4,28},{28... | collective-permute-start | bytes 3649544 | tf_op jit(solution)/shard_map/ppermute | solution.py:577
  73.8 3.3 %pick.5 = (bf16[144,1152]{1,0:T(8,128)(2,1)S(1)}, bf16[144,1152]{1,0:T(8,128)(2,1)S(1)}, bf16[144,1152]{1,0:T(8,128)(2,1)S(1)}, bf16[144,1152]{1,0:T(8,128)(2,1)S(1)}) custom-call(s32[5]{0:T(128)S(1)} %stack.101.at_ref, bf16[528,1152]{1,0:T(8,128)(2,1)} %collective-permute-done.6.refs_0_, bf16[528,1152]{1,0:T(8,128)(2,1)} %collective-permute-done.5.refs_1_), custom_call_target="tpu_custom_call" | custom-call | flops 11500000256 | bytes 1 | tf_op jit(solution)/shard_map/pick/pallas_call | solution.py:184
  77.2 1.6 %collective-permute-start.11 = (bf16[144,1152]{1,0:T(8,128)(2,1)S(1)}, bf16[144,1152]{1,0:T(8,128)(2,1)S(1)}, u32[]{:S(2)}, u32[]{:S(2)}) collective-permute-start(bf16[144,1152]{1,0:T(8,128)(2,1)S(1)} %get-tuple-element.75), channel_id=1, source_target_pairs={{0,2},{2,0},{4,6},{6,4},{1,3},{3,1},{5,7},{7,5},{8,10},{10,8},{12,... | collective-permute-start | bytes 995336 | tf_op jit(solution)/shard_map/ppermute | solution.py:537
  80.8 8.0 %learn.5 = (f32[1152,768]{1,0:T(8,128)S(1)}, f32[2,768]{1,0:T(2,128)S(1)}) custom-call(s32[2]{0:T(128)S(1)} %pad_add_fusion.1.at_ref, bf16[272,1152]{1,0:T(8,128)(2,1)S(1)} %get-tuple-element.57.refs_0_, bf16[272,1152]{1,0:T(8,128)(2,1)S(1)} %collective-permute-done.8.refs_1_, bf16[272,1152]{1,0:T(8,128)(2,1)S(1)} %collective-permute-done.9.refs_2_, ...), custom_call_target="tpu_custom_call" | custom-call | flops 46000001024 | bytes 1 | tf_op jit(solution)/shard_map/learn/pallas_call | solution.py:412
  88.8 4.2 %collective-permute-done.12.refs_2_ = bf16[144,1152]{1,0:T(8,128)(2,1)S(1)} collective-permute-done((bf16[144,1152]{1,0:T(8,128)(2,1)S(1)}, bf16[144,1152]{1,0:T(8,128)(2,1)S(1)}, u32[]{:S(2)}, u32[]{:S(2)}) %collective-permute-start.12) | collective-permute-done | bytes 331808 | tf_op jit(solution)/shard_map/ppermute | solution.py:537
  93.0 4.5 %learn.6 = (f32[1152,768]{1,0:T(8,128)S(1)}, f32[2,768]{1,0:T(2,128)S(1)}) custom-call(s32[2]{0:T(128)S(1)} %pad_add_fusion.1.at_ref, bf16[144,1152]{1,0:T(8,128)(2,1)S(1)} %get-tuple-element.74.refs_0_, bf16[144,1152]{1,0:T(8,128)(2,1)S(1)} %collective-permute-done.11.refs_1_, bf16[144,1152]{1,0:T(8,128)(2,1)S(1)} %collective-permute-done.12.refs_2_, ...), custom_call_target="tpu_custom_call" | custom-call | flops 23000000512 | bytes 1 | tf_op jit(solution)/shard_map/learn/pallas_call | solution.py:412
  97.5 4.3 %collective-permute-done.7.refs_0_ = bf16[528,1152]{1,0:T(8,128)(2,1)S(1)} collective-permute-done((bf16[528,1152]{1,0:T(8,128)(2,1)S(1)}, bf16[528,1152]{1,0:T(8,128)(2,1)S(1)}, u32[]{:S(2)}, u32[]{:S(2)}) %collective-permute-start.7) | collective-permute-done | bytes 1216544 | tf_op jit(solution)/shard_map/ppermute | solution.py:577
  101.8 4.1 %learn.7 = (f32[584,768]{1,0:T(8,128)S(1)}, f32[2,768]{1,0:T(2,128)S(1)}, bf16[512,768]{1,0:T(8,128)(2,1)S(1)}) custom-call(s32[2]{0:T(128)S(1)} %pad_add_fusion.1.at_ref, bf16[528,1152]{1,0:T(8,128)(2,1)S(1)} %collective-permute-done.7.refs_0_, bf16[1152,768]{1,0:T(8,128)(2,1)S(1)} %bitcast.24, bf16[1,768]{1,0:T(2,128)(2,1)S(1)} %copy-done.7, ...), custom_call_target="tpu_custom_call" | custom-call | flops 1 | bytes 1 | tf_op jit(solution)/shard_map/learn/pallas_call | solution.py:412
  107.3 2.4 %collective-permute-done.14.got.got_vec = f32[584,768]{1,0:T(8,128)S(1)} collective-permute-done((f32[584,768]{1,0:T(8,128)S(1)}, f32[584,768]{1,0:T(8,128)S(1)}, u32[]{:S(2)}, u32[]{:S(2)}) %collective-permute-start.14) | collective-permute-done | bytes 1794080 | tf_op jit(solution)/shard_map/ppermute | solution.py:616
  109.8 3.3 %step.1 = (bf16[576,768]{1,0:T(8,128)(2,1)S(1)}, bf16[1,1152,768]{2,1,0:T(8,128)(2,1)}, bf16[1,2,768]{2,1,0:T(2,128)(2,1)}, f32[1,576,768]{2,1,0:T(8,128)}, f32[...) custom-call(s32[1]{0:T(128)} %bitcast.at_ref, f32[576,768]{1,0:T(8,128)S(1)} %keep.1.kept, ...), custom_call_target="tpu_custom_call" | custom-call | tf_op jit(solution)/shard_map/step/pallas_call | solution.py:472
  113.2 2.3 %collective-permute-done.15.other_ref = bf16[576,768]{1,0:T(8,128)(2,1)S(1)} collective-permute-done((bf16[576,768]{1,0:T(8,128)(2,1)S(1)}, bf16[576,768]{1,0:T(8,128)(2,1)S(1)}, u32[]{:S(2)}, u32[]{:S(2)}) %collective-permute-start.15) | collective-permute-done | bytes 884768 | tf_op jit(solution)/shard_map/ppermute | solution.py:622
  (48 shorter events, 13.8 us)
Async XLA Ops:
  2.8 31.3 %collective-permute-start = (bf16[528,1152]{1,0:T(8,128)(2,1)}, bf16[528,1152]{1,0:T(8,128)(2,1)}, u32[]{:S(2)}, u32[]{:S(2)}) collective-permute-start(bf16[528,1152]{1,0:T(8,128)(2,1)} %shard.1.refs_0_.refs_2_), channel_id=1, source_target_pairs={{0,8},{8,16},{16,24},{1,9},{9,17},{17,25},{2,10},{10,18},{18,26},{... | collective-permute-start | bytes 3649544 | tf_op jit(solution)/shard_map/ppermute | solution.py:546
  8.8 30.4 %collective-permute-start.1 = (bf16[528,1152]{1,0:T(8,128)(2,1)}, bf16[528,1152]{1,0:T(8,128)(2,1)}, u32[]{:S(2)}, u32[]{:S(2)}) collective-permute-start(bf16[528,1152]{1,0:T(8,128)(2,1)} %shard.1.refs_0_.refs_2_), channel_id=1, source_target_pairs={{8,0},{16,8},{24,16},{9,1},{17,9},{25,17},{10,2},{18,10},{26,18},{... | collective-permute-start | bytes 3649544 | tf_op jit(solution)/shard_map/ppermute | solution.py:547
  11.5 31.1 %copy-start.2 = (bf16[528,1152]{1,0:T(8,128)(2,1)S(1)}, bf16[528,1152]{1,0:T(8,128)(2,1)}, u32[]{:S(2)}) copy-start(bf16[528,1152]{1,0:T(8,128)(2,1)} %shard.1.refs_0_.refs_2_) | copy-start | bytes 3649540
  13.8 10.8 %collective-permute-start.2 = (bf16[144,1152]{1,0:T(8,128)(2,1)S(1)}, bf16[144,1152]{1,0:T(8,128)(2,1)S(1)}, u32[]{:S(2)}, u32[]{:S(2)}) collective-permute-start(bf16[144,1152]{1,0:T(8,128)(2,1)S(1)} %get-tuple-element.51), channel_id=1, source_target_pairs={{0,2},{2,0},{4,6},{6,4},{1,3},{3,1},{5,7},{7,5},{8,10},{10,8},{12,... | collective-permute-start | bytes 995336 | tf_op jit(solution)/shard_map/ppermute | solution.py:537
  15.3 16.1 %collective-permute-start.3 = (bf16[144,1152]{1,0:T(8,128)(2,1)S(1)}, bf16[144,1152]{1,0:T(8,128)(2,1)S(1)}, u32[]{:S(2)}, u32[]{:S(2)}) collective-permute-start(bf16[144,1152]{1,0:T(8,128)(2,1)S(1)} %get-tuple-element.52), channel_id=1, source_target_pairs={{0,4},{2,6},{4,0},{6,2},{1,5},{3,7},{5,1},{7,3},{8,12},{10,14},{12... | collective-permute-start | bytes 995336 | tf_op jit(solution)/shard_map/ppermute | solution.py:537
  16.9 14.6 %collective-permute-start.4 = (bf16[144,1152]{1,0:T(8,128)(2,1)S(1)}, bf16[144,1152]{1,0:T(8,128)(2,1)S(1)}, u32[]{:S(2)}, u32[]{:S(2)}) collective-permute-start(bf16[144,1152]{1,0:T(8,128)(2,1)S(1)} %get-tuple-element.53), channel_id=1, source_target_pairs={{0,6},{2,4},{4,2},{6,0},{1,7},{3,5},{5,3},{7,1},{8,14},{10,12},{12... | collective-permute-start | bytes 995336 | tf_op jit(solution)/shard_map/ppermute | solution.py:537
  39.2 15.3 %collective-permute-start.5 = (bf16[528,1152]{1,0:T(8,128)(2,1)}, bf16[528,1152]{1,0:T(8,128)(2,1)}, u32[]{:S(2)}, u32[]{:S(2)}) collective-permute-start(bf16[528,1152]{1,0:T(8,128)(2,1)} %collective-permute-done.refs_0_), channel_id=1, source_target_pairs={{8,16},{16,24},{9,17},{17,25},{10,18},{18,26},{11,19},{19,27},{12,... | collective-permute-start | bytes 3649544 | tf_op jit(solution)/shard_map/ppermute | solution.py:567
  40.9 30.9 %collective-permute-start.6 = (bf16[528,1152]{1,0:T(8,128)(2,1)}, bf16[528,1152]{1,0:T(8,128)(2,1)}, u32[]{:S(2)}, u32[]{:S(2)}) collective-permute-start(bf16[528,1152]{1,0:T(8,128)(2,1)} %collective-permute-done.1.refs_1_), channel_id=1, source_target_pairs={{8,0},{16,8},{9,1},{17,9},{10,2},{18,10},{11,3},{19,11},{12,4},{20... | collective-permute-start | bytes 3649544 | tf_op jit(solution)/shard_map/ppermute | solution.py:568
  42.5 7.5 %copy-start = (bf16[1,1152,768]{2,1,0:T(8,128)(2,1)S(1)}, bf16[1,1152,768]{2,1,0:T(8,128)(2,1)}, u32[]{:S(2)}) copy-start(bf16[1,1152,768]{2,1,0:T(8,128)(2,1)} %param.13) | copy-start | bytes 5308420
  42.5 7.5 %copy-start.7 = (bf16[1,768]{1,0:T(2,128)(2,1)S(1)}, bf16[1,768]{1,0:T(2,128)(2,1)}, u32[]{:S(2)}) copy-start(bf16[1,768]{1,0:T(2,128)(2,1)} %refs_2_.1) | copy-start | bytes 4612
  42.6 7.5 %copy-start.8 = (bf16[1,768]{1,0:T(2,128)(2,1)S(1)}, bf16[1,768]{1,0:T(2,128)(2,1)}, u32[]{:S(2)}) copy-start(bf16[1,768]{1,0:T(2,128)(2,1)} %refs_3_.1) | copy-start | bytes 4612
  46.4 25.3 %copy-start.6 = (bf16[528,1152]{1,0:T(8,128)(2,1)S(1)}, bf16[528,1152]{1,0:T(8,128)(2,1)}, u32[]{:S(2)}) copy-start(bf16[528,1152]{1,0:T(8,128)(2,1)} %copy-done.5) | copy-start | bytes 3649540
  46.5 30.7 %collective-permute-start.8 = (bf16[272,1152]{1,0:T(8,128)(2,1)S(1)}, bf16[272,1152]{1,0:T(8,128)(2,1)S(1)}, u32[]{:S(2)}, u32[]{:S(2)}) collective-permute-start(bf16[272,1152]{1,0:T(8,128)(2,1)S(1)} %get-tuple-element.58), channel_id=1, source_target_pairs={{0,2},{2,0},{4,6},{6,4},{1,3},{3,1},{5,7},{7,5},{8,10},{10,8},{12,... | collective-permute-start | bytes 1880072 | tf_op jit(solution)/shard_map/ppermute | solution.py:537
  48.0 29.2 %collective-permute-start.9 = (bf16[272,1152]{1,0:T(8,128)(2,1)S(1)}, bf16[272,1152]{1,0:T(8,128)(2,1)S(1)}, u32[]{:S(2)}, u32[]{:S(2)}) collective-permute-start(bf16[272,1152]{1,0:T(8,128)(2,1)S(1)} %get-tuple-element.59), channel_id=1, source_target_pairs={{0,4},{2,6},{4,0},{6,2},{1,5},{3,7},{5,1},{7,3},{8,12},{10,14},{12... | collective-permute-start | bytes 1880072 | tf_op jit(solution)/shard_map/ppermute | solution.py:537
  49.5 27.7 %collective-permute-start.10 = (bf16[272,1152]{1,0:T(8,128)(2,1)S(1)}, bf16[272,1152]{1,0:T(8,128)(2,1)S(1)}, u32[]{:S(2)}, u32[]{:S(2)}) collective-permute-start(bf16[272,1152]{1,0:T(8,128)(2,1)S(1)} %get-tuple-element.60), channel_id=1, source_target_pairs={{0,6},{2,4},{4,2},{6,0},{1,7},{3,5},{5,3},{7,1},{8,14},{10,12},{12... | collective-permute-start | bytes 1880072 | tf_op jit(solution)/shard_map/ppermute | solution.py:537
  71.8 30.1 %collective-permute-start.7 = (bf16[528,1152]{1,0:T(8,128)(2,1)S(1)}, bf16[528,1152]{1,0:T(8,128)(2,1)S(1)}, u32[]{:S(2)}, u32[]{:S(2)}) collective-permute-start(bf16[528,1152]{1,0:T(8,128)(2,1)S(1)} %copy-done.6), channel_id=1, source_target_pairs={{0,24},{24,0},{1,25},{25,1},{2,26},{26,2},{3,27},{27,3},{4,28},{28... | collective-permute-start | bytes 3649544 | tf_op jit(solution)/shard_map/ppermute | solution.py:577
  77.2 11.6 %collective-permute-start.11 = (bf16[144,1152]{1,0:T(8,128)(2,1)S(1)}, bf16[144,1152]{1,0:T(8,128)(2,1)S(1)}, u32[]{:S(2)}, u32[]{:S(2)}) collective-permute-start(bf16[144,1152]{1,0:T(8,128)(2,1)S(1)} %get-tuple-element.75), channel_id=1, source_target_pairs={{0,2},{2,0},{4,6},{6,4},{1,3},{3,1},{5,7},{7,5},{8,10},{10,8},{12,... | collective-permute-start | bytes 995336 | tf_op jit(solution)/shard_map/ppermute | solution.py:537
  78.8 14.3 %collective-permute-start.12 = (bf16[144,1152]{1,0:T(8,128)(2,1)S(1)}, bf16[144,1152]{1,0:T(8,128)(2,1)S(1)}, u32[]{:S(2)}, u32[]{:S(2)}) collective-permute-start(bf16[144,1152]{1,0:T(8,128)(2,1)S(1)} %get-tuple-element.76), channel_id=1, source_target_pairs={{0,4},{2,6},{4,0},{6,2},{1,5},{3,7},{5,1},{7,3},{8,12},{10,14},{12... | collective-permute-start | bytes 995336 | tf_op jit(solution)/shard_map/ppermute | solution.py:537
  80.3 12.7 %collective-permute-start.13 = (bf16[144,1152]{1,0:T(8,128)(2,1)S(1)}, bf16[144,1152]{1,0:T(8,128)(2,1)S(1)}, u32[]{:S(2)}, u32[]{:S(2)}) collective-permute-start(bf16[144,1152]{1,0:T(8,128)(2,1)S(1)} %get-tuple-element.77), channel_id=1, source_target_pairs={{0,6},{2,4},{4,2},{6,0},{1,7},{3,5},{5,3},{7,1},{8,14},{10,12},{12... | collective-permute-start | bytes 995336 | tf_op jit(solution)/shard_map/ppermute | solution.py:537
  106.0 3.8 %collective-permute-start.14 = (f32[584,768]{1,0:T(8,128)S(1)}, f32[584,768]{1,0:T(8,128)S(1)}, u32[]{:S(2)}, u32[]{:S(2)}) collective-permute-start(f32[584,768]{1,0:T(8,128)S(1)} %get-tuple-element.85), channel_id=1, source_target_pairs={{0,1},{1,0},{2,3},{3,2},{4,5},{5,4},{6,7},{7,6},{8,9},{9,8},{10,11... | collective-permute-start | bytes 5382152 | tf_op jit(solution)/shard_map/ppermute | solution.py:616
  106.1 3.7 %copy-start.3 = (f32[1,576,768]{2,1,0:T(8,128)S(1)}, f32[1,576,768]{2,1,0:T(8,128)}, u32[]{:S(2)}) copy-start(f32[1,576,768]{2,1,0:T(8,128)} %first_w.1) | copy-start | bytes 5308420
  106.1 3.7 %copy-start.4 = (f32[1,576,768]{2,1,0:T(8,128)S(1)}, f32[1,576,768]{2,1,0:T(8,128)}, u32[]{:S(2)}) copy-start(f32[1,576,768]{2,1,0:T(8,128)} %second_w.1) | copy-start | bytes 5308420
  106.1 3.7 %copy-start.9 = (f32[1,2,768]{2,1,0:T(2,128)S(1)}, f32[1,2,768]{2,1,0:T(2,128)}, u32[]{:S(2)}) copy-start(f32[1,2,768]{2,1,0:T(2,128)} %first_vec.1) | copy-start | bytes 18436
  113.0 2.5 %collective-permute-start.15 = (bf16[576,768]{1,0:T(8,128)(2,1)S(1)}, bf16[576,768]{1,0:T(8,128)(2,1)S(1)}, u32[]{:S(2)}, u32[]{:S(2)}) collective-permute-start(bf16[576,768]{1,0:T(8,128)(2,1)S(1)} %get-tuple-element.87), channel_id=1, source_target_pairs={{0,1},{1,0},{2,3},{3,2},{4,5},{5,4},{6,7},{7,6},{8,9},{9,8},{10,11... | collective-permute-start | bytes 2654216 | tf_op jit(solution)/shard_map/ppermute | solution.py:622
  (3 other events, 6.0 us)

commit v5 on v4

--- a/solution.py
+++ b/solution.py
@@ -543,8 +543,8 @@
         return found if real is None else [jnp.where(real, h, -1) for h in found]
 
     own = make_shard(embeddings.reshape(rows, feature), coverage, labels, owners)
+    left = lax.ppermute(own, "dp", left_pairs(1))
     right = lax.ppermute(own, "dp", right_pairs(1))
-    left = lax.ppermute(own, "dp", left_pairs(1))
     always = jnp.ones((), jnp.bool_)
     at_end = (z == 0) | (z == planes - 1)
 
@@ -563,14 +563,14 @@
         from_left = z >= hop
         from_right = z + hop < planes
         if hop + 1 < planes - 1:
-            right, left, far_sent = lax.optimization_barrier((right, left, far_sent))
+            left, right, far_sent = lax.optimization_barrier((left, right, far_sent))
+            next_left = lax.ppermute(left, "dp", left_pairs(hop + 1))
             next_right = lax.ppermute(right, "dp", right_pairs(hop + 1))
-            next_left = lax.ppermute(left, "dp", left_pairs(hop + 1))
         else:
             next_right, next_left = None, None
         if hop == planes - 2 and hop > 1:
-            far_sent, right, left, grad, vec = lax.optimization_barrier(
-                (far_sent, right, left, *total)
+            far_sent, left, right, grad, vec = lax.optimization_barrier(
+                (far_sent, left, right, *total)
             )
             total = (grad, vec)
             ends = [(0, planes - 1), (planes - 1, 0)]
@@ -580,8 +580,8 @@
             messages = pick(
                 unit,
                 per_block,
-                [right, left, own],
-                [(0, 2), (1, 2)],
+                [left, right, own],
+                [(1, 2), (0, 2)],
                 plane_heads(z, from_left | fill) + plane_heads(z, from_right | fill),
                 [from_left, from_right],
                 PB,

time: 117 us -> 115 us (0.983)
  waiting for transfers between devices: 50.7 us -> 41.5 us
  starting transfers between devices: 23.2 us -> 30.2 us
    ppermute x1, starting transfers between devices: 2.09 us -> 8.38 us  [gathered(): far_got = lax.ppermute(far_sent, 'dp', ends)]
    ppermute x1, waiting for transfers between devices: 5.15 us -> 0.98 us  [gathered(): left = lax.ppermute(own, 'dp', left_pairs(1))]
    ppermute x1, waiting for transfers between devices: 4.28 us -> 1.05 us  [gathered(): far_got = lax.ppermute(far_sent, 'dp', ends)]
    ppermute x1, waiting for transfers between devices: 17.2 us -> 15.3 us  [gathered(): next_left = lax.ppermute(left, 'dp', left_pairs(hop + 1))]
  transfers between devices with their start and end apart: 16 -> 16, of which waited for: 9 -> 9; matrix products, arithmetic and copies ran while one was open for 0% -> 0% of each run, Pallas kernels for 24% -> 25%
where the time goes in v5:
time: 115 us; the launch traced here: 114 us
  waiting for transfers between devices  41.5 us (36%)
  Pallas kernels  38.7 us (34%)
  starting transfers between devices  30.2 us (26%)
  local copies, waits for them, and re-layouts  2.6 us (2%)
    pallas_call x4, Pallas kernels, learn(): pl.pallas_call(kernel, out_shape=outs, in_specs=[SMEM] + [HBM] * len(part...  21.1 us
    ppermute x9, waiting for transfers between devices, exchange(): lax.ppermute(units[k], 'head', [(i, i ^ k) for i in range(heads)])  18.2 us
    ppermute x1, waiting for transfers between devices, gathered(): next_left = lax.ppermute(left, 'dp', left_pairs(hop + 1))  15.3 us
    ppermute x9, starting transfers between devices, exchange(): lax.ppermute(units[k], 'head', [(i, i ^ k) for i in range(heads)])  10.7 us
    pallas_call x3, Pallas kernels, pick(): pl.pallas_call(functools.partial(pick_kernel, unit, per_block, plan, len(...  9.48 us
    ppermute x1, starting transfers between devices, gathered(): far_got = lax.ppermute(far_sent, 'dp', ends)  8.38 us
    ppermute x1, starting transfers between devices, gathered(): right = lax.ppermute(own, 'dp', right_pairs(1))  6.61 us
    pallas_call x1, Pallas kernels, take_step(): pl.pallas_call(step_kernel, grid_spec=pltpu.PrefetchScalarGridSpec(num_sc...  3.26 us
  transfers between devices with their start and end apart: 16, of which 9 were waited for; matrix products, arithmetic and copies ran while one was open for 0% of the time, Pallas kernels for 25%

profile of v5, /device:TPU:0, one launch (start us, length us, event | category | flops | bytes accessed | tf_op | source)
XLA Modules:
  0.0 114.2 jit_solution(13955483083367202066)
XLA Ops:
  0.6 2.2 %shard.1.refs_0_.refs_2_ = bf16[528,1152]{1,0:T(8,128)(2,1)} custom-call(s32[2,64]{1,0:T(2,128)} %bitcast.28, s32[2,8,64]{2,1,0:T(8,128)} %bitcast.27, bf16[512,1152]{1,0:T(8,128)(2,1)} %bitcast.26), custom_call_target="tpu_custom_call" | custom-call | tf_op jit(solution)/shard_map/shard/pallas_call | solution.py:100
  4.1 6.6 %collective-permute-start.1 = (bf16[528,1152]{1,0:T(8,128)(2,1)}, bf16[528,1152]{1,0:T(8,128)(2,1)}, u32[]{:S(2)}, u32[]{:S(2)}) collective-permute-start(bf16[528,1152]{1,0:T(8,128)(2,1)} %shard.1.refs_0_.refs_2_), channel_id=1, source_target_pairs={{0,8},{8,16},{16,24},{1,9},{9,17},{17,25},{2,10},{10,18},{18,26},{... | collective-permute-start | bytes 3649544 | tf_op jit(solution)/shard_map/ppermute | solution.py:547
  12.1 2.3 %pick.3 = (bf16[144,1152]{1,0:T(8,128)(2,1)S(1)}, bf16[144,1152]{1,0:T(8,128)(2,1)S(1)}, bf16[144,1152]{1,0:T(8,128)(2,1)S(1)}, bf16[144,1152]{1,0:T(8,128)(2,1)S(1)}) custom-call(s32[5]{0:T(128)S(1)} %stack.82.at_ref, bf16[528,1152]{1,0:T(8,128)(2,1)S(1)} %copy-done.1), custom_call_target="tpu_custom_call" | custom-call | flops 1 | bytes 1 | tf_op jit(solution)/shard_map/pick/pallas_call | solution.py:184
  14.4 2.0 %collective-permute-start.2 = (bf16[144,1152]{1,0:T(8,128)(2,1)S(1)}, bf16[144,1152]{1,0:T(8,128)(2,1)S(1)}, u32[]{:S(2)}, u32[]{:S(2)}) collective-permute-start(bf16[144,1152]{1,0:T(8,128)(2,1)S(1)} %get-tuple-element.51), channel_id=1, source_target_pairs={{0,2},{2,0},{4,6},{6,4},{1,3},{3,1},{5,7},{7,5},{8,10},{10,8},{12,... | collective-permute-start | bytes 995336 | tf_op jit(solution)/shard_map/ppermute | solution.py:537
  16.4 1.5 %collective-permute-start.3 = (bf16[144,1152]{1,0:T(8,128)(2,1)S(1)}, bf16[144,1152]{1,0:T(8,128)(2,1)S(1)}, u32[]{:S(2)}, u32[]{:S(2)}) collective-permute-start(bf16[144,1152]{1,0:T(8,128)(2,1)S(1)} %get-tuple-element.52), channel_id=1, source_target_pairs={{0,4},{2,6},{4,0},{6,2},{1,5},{3,7},{5,1},{7,3},{8,12},{10,14},{12... | collective-permute-start | bytes 995336 | tf_op jit(solution)/shard_map/ppermute | solution.py:537
  18.0 7.2 %collective-permute-done.2.refs_1_ = bf16[144,1152]{1,0:T(8,128)(2,1)S(1)} collective-permute-done((bf16[144,1152]{1,0:T(8,128)(2,1)S(1)}, bf16[144,1152]{1,0:T(8,128)(2,1)S(1)}, u32[]{:S(2)}, u32[]{:S(2)}) %collective-permute-start.2) | collective-permute-done | bytes 331808 | tf_op jit(solution)/shard_map/ppermute | solution.py:537
  25.2 7.0 %collective-permute-done.3.refs_2_ = bf16[144,1152]{1,0:T(8,128)(2,1)S(1)} collective-permute-done((bf16[144,1152]{1,0:T(8,128)(2,1)S(1)}, bf16[144,1152]{1,0:T(8,128)(2,1)S(1)}, u32[]{:S(2)}, u32[]{:S(2)}) %collective-permute-start.3) | collective-permute-done | bytes 331808 | tf_op jit(solution)/shard_map/ppermute | solution.py:537
  37.3 1.7 %collective-permute-start.6 = (bf16[528,1152]{1,0:T(8,128)(2,1)}, bf16[528,1152]{1,0:T(8,128)(2,1)}, u32[]{:S(2)}, u32[]{:S(2)}) collective-permute-start(bf16[528,1152]{1,0:T(8,128)(2,1)} %collective-permute-done.1.refs_1_), channel_id=1, source_target_pairs={{8,16},{16,24},{9,17},{17,25},{10,18},{18,26},{11,19},{19,27},{12,... | collective-permute-start | bytes 3649544 | tf_op jit(solution)/shard_map/ppermute | solution.py:568
  39.3 3.9 %pick.4 = (bf16[272,1152]{1,0:T(8,128)(2,1)S(1)}, bf16[272,1152]{1,0:T(8,128)(2,1)S(1)}, bf16[272,1152]{1,0:T(8,128)(2,1)S(1)}, bf16[272,1152]{1,0:T(8,128)(2,1)S(1)}) custom-call(s32[10]{0:T(128)S(1)} %stack.93.at_ref, bf16[528,1152]{1,0:T(8,128)(2,1)} %collective-permute-done.refs_0_, bf16[528,1152]{1,0:T(8,128)(2,1)} %collective-permute-done.1.refs_1_, ...), custom_call_target="tpu_custom_call" | custom-call | flops 1 | bytes 1 | tf_op jit(solution)/shard_map/pick/pallas_call | solution.py:184
  43.2 1.7 %collective-permute-start.8 = (bf16[272,1152]{1,0:T(8,128)(2,1)S(1)}, bf16[272,1152]{1,0:T(8,128)(2,1)S(1)}, u32[]{:S(2)}, u32[]{:S(2)}) collective-permute-start(bf16[272,1152]{1,0:T(8,128)(2,1)S(1)} %get-tuple-element.58), channel_id=1, source_target_pairs={{0,2},{2,0},{4,6},{6,4},{1,3},{3,1},{5,7},{7,5},{8,10},{10,8},{12,... | collective-permute-start | bytes 1880072 | tf_op jit(solution)/shard_map/ppermute | solution.py:537
  44.9 1.5 %collective-permute-start.9 = (bf16[272,1152]{1,0:T(8,128)(2,1)S(1)}, bf16[272,1152]{1,0:T(8,128)(2,1)S(1)}, u32[]{:S(2)}, u32[]{:S(2)}) collective-permute-start(bf16[272,1152]{1,0:T(8,128)(2,1)S(1)} %get-tuple-element.59), channel_id=1, source_target_pairs={{0,4},{2,6},{4,0},{6,2},{1,5},{3,7},{5,1},{7,3},{8,12},{10,14},{12... | collective-permute-start | bytes 1880072 | tf_op jit(solution)/shard_map/ppermute | solution.py:537
  46.8 4.5 %learn.4 = (f32[1152,768]{1,0:T(8,128)S(1)}, f32[2,768]{1,0:T(2,128)S(1)}) custom-call(s32[2]{0:T(128)S(1)} %pad_add_fusion.at_ref, bf16[144,1152]{1,0:T(8,128)(2,1)S(1)} %get-tuple-element.61.refs_0_, bf16[144,1152]{1,0:T(8,128)(2,1)S(1)} %collective-permute-done.2.refs_1_, bf16[144,1152]{1,0:T(8,128)(2,1)S(1)} %collective-permute-done.3.refs_2_, ...), custom_call_target="tpu_custom_call" | custom-call | flops 1 | bytes 1 | tf_op jit(solution)/shard_map/learn/pallas_call | solution.py:412
  51.3 15.3 %collective-permute-done.5.refs_0_ = bf16[528,1152]{1,0:T(8,128)(2,1)} collective-permute-done((bf16[528,1152]{1,0:T(8,128)(2,1)}, bf16[528,1152]{1,0:T(8,128)(2,1)}, u32[]{:S(2)}, u32[]{:S(2)}) %collective-permute-start.5) | collective-permute-done | bytes 1216544 | tf_op jit(solution)/shard_map/ppermute | solution.py:567
  66.6 8.4 %collective-permute-start.7 = (bf16[528,1152]{1,0:T(8,128)(2,1)S(1)}, bf16[528,1152]{1,0:T(8,128)(2,1)S(1)}, u32[]{:S(2)}, u32[]{:S(2)}) collective-permute-start(bf16[528,1152]{1,0:T(8,128)(2,1)S(1)} %copy-done.6), channel_id=1, source_target_pairs={{0,24},{24,0},{1,25},{25,1},{2,26},{26,2},{3,27},{27,3},{4,28},{28... | collective-permute-start | bytes 3649544 | tf_op jit(solution)/shard_map/ppermute | solution.py:577
  75.0 3.3 %pick.5 = (bf16[144,1152]{1,0:T(8,128)(2,1)S(1)}, bf16[144,1152]{1,0:T(8,128)(2,1)S(1)}, bf16[144,1152]{1,0:T(8,128)(2,1)S(1)}, bf16[144,1152]{1,0:T(8,128)(2,1)S(1)}) custom-call(s32[5]{0:T(128)S(1)} %stack.101.at_ref, bf16[528,1152]{1,0:T(8,128)(2,1)} %collective-permute-done.5.refs_0_, bf16[528,1152]{1,0:T(8,128)(2,1)} %collective-permute-done.6.refs_1_), custom_call_target="tpu_custom_call" | custom-call | flops 11500000256 | bytes 1 | tf_op jit(solution)/shard_map/pick/pallas_call | solution.py:184
  78.3 1.6 %collective-permute-start.11 = (bf16[144,1152]{1,0:T(8,128)(2,1)S(1)}, bf16[144,1152]{1,0:T(8,128)(2,1)S(1)}, u32[]{:S(2)}, u32[]{:S(2)}) collective-permute-start(bf16[144,1152]{1,0:T(8,128)(2,1)S(1)} %get-tuple-element.75), channel_id=1, source_target_pairs={{0,2},{2,0},{4,6},{6,4},{1,3},{3,1},{5,7},{7,5},{8,10},{10,8},{12,... | collective-permute-start | bytes 995336 | tf_op jit(solution)/shard_map/ppermute | solution.py:537
  79.9 1.5 %collective-permute-start.12 = (bf16[144,1152]{1,0:T(8,128)(2,1)S(1)}, bf16[144,1152]{1,0:T(8,128)(2,1)S(1)}, u32[]{:S(2)}, u32[]{:S(2)}) collective-permute-start(bf16[144,1152]{1,0:T(8,128)(2,1)S(1)} %get-tuple-element.76), channel_id=1, source_target_pairs={{0,4},{2,6},{4,0},{6,2},{1,5},{3,7},{5,1},{7,3},{8,12},{10,14},{12... | collective-permute-start | bytes 995336 | tf_op jit(solution)/shard_map/ppermute | solution.py:537
  81.9 8.0 %learn.5 = (f32[1152,768]{1,0:T(8,128)S(1)}, f32[2,768]{1,0:T(2,128)S(1)}) custom-call(s32[2]{0:T(128)S(1)} %pad_add_fusion.1.at_ref, bf16[272,1152]{1,0:T(8,128)(2,1)S(1)} %get-tuple-element.57.refs_0_, bf16[272,1152]{1,0:T(8,128)(2,1)S(1)} %collective-permute-done.8.refs_1_, bf16[272,1152]{1,0:T(8,128)(2,1)S(1)} %collective-permute-done.9.refs_2_, ...), custom_call_target="tpu_custom_call" | custom-call | flops 46000001024 | bytes 1 | tf_op jit(solution)/shard_map/learn/pallas_call | solution.py:412
  89.9 4.0 %collective-permute-done.12.refs_2_ = bf16[144,1152]{1,0:T(8,128)(2,1)S(1)} collective-permute-done((bf16[144,1152]{1,0:T(8,128)(2,1)S(1)}, bf16[144,1152]{1,0:T(8,128)(2,1)S(1)}, u32[]{:S(2)}, u32[]{:S(2)}) %collective-permute-start.12) | collective-permute-done | bytes 331808 | tf_op jit(solution)/shard_map/ppermute | solution.py:537
  93.8 4.5 %learn.6 = (f32[1152,768]{1,0:T(8,128)S(1)}, f32[2,768]{1,0:T(2,128)S(1)}) custom-call(s32[2]{0:T(128)S(1)} %pad_add_fusion.1.at_ref, bf16[144,1152]{1,0:T(8,128)(2,1)S(1)} %get-tuple-element.74.refs_0_, bf16[144,1152]{1,0:T(8,128)(2,1)S(1)} %collective-permute-done.11.refs_1_, bf16[144,1152]{1,0:T(8,128)(2,1)S(1)} %collective-permute-done.12.refs_2_, ...), custom_call_target="tpu_custom_call" | custom-call | flops 23000000512 | bytes 1 | tf_op jit(solution)/shard_map/learn/pallas_call | solution.py:412
  99.4 4.1 %learn.7 = (f32[584,768]{1,0:T(8,128)S(1)}, f32[2,768]{1,0:T(2,128)S(1)}, bf16[512,768]{1,0:T(8,128)(2,1)S(1)}) custom-call(s32[2]{0:T(128)S(1)} %pad_add_fusion.1.at_ref, bf16[528,1152]{1,0:T(8,128)(2,1)S(1)} %collective-permute-done.7.refs_0_, bf16[1152,768]{1,0:T(8,128)(2,1)S(1)} %bitcast.24, bf16[1,768]{1,0:T(2,128)(2,1)S(1)} %copy-done.7, ...), custom_call_target="tpu_custom_call" | custom-call | flops 1 | bytes 1 | tf_op jit(solution)/shard_map/learn/pallas_call | solution.py:412
  104.9 2.4 %collective-permute-done.14.got.got_vec = f32[584,768]{1,0:T(8,128)S(1)} collective-permute-done((f32[584,768]{1,0:T(8,128)S(1)}, f32[584,768]{1,0:T(8,128)S(1)}, u32[]{:S(2)}, u32[]{:S(2)}) %collective-permute-start.14) | collective-permute-done | bytes 1794080 | tf_op jit(solution)/shard_map/ppermute | solution.py:616
  107.4 3.3 %step.1 = (bf16[576,768]{1,0:T(8,128)(2,1)S(1)}, bf16[1,1152,768]{2,1,0:T(8,128)(2,1)}, bf16[1,2,768]{2,1,0:T(2,128)(2,1)}, f32[1,576,768]{2,1,0:T(8,128)}, f32[...) custom-call(s32[1]{0:T(128)} %bitcast.at_ref, f32[576,768]{1,0:T(8,128)S(1)} %keep.1.kept, ...), custom_call_target="tpu_custom_call" | custom-call | tf_op jit(solution)/shard_map/step/pallas_call | solution.py:472
  110.8 2.3 %collective-permute-done.15.other_ref = bf16[576,768]{1,0:T(8,128)(2,1)S(1)} collective-permute-done((bf16[576,768]{1,0:T(8,128)(2,1)S(1)}, bf16[576,768]{1,0:T(8,128)(2,1)S(1)}, u32[]{:S(2)}, u32[]{:S(2)}) %collective-permute-start.15) | collective-permute-done | bytes 884768 | tf_op jit(solution)/shard_map/ppermute | solution.py:622
  (48 shorter events, 12.3 us)
Async XLA Ops:
  2.8 32.0 %collective-permute-start = (bf16[528,1152]{1,0:T(8,128)(2,1)}, bf16[528,1152]{1,0:T(8,128)(2,1)}, u32[]{:S(2)}, u32[]{:S(2)}) collective-permute-start(bf16[528,1152]{1,0:T(8,128)(2,1)} %shard.1.refs_0_.refs_2_), channel_id=1, source_target_pairs={{8,0},{16,8},{24,16},{9,1},{17,9},{25,17},{10,2},{18,10},{26,18},{... | collective-permute-start | bytes 3649544 | tf_op jit(solution)/shard_map/ppermute | solution.py:546
  4.1 31.9 %collective-permute-start.1 = (bf16[528,1152]{1,0:T(8,128)(2,1)}, bf16[528,1152]{1,0:T(8,128)(2,1)}, u32[]{:S(2)}, u32[]{:S(2)}) collective-permute-start(bf16[528,1152]{1,0:T(8,128)(2,1)} %shard.1.refs_0_.refs_2_), channel_id=1, source_target_pairs={{0,8},{8,16},{16,24},{1,9},{9,17},{17,25},{2,10},{10,18},{18,26},{... | collective-permute-start | bytes 3649544 | tf_op jit(solution)/shard_map/ppermute | solution.py:547
  12.1 27.2 %copy-start.2 = (bf16[528,1152]{1,0:T(8,128)(2,1)S(1)}, bf16[528,1152]{1,0:T(8,128)(2,1)}, u32[]{:S(2)}) copy-start(bf16[528,1152]{1,0:T(8,128)(2,1)} %shard.1.refs_0_.refs_2_) | copy-start | bytes 3649540
  14.4 10.8 %collective-permute-start.2 = (bf16[144,1152]{1,0:T(8,128)(2,1)S(1)}, bf16[144,1152]{1,0:T(8,128)(2,1)S(1)}, u32[]{:S(2)}, u32[]{:S(2)}) collective-permute-start(bf16[144,1152]{1,0:T(8,128)(2,1)S(1)} %get-tuple-element.51), channel_id=1, source_target_pairs={{0,2},{2,0},{4,6},{6,4},{1,3},{3,1},{5,7},{7,5},{8,10},{10,8},{12,... | collective-permute-start | bytes 995336 | tf_op jit(solution)/shard_map/ppermute | solution.py:537
  16.4 15.8 %collective-permute-start.3 = (bf16[144,1152]{1,0:T(8,128)(2,1)S(1)}, bf16[144,1152]{1,0:T(8,128)(2,1)S(1)}, u32[]{:S(2)}, u32[]{:S(2)}) collective-permute-start(bf16[144,1152]{1,0:T(8,128)(2,1)S(1)} %get-tuple-element.52), channel_id=1, source_target_pairs={{0,4},{2,6},{4,0},{6,2},{1,5},{3,7},{5,1},{7,3},{8,12},{10,14},{12... | collective-permute-start | bytes 995336 | tf_op jit(solution)/shard_map/ppermute | solution.py:537
  17.9 14.3 %collective-permute-start.4 = (bf16[144,1152]{1,0:T(8,128)(2,1)S(1)}, bf16[144,1152]{1,0:T(8,128)(2,1)S(1)}, u32[]{:S(2)}, u32[]{:S(2)}) collective-permute-start(bf16[144,1152]{1,0:T(8,128)(2,1)S(1)} %get-tuple-element.53), channel_id=1, source_target_pairs={{0,6},{2,4},{4,2},{6,0},{1,7},{3,5},{5,3},{7,1},{8,14},{10,12},{12... | collective-permute-start | bytes 995336 | tf_op jit(solution)/shard_map/ppermute | solution.py:537
  36.0 30.6 %collective-permute-start.5 = (bf16[528,1152]{1,0:T(8,128)(2,1)}, bf16[528,1152]{1,0:T(8,128)(2,1)}, u32[]{:S(2)}, u32[]{:S(2)}) collective-permute-start(bf16[528,1152]{1,0:T(8,128)(2,1)} %collective-permute-done.refs_0_), channel_id=1, source_target_pairs={{8,0},{16,8},{9,1},{17,9},{10,2},{18,10},{11,3},{19,11},{12,4},{20... | collective-permute-start | bytes 3649544 | tf_op jit(solution)/shard_map/ppermute | solution.py:567
  37.3 29.3 %collective-permute-start.6 = (bf16[528,1152]{1,0:T(8,128)(2,1)}, bf16[528,1152]{1,0:T(8,128)(2,1)}, u32[]{:S(2)}, u32[]{:S(2)}) collective-permute-start(bf16[528,1152]{1,0:T(8,128)(2,1)} %collective-permute-done.1.refs_1_), channel_id=1, source_target_pairs={{8,16},{16,24},{9,17},{17,25},{10,18},{18,26},{11,19},{19,27},{12,... | collective-permute-start | bytes 3649544 | tf_op jit(solution)/shard_map/ppermute | solution.py:568
  39.3 7.5 %copy-start = (bf16[1,1152,768]{2,1,0:T(8,128)(2,1)S(1)}, bf16[1,1152,768]{2,1,0:T(8,128)(2,1)}, u32[]{:S(2)}) copy-start(bf16[1,1152,768]{2,1,0:T(8,128)(2,1)} %param.13) | copy-start | bytes 5308420
  39.3 7.5 %copy-start.7 = (bf16[1,768]{1,0:T(2,128)(2,1)S(1)}, bf16[1,768]{1,0:T(2,128)(2,1)}, u32[]{:S(2)}) copy-start(bf16[1,768]{1,0:T(2,128)(2,1)} %refs_2_.1) | copy-start | bytes 4612
  39.3 7.5 %copy-start.8 = (bf16[1,768]{1,0:T(2,128)(2,1)S(1)}, bf16[1,768]{1,0:T(2,128)(2,1)}, u32[]{:S(2)}) copy-start(bf16[1,768]{1,0:T(2,128)(2,1)} %refs_3_.1) | copy-start | bytes 4612
  43.2 23.4 %copy-start.6 = (bf16[528,1152]{1,0:T(8,128)(2,1)S(1)}, bf16[528,1152]{1,0:T(8,128)(2,1)}, u32[]{:S(2)}) copy-start(bf16[528,1152]{1,0:T(8,128)(2,1)} %copy-done.5) | copy-start | bytes 3649540
  43.2 35.1 %collective-permute-start.8 = (bf16[272,1152]{1,0:T(8,128)(2,1)S(1)}, bf16[272,1152]{1,0:T(8,128)(2,1)S(1)}, u32[]{:S(2)}, u32[]{:S(2)}) collective-permute-start(bf16[272,1152]{1,0:T(8,128)(2,1)S(1)} %get-tuple-element.58), channel_id=1, source_target_pairs={{0,2},{2,0},{4,6},{6,4},{1,3},{3,1},{5,7},{7,5},{8,10},{10,8},{12,... | collective-permute-start | bytes 1880072 | tf_op jit(solution)/shard_map/ppermute | solution.py:537
  44.9 33.4 %collective-permute-start.9 = (bf16[272,1152]{1,0:T(8,128)(2,1)S(1)}, bf16[272,1152]{1,0:T(8,128)(2,1)S(1)}, u32[]{:S(2)}, u32[]{:S(2)}) collective-permute-start(bf16[272,1152]{1,0:T(8,128)(2,1)S(1)} %get-tuple-element.59), channel_id=1, source_target_pairs={{0,4},{2,6},{4,0},{6,2},{1,5},{3,7},{5,1},{7,3},{8,12},{10,14},{12... | collective-permute-start | bytes 1880072 | tf_op jit(solution)/shard_map/ppermute | solution.py:537
  46.4 31.9 %collective-permute-start.10 = (bf16[272,1152]{1,0:T(8,128)(2,1)S(1)}, bf16[272,1152]{1,0:T(8,128)(2,1)S(1)}, u32[]{:S(2)}, u32[]{:S(2)}) collective-permute-start(bf16[272,1152]{1,0:T(8,128)(2,1)S(1)} %get-tuple-element.60), channel_id=1, source_target_pairs={{0,6},{2,4},{4,2},{6,0},{1,7},{3,5},{5,3},{7,1},{8,14},{10,12},{12... | collective-permute-start | bytes 1880072 | tf_op jit(solution)/shard_map/ppermute | solution.py:537
  66.6 32.8 %collective-permute-start.7 = (bf16[528,1152]{1,0:T(8,128)(2,1)S(1)}, bf16[528,1152]{1,0:T(8,128)(2,1)S(1)}, u32[]{:S(2)}, u32[]{:S(2)}) collective-permute-start(bf16[528,1152]{1,0:T(8,128)(2,1)S(1)} %copy-done.6), channel_id=1, source_target_pairs={{0,24},{24,0},{1,25},{25,1},{2,26},{26,2},{3,27},{27,3},{4,28},{28... | collective-permute-start | bytes 3649544 | tf_op jit(solution)/shard_map/ppermute | solution.py:577
  78.3 11.6 %collective-permute-start.11 = (bf16[144,1152]{1,0:T(8,128)(2,1)S(1)}, bf16[144,1152]{1,0:T(8,128)(2,1)S(1)}, u32[]{:S(2)}, u32[]{:S(2)}) collective-permute-start(bf16[144,1152]{1,0:T(8,128)(2,1)S(1)} %get-tuple-element.75), channel_id=1, source_target_pairs={{0,2},{2,0},{4,6},{6,4},{1,3},{3,1},{5,7},{7,5},{8,10},{10,8},{12,... | collective-permute-start | bytes 995336 | tf_op jit(solution)/shard_map/ppermute | solution.py:537
  79.9 14.0 %collective-permute-start.12 = (bf16[144,1152]{1,0:T(8,128)(2,1)S(1)}, bf16[144,1152]{1,0:T(8,128)(2,1)S(1)}, u32[]{:S(2)}, u32[]{:S(2)}) collective-permute-start(bf16[144,1152]{1,0:T(8,128)(2,1)S(1)} %get-tuple-element.76), channel_id=1, source_target_pairs={{0,4},{2,6},{4,0},{6,2},{1,5},{3,7},{5,1},{7,3},{8,12},{10,14},{12... | collective-permute-start | bytes 995336 | tf_op jit(solution)/shard_map/ppermute | solution.py:537
  81.4 12.5 %collective-permute-start.13 = (bf16[144,1152]{1,0:T(8,128)(2,1)S(1)}, bf16[144,1152]{1,0:T(8,128)(2,1)S(1)}, u32[]{:S(2)}, u32[]{:S(2)}) collective-permute-start(bf16[144,1152]{1,0:T(8,128)(2,1)S(1)} %get-tuple-element.77), channel_id=1, source_target_pairs={{0,6},{2,4},{4,2},{6,0},{1,7},{3,5},{5,3},{7,1},{8,14},{10,12},{12... | collective-permute-start | bytes 995336 | tf_op jit(solution)/shard_map/ppermute | solution.py:537
  103.6 3.8 %collective-permute-start.14 = (f32[584,768]{1,0:T(8,128)S(1)}, f32[584,768]{1,0:T(8,128)S(1)}, u32[]{:S(2)}, u32[]{:S(2)}) collective-permute-start(f32[584,768]{1,0:T(8,128)S(1)} %get-tuple-element.85), channel_id=1, source_target_pairs={{0,1},{1,0},{2,3},{3,2},{4,5},{5,4},{6,7},{7,6},{8,9},{9,8},{10,11... | collective-permute-start | bytes 5382152 | tf_op jit(solution)/shard_map/ppermute | solution.py:616
  103.7 3.7 %copy-start.3 = (f32[1,576,768]{2,1,0:T(8,128)S(1)}, f32[1,576,768]{2,1,0:T(8,128)}, u32[]{:S(2)}) copy-start(f32[1,576,768]{2,1,0:T(8,128)} %first_w.1) | copy-start | bytes 5308420
  103.7 3.7 %copy-start.4 = (f32[1,576,768]{2,1,0:T(8,128)S(1)}, f32[1,576,768]{2,1,0:T(8,128)}, u32[]{:S(2)}) copy-start(f32[1,576,768]{2,1,0:T(8,128)} %second_w.1) | copy-start | bytes 5308420
  103.7 3.7 %copy-start.9 = (f32[1,2,768]{2,1,0:T(2,128)S(1)}, f32[1,2,768]{2,1,0:T(2,128)}, u32[]{:S(2)}) copy-start(f32[1,2,768]{2,1,0:T(2,128)} %first_vec.1) | copy-start | bytes 18436
  110.6 2.5 %collective-permute-start.15 = (bf16[576,768]{1,0:T(8,128)(2,1)S(1)}, bf16[576,768]{1,0:T(8,128)(2,1)S(1)}, u32[]{:S(2)}, u32[]{:S(2)}) collective-permute-start(bf16[576,768]{1,0:T(8,128)(2,1)S(1)} %get-tuple-element.87), channel_id=1, source_target_pairs={{0,1},{1,0},{2,3},{3,2},{4,5},{5,4},{6,7},{7,6},{8,9},{9,8},{10,11... | collective-permute-start | bytes 2654216 | tf_op jit(solution)/shard_map/ppermute | solution.py:622
  (3 other events, 6.0 us)

commit v6 on v5

--- a/solution.py
+++ b/solution.py
@@ -526,11 +526,10 @@
     slots = 2 * blocks * per_block // owners
     unit = slots * rows_block
     rows = blocks * rows_block
-    def right_pairs(hop):
-        return [(i, i + 1) for i in range(hop - 1, planes - 1)]
-
-    def left_pairs(hop):
-        return [(i + 1, i) for i in range(planes - hop)]
+    outer_pairs = [(i, i ^ 1) for i in range(planes)]
+    inner_pairs = [(i, i + 1 if i % 2 else i - 1) for i in range(1, planes - 1)]
+    out_pairs = [(i, i ^ 1) for i in range(1, planes - 1)]
+    end_pairs = [(0, planes - 1), (planes - 1, 0)]
 
     def exchange(units):
         return [units[0]] + [
@@ -543,8 +542,8 @@
         return found if real is None else [jnp.where(real, h, -1) for h in found]
 
     own = make_shard(embeddings.reshape(rows, feature), coverage, labels, owners)
-    left = lax.ppermute(own, "dp", left_pairs(1))
-    right = lax.ppermute(own, "dp", right_pairs(1))
+    outer = lax.ppermute(own, "dp", outer_pairs)
+    inner = lax.ppermute(own, "dp", inner_pairs)
     always = jnp.ones((), jnp.bool_)
     at_end = (z == 0) | (z == planes - 1)
 
@@ -558,54 +557,29 @@
     one = jnp.ones((), jnp.int32)
     first_spots = [(k, 0, 0) for k in range(heads)]
     middle = 1 - at_end.astype(jnp.int32)
-    rest = []
-    for hop in range(1, planes - 1):
-        from_left = z >= hop
-        from_right = z + hop < planes
-        if hop + 1 < planes - 1:
-            left, right, far_sent = lax.optimization_barrier((left, right, far_sent))
-            next_left = lax.ppermute(left, "dp", left_pairs(hop + 1))
-            next_right = lax.ppermute(right, "dp", right_pairs(hop + 1))
-        else:
-            next_right, next_left = None, None
-        if hop == planes - 2 and hop > 1:
-            far_sent, left, right, grad, vec = lax.optimization_barrier(
-                (far_sent, left, right, *total)
-            )
-            total = (grad, vec)
-            ends = [(0, planes - 1), (planes - 1, 0)]
-            far_got = lax.ppermute(far_sent, "dp", ends)
-        if 2 * hop < planes:
-            fill = hop == 1
-            messages = pick(
-                unit,
-                per_block,
-                [left, right, own],
-                [(1, 2), (0, 2)],
-                plane_heads(z, from_left | fill) + plane_heads(z, from_right | fill),
-                [from_left, from_right],
-                PB,
-            )
-            units = 2
-        else:
-            messages = pick(
-                unit,
-                per_block,
-                [left, right],
-                [(0, 1)],
-                plane_heads(z, from_left | from_right),
-                [from_right],
-                PC,
-            )
-            units = 1
-        where = [(k, g * unit, g) for k in range(heads) for g in range(units)]
-        if hop == 1:
-            first_units = lax.optimization_barrier((*first_units, *messages))[:heads]
-            total = add(None, first_units, first_spots, middle, LA)
-        else:
-            messages = lax.optimization_barrier((*messages, *rest[-1][0]))[:heads]
-        rest.append((exchange(messages), where))
-        right, left = next_right, next_left
+    outer, inner, far_sent = lax.optimization_barrier((outer, inner, far_sent))
+    next_in = lax.ppermute(outer, "dp", inner_pairs)
+    next_out = lax.ppermute(inner, "dp", out_pairs)
+    messages = pick(
+        unit, per_block, [outer, inner, own], [(0, 0), (1, 2)], plane_heads(z) * 2,
+        [always, jnp.logical_not(at_end)], PB,
+    )
+    first_units = lax.optimization_barrier((*first_units, *messages))[:heads]
+    total = add(None, first_units, first_spots, middle, LA)
+    near = exchange(messages)
+    far_sent, next_out, next_in, *total = lax.optimization_barrier(
+        (far_sent, next_out, next_in, *total)
+    )
+    far_got = lax.ppermute(far_sent, "dp", end_pairs)
+    messages = pick(
+        unit, per_block, [next_in, next_out], [(0, 1)], plane_heads(z),
+        [jnp.logical_not(at_end)], PC,
+    )
+    messages = lax.optimization_barrier((*messages, *near))[:heads]
+    rest = [
+        (near, [(k, g * unit, g) for k in range(heads) for g in range(2)]),
+        (exchange(messages), [(k, 0, 0) for k in range(heads)]),
+    ]
     rest.append(([far_got], [(0, k * unit, k) for k in range(heads)]))
 
     for at, (parts, spots) in enumerate(rest):
@@ -724,7 +698,7 @@
         P(("dp", "head"), None, None),
     )
     planes, heads, reps = mesh.shape["dp"], mesh.shape["head"], mesh.shape["rep"]
-    short = 3 < planes <= heads and heads & (heads - 1) == 0 and reps == 2
+    short = planes == 4 and heads & (heads - 1) == 0 and reps == 2
     return jax.shard_map(
         gathered if short else routed,
         mesh=mesh,

time: 115 us -> 111 us (0.965)
  starting transfers between devices: 30.2 us -> 23.1 us
  waiting for transfers between devices: 41.5 us -> 44.4 us
    ppermute x5, starting transfers between devices: 19.3 us -> 12.1 us  [the longest x1 4.39 us: gathered(): far_got = lax.ppermute(far_sent, 'dp', end_pairs)]
    ppermute x5, waiting for transfers between devices: 18.5 us -> 21.3 us  [the longest x1 16.2 us: gathered(): next_out = lax.ppermute(inner, 'dp', out_pairs)]
  transfers between devices with their start and end apart: 16 -> 16, of which waited for: 9 -> 8; matrix products, arithmetic and copies ran while one was open for 0% -> 0% of each run, Pallas kernels for 25% -> 26%
where the time goes in v6:
time: 111 us
  waiting for transfers between devices  44.4 us (40%)
  Pallas kernels  39.4 us (35%)
  starting transfers between devices  23.1 us (21%)
  local copies, waits for them, and re-layouts  2.6 us (2%)
    pallas_call x4, Pallas kernels, learn(): pl.pallas_call(kernel, out_shape=outs, in_specs=[SMEM] + [HBM] * len(part...  21.1 us
    ppermute x9, waiting for transfers between devices, exchange(): lax.ppermute(units[k], 'head', [(i, i ^ k) for i in range(heads)])  18.4 us
    ppermute x1, waiting for transfers between devices, gathered(): next_out = lax.ppermute(inner, 'dp', out_pairs)  16.2 us
    ppermute x9, starting transfers between devices, exchange(): lax.ppermute(units[k], 'head', [(i, i ^ k) for i in range(heads)])  10.7 us
    pallas_call x3, Pallas kernels, pick(): pl.pallas_call(functools.partial(pick_kernel, unit, per_block, plan, len(...  10.2 us
    ppermute x1, starting transfers between devices, gathered(): far_got = lax.ppermute(far_sent, 'dp', end_pairs)  4.39 us
    pallas_call x1, Pallas kernels, take_step(): pl.pallas_call(step_kernel, grid_spec=pltpu.PrefetchScalarGridSpec(num_sc...  3.26 us
    ppermute x1, starting transfers between devices, gathered(): outer = lax.ppermute(own, 'dp', outer_pairs)  3.09 us
  transfers between devices with their start and end apart: 16, of which 8 were waited for; matrix products, arithmetic and copies ran while one was open for 0% of the time, Pallas kernels for 26%

profile of v6, /device:TPU:0, one launch (start us, length us, event | category | flops | bytes accessed | tf_op | source)
XLA Modules:
  0.0 110.6 jit_solution(708203107363049363)
XLA Ops:
  0.6 2.2 %shard.1.refs_0_.refs_2_ = bf16[528,1152]{1,0:T(8,128)(2,1)} custom-call(s32[2,64]{1,0:T(2,128)} %bitcast.22, s32[2,8,64]{2,1,0:T(8,128)} %bitcast.21, bf16[512,1152]{1,0:T(8,128)(2,1)} %bitcast.20), custom_call_target="tpu_custom_call" | custom-call | tf_op jit(solution)/shard_map/shard/pallas_call | solution.py:100
  2.8 3.1 %collective-permute-start = (bf16[528,1152]{1,0:T(8,128)(2,1)}, bf16[528,1152]{1,0:T(8,128)(2,1)}, u32[]{:S(2)}, u32[]{:S(2)}) collective-permute-start(bf16[528,1152]{1,0:T(8,128)(2,1)} %shard.1.refs_0_.refs_2_), channel_id=1, source_target_pairs={{0,8},{8,0},{16,24},{24,16},{1,9},{9,1},{17,25},{25,17},{2,10},{10... | collective-permute-start | bytes 3649544 | tf_op jit(solution)/shard_map/ppermute | solution.py:545
  5.9 1.7 %collective-permute-start.1 = (bf16[528,1152]{1,0:T(8,128)(2,1)}, bf16[528,1152]{1,0:T(8,128)(2,1)}, u32[]{:S(2)}, u32[]{:S(2)}) collective-permute-start(bf16[528,1152]{1,0:T(8,128)(2,1)} %shard.1.refs_0_.refs_2_), channel_id=1, source_target_pairs={{8,16},{16,8},{9,17},{17,9},{10,18},{18,10},{11,19},{19,11},{12,20... | collective-permute-start | bytes 3649544 | tf_op jit(solution)/shard_map/ppermute | solution.py:546
  8.9 2.3 %pick.3 = (bf16[144,1152]{1,0:T(8,128)(2,1)S(1)}, bf16[144,1152]{1,0:T(8,128)(2,1)S(1)}, bf16[144,1152]{1,0:T(8,128)(2,1)S(1)}, bf16[144,1152]{1,0:T(8,128)(2,1)S(1)}) custom-call(s32[5]{0:T(128)S(1)} %stack.63.at_ref, bf16[528,1152]{1,0:T(8,128)(2,1)S(1)} %copy-done.1), custom_call_target="tpu_custom_call" | custom-call | flops 1 | bytes 1 | tf_op jit(solution)/shard_map/pick/pallas_call | solution.py:184
  11.3 1.6 %collective-permute-start.2 = (bf16[144,1152]{1,0:T(8,128)(2,1)S(1)}, bf16[144,1152]{1,0:T(8,128)(2,1)S(1)}, u32[]{:S(2)}, u32[]{:S(2)}) collective-permute-start(bf16[144,1152]{1,0:T(8,128)(2,1)S(1)} %get-tuple-element.51), channel_id=1, source_target_pairs={{0,2},{2,0},{4,6},{6,4},{1,3},{3,1},{5,7},{7,5},{8,10},{10,8},{12,... | collective-permute-start | bytes 995336 | tf_op jit(solution)/shard_map/ppermute | solution.py:536
  14.8 7.2 %collective-permute-done.2.refs_1_ = bf16[144,1152]{1,0:T(8,128)(2,1)S(1)} collective-permute-done((bf16[144,1152]{1,0:T(8,128)(2,1)S(1)}, bf16[144,1152]{1,0:T(8,128)(2,1)S(1)}, u32[]{:S(2)}, u32[]{:S(2)}) %collective-permute-start.2) | collective-permute-done | bytes 331808 | tf_op jit(solution)/shard_map/ppermute | solution.py:536
  22.1 6.9 %collective-permute-done.3.refs_2_ = bf16[144,1152]{1,0:T(8,128)(2,1)S(1)} collective-permute-done((bf16[144,1152]{1,0:T(8,128)(2,1)S(1)}, bf16[144,1152]{1,0:T(8,128)(2,1)S(1)}, u32[]{:S(2)}, u32[]{:S(2)}) %collective-permute-start.3) | collective-permute-done | bytes 331808 | tf_op jit(solution)/shard_map/ppermute | solution.py:536
  30.5 2.4 %collective-permute-done.refs_0_ = bf16[528,1152]{1,0:T(8,128)(2,1)} collective-permute-done((bf16[528,1152]{1,0:T(8,128)(2,1)}, bf16[528,1152]{1,0:T(8,128)(2,1)}, u32[]{:S(2)}, u32[]{:S(2)}) %collective-permute-start) | collective-permute-done | bytes 1216544 | tf_op jit(solution)/shard_map/ppermute | solution.py:545
  34.3 1.7 %collective-permute-start.6 = (bf16[528,1152]{1,0:T(8,128)(2,1)}, bf16[528,1152]{1,0:T(8,128)(2,1)}, u32[]{:S(2)}, u32[]{:S(2)}) collective-permute-start(bf16[528,1152]{1,0:T(8,128)(2,1)} %collective-permute-done.refs_0_), channel_id=1, source_target_pairs={{8,16},{16,8},{9,17},{17,9},{10,18},{18,10},{11,19},{19,11},{12,20... | collective-permute-start | bytes 3649544 | tf_op jit(solution)/shard_map/ppermute | solution.py:561
  36.3 4.6 %pick.4 = (bf16[272,1152]{1,0:T(8,128)(2,1)S(1)}, bf16[272,1152]{1,0:T(8,128)(2,1)S(1)}, bf16[272,1152]{1,0:T(8,128)(2,1)S(1)}, bf16[272,1152]{1,0:T(8,128)(2,1)S(1)}) custom-call(s32[10]{0:T(128)S(1)} %stack.72.at_ref, bf16[528,1152]{1,0:T(8,128)(2,1)} %collective-permute-done.refs_0_, bf16[528,1152]{1,0:T(8,128)(2,1)} %collective-permute-done.1.refs_1_, ...), custom_call_target="tpu_custom_call" | custom-call | flops 1 | bytes 1 | tf_op jit(solution)/shard_map/pick/pallas_call | solution.py:184
  40.9 1.7 %collective-permute-start.8 = (bf16[272,1152]{1,0:T(8,128)(2,1)S(1)}, bf16[272,1152]{1,0:T(8,128)(2,1)S(1)}, u32[]{:S(2)}, u32[]{:S(2)}) collective-permute-start(bf16[272,1152]{1,0:T(8,128)(2,1)S(1)} %get-tuple-element.58), channel_id=1, source_target_pairs={{0,2},{2,0},{4,6},{6,4},{1,3},{3,1},{5,7},{7,5},{8,10},{10,8},{12,... | collective-permute-start | bytes 1880072 | tf_op jit(solution)/shard_map/ppermute | solution.py:536
  44.5 4.5 %learn.4 = (f32[1152,768]{1,0:T(8,128)S(1)}, f32[2,768]{1,0:T(2,128)S(1)}) custom-call(s32[2]{0:T(128)S(1)} %pad_add_fusion.at_ref, bf16[144,1152]{1,0:T(8,128)(2,1)S(1)} %get-tuple-element.61.refs_0_, bf16[144,1152]{1,0:T(8,128)(2,1)S(1)} %collective-permute-done.2.refs_1_, bf16[144,1152]{1,0:T(8,128)(2,1)S(1)} %collective-permute-done.3.refs_2_, ...), custom_call_target="tpu_custom_call" | custom-call | flops 1 | bytes 1 | tf_op jit(solution)/shard_map/learn/pallas_call | solution.py:412
  49.0 16.2 %collective-permute-done.5.refs_1_ = bf16[528,1152]{1,0:T(8,128)(2,1)} collective-permute-done((bf16[528,1152]{1,0:T(8,128)(2,1)}, bf16[528,1152]{1,0:T(8,128)(2,1)}, u32[]{:S(2)}, u32[]{:S(2)}) %collective-permute-start.5) | collective-permute-done | bytes 1216544 | tf_op jit(solution)/shard_map/ppermute | solution.py:562
  65.2 4.4 %collective-permute-start.7 = (bf16[528,1152]{1,0:T(8,128)(2,1)S(1)}, bf16[528,1152]{1,0:T(8,128)(2,1)S(1)}, u32[]{:S(2)}, u32[]{:S(2)}) collective-permute-start(bf16[528,1152]{1,0:T(8,128)(2,1)S(1)} %copy-done.6), channel_id=1, source_target_pairs={{0,24},{24,0},{1,25},{25,1},{2,26},{26,2},{3,27},{27,3},{4,28},{28... | collective-permute-start | bytes 3649544 | tf_op jit(solution)/shard_map/ppermute | solution.py:573
  69.6 3.3 %pick.5 = (bf16[144,1152]{1,0:T(8,128)(2,1)S(1)}, bf16[144,1152]{1,0:T(8,128)(2,1)S(1)}, bf16[144,1152]{1,0:T(8,128)(2,1)S(1)}, bf16[144,1152]{1,0:T(8,128)(2,1)S(1)}) custom-call(s32[5]{0:T(128)S(1)} %stack.74.at_ref, bf16[528,1152]{1,0:T(8,128)(2,1)} %collective-permute-done.6.refs_0_, bf16[528,1152]{1,0:T(8,128)(2,1)} %collective-permute-done.5.refs_1_), custom_call_target="tpu_custom_call" | custom-call | flops 11500000256 | bytes 1 | tf_op jit(solution)/shard_map/pick/pallas_call | solution.py:184
  73.0 1.6 %collective-permute-start.11 = (bf16[144,1152]{1,0:T(8,128)(2,1)S(1)}, bf16[144,1152]{1,0:T(8,128)(2,1)S(1)}, u32[]{:S(2)}, u32[]{:S(2)}) collective-permute-start(bf16[144,1152]{1,0:T(8,128)(2,1)S(1)} %get-tuple-element.75), channel_id=1, source_target_pairs={{0,2},{2,0},{4,6},{6,4},{1,3},{3,1},{5,7},{7,5},{8,10},{10,8},{12,... | collective-permute-start | bytes 995336 | tf_op jit(solution)/shard_map/ppermute | solution.py:536
  76.5 8.0 %learn.5 = (f32[1152,768]{1,0:T(8,128)S(1)}, f32[2,768]{1,0:T(2,128)S(1)}) custom-call(s32[2]{0:T(128)S(1)} %pad_add_fusion.1.at_ref, bf16[272,1152]{1,0:T(8,128)(2,1)S(1)} %get-tuple-element.57.refs_0_, bf16[272,1152]{1,0:T(8,128)(2,1)S(1)} %collective-permute-done.8.refs_1_, bf16[272,1152]{1,0:T(8,128)(2,1)S(1)} %collective-permute-done.9.refs_2_, ...), custom_call_target="tpu_custom_call" | custom-call | flops 46000001024 | bytes 1 | tf_op jit(solution)/shard_map/learn/pallas_call | solution.py:412
  84.5 4.2 %collective-permute-done.12.refs_2_ = bf16[144,1152]{1,0:T(8,128)(2,1)S(1)} collective-permute-done((bf16[144,1152]{1,0:T(8,128)(2,1)S(1)}, bf16[144,1152]{1,0:T(8,128)(2,1)S(1)}, u32[]{:S(2)}, u32[]{:S(2)}) %collective-permute-start.12) | collective-permute-done | bytes 331808 | tf_op jit(solution)/shard_map/ppermute | solution.py:536
  88.8 4.5 %learn.6 = (f32[1152,768]{1,0:T(8,128)S(1)}, f32[2,768]{1,0:T(2,128)S(1)}) custom-call(s32[2]{0:T(128)S(1)} %pad_add_fusion.1.at_ref, bf16[144,1152]{1,0:T(8,128)(2,1)S(1)} %get-tuple-element.74.refs_0_, bf16[144,1152]{1,0:T(8,128)(2,1)S(1)} %collective-permute-done.11.refs_1_, bf16[144,1152]{1,0:T(8,128)(2,1)S(1)} %collective-permute-done.12.refs_2_, ...), custom_call_target="tpu_custom_call" | custom-call | flops 23000000512 | bytes 1 | tf_op jit(solution)/shard_map/learn/pallas_call | solution.py:412
  93.3 2.6 %collective-permute-done.7.refs_0_ = bf16[528,1152]{1,0:T(8,128)(2,1)S(1)} collective-permute-done((bf16[528,1152]{1,0:T(8,128)(2,1)S(1)}, bf16[528,1152]{1,0:T(8,128)(2,1)S(1)}, u32[]{:S(2)}, u32[]{:S(2)}) %collective-permute-start.7) | collective-permute-done | bytes 1216544 | tf_op jit(solution)/shard_map/ppermute | solution.py:573
  95.9 4.1 %learn.7 = (f32[584,768]{1,0:T(8,128)S(1)}, f32[2,768]{1,0:T(2,128)S(1)}, bf16[512,768]{1,0:T(8,128)(2,1)S(1)}) custom-call(s32[2]{0:T(128)S(1)} %pad_add_fusion.1.at_ref, bf16[528,1152]{1,0:T(8,128)(2,1)S(1)} %collective-permute-done.7.refs_0_, bf16[1152,768]{1,0:T(8,128)(2,1)S(1)} %bitcast.18, bf16[1,768]{1,0:T(2,128)(2,1)S(1)} %copy-done.7, ...), custom_call_target="tpu_custom_call" | custom-call | flops 1 | bytes 1 | tf_op jit(solution)/shard_map/learn/pallas_call | solution.py:412
  101.4 2.4 %collective-permute-done.14.got.got_vec = f32[584,768]{1,0:T(8,128)S(1)} collective-permute-done((f32[584,768]{1,0:T(8,128)S(1)}, f32[584,768]{1,0:T(8,128)S(1)}, u32[]{:S(2)}, u32[]{:S(2)}) %collective-permute-start.14) | collective-permute-done | bytes 1794080 | tf_op jit(solution)/shard_map/ppermute | solution.py:590
  103.8 3.3 %step.1 = (bf16[576,768]{1,0:T(8,128)(2,1)S(1)}, bf16[1,1152,768]{2,1,0:T(8,128)(2,1)}, bf16[1,2,768]{2,1,0:T(2,128)(2,1)}, f32[1,576,768]{2,1,0:T(8,128)}, f32[...) custom-call(s32[1]{0:T(128)} %bitcast.at_ref, f32[576,768]{1,0:T(8,128)S(1)} %keep.1.kept, ...), custom_call_target="tpu_custom_call" | custom-call | tf_op jit(solution)/shard_map/step/pallas_call | solution.py:472
  107.3 2.3 %collective-permute-done.15.other_ref = bf16[576,768]{1,0:T(8,128)(2,1)S(1)} collective-permute-done((bf16[576,768]{1,0:T(8,128)(2,1)S(1)}, bf16[576,768]{1,0:T(8,128)(2,1)S(1)}, u32[]{:S(2)}, u32[]{:S(2)}) %collective-permute-start.15) | collective-permute-done | bytes 884768 | tf_op jit(solution)/shard_map/ppermute | solution.py:596
  (48 shorter events, 12.8 us)
Async XLA Ops:
  2.8 30.2 %collective-permute-start = (bf16[528,1152]{1,0:T(8,128)(2,1)}, bf16[528,1152]{1,0:T(8,128)(2,1)}, u32[]{:S(2)}, u32[]{:S(2)}) collective-permute-start(bf16[528,1152]{1,0:T(8,128)(2,1)} %shard.1.refs_0_.refs_2_), channel_id=1, source_target_pairs={{0,8},{8,0},{16,24},{24,16},{1,9},{9,1},{17,25},{25,17},{2,10},{10... | collective-permute-start | bytes 3649544 | tf_op jit(solution)/shard_map/ppermute | solution.py:545
  5.9 27.1 %collective-permute-start.1 = (bf16[528,1152]{1,0:T(8,128)(2,1)}, bf16[528,1152]{1,0:T(8,128)(2,1)}, u32[]{:S(2)}, u32[]{:S(2)}) collective-permute-start(bf16[528,1152]{1,0:T(8,128)(2,1)} %shard.1.refs_0_.refs_2_), channel_id=1, source_target_pairs={{8,16},{16,8},{9,17},{17,9},{10,18},{18,10},{11,19},{19,11},{12,20... | collective-permute-start | bytes 3649544 | tf_op jit(solution)/shard_map/ppermute | solution.py:546
  8.9 27.3 %copy-start.2 = (bf16[528,1152]{1,0:T(8,128)(2,1)S(1)}, bf16[528,1152]{1,0:T(8,128)(2,1)}, u32[]{:S(2)}) copy-start(bf16[528,1152]{1,0:T(8,128)(2,1)} %shard.1.refs_0_.refs_2_) | copy-start | bytes 3649540
  11.3 10.8 %collective-permute-start.2 = (bf16[144,1152]{1,0:T(8,128)(2,1)S(1)}, bf16[144,1152]{1,0:T(8,128)(2,1)S(1)}, u32[]{:S(2)}, u32[]{:S(2)}) collective-permute-start(bf16[144,1152]{1,0:T(8,128)(2,1)S(1)} %get-tuple-element.51), channel_id=1, source_target_pairs={{0,2},{2,0},{4,6},{6,4},{1,3},{3,1},{5,7},{7,5},{8,10},{10,8},{12,... | collective-permute-start | bytes 995336 | tf_op jit(solution)/shard_map/ppermute | solution.py:536
  12.8 16.1 %collective-permute-start.3 = (bf16[144,1152]{1,0:T(8,128)(2,1)S(1)}, bf16[144,1152]{1,0:T(8,128)(2,1)S(1)}, u32[]{:S(2)}, u32[]{:S(2)}) collective-permute-start(bf16[144,1152]{1,0:T(8,128)(2,1)S(1)} %get-tuple-element.52), channel_id=1, source_target_pairs={{0,4},{2,6},{4,0},{6,2},{1,5},{3,7},{5,1},{7,3},{8,12},{10,14},{12... | collective-permute-start | bytes 995336 | tf_op jit(solution)/shard_map/ppermute | solution.py:536
  14.3 14.6 %collective-permute-start.4 = (bf16[144,1152]{1,0:T(8,128)(2,1)S(1)}, bf16[144,1152]{1,0:T(8,128)(2,1)S(1)}, u32[]{:S(2)}, u32[]{:S(2)}) collective-permute-start(bf16[144,1152]{1,0:T(8,128)(2,1)S(1)} %get-tuple-element.53), channel_id=1, source_target_pairs={{0,6},{2,4},{4,2},{6,0},{1,7},{3,5},{5,3},{7,1},{8,14},{10,12},{12... | collective-permute-start | bytes 995336 | tf_op jit(solution)/shard_map/ppermute | solution.py:536
  33.0 32.2 %collective-permute-start.5 = (bf16[528,1152]{1,0:T(8,128)(2,1)}, bf16[528,1152]{1,0:T(8,128)(2,1)}, u32[]{:S(2)}, u32[]{:S(2)}) collective-permute-start(bf16[528,1152]{1,0:T(8,128)(2,1)} %collective-permute-done.1.refs_1_), channel_id=1, source_target_pairs={{8,0},{16,24},{9,1},{17,25},{10,2},{18,26},{11,3},{19,27},{12,4},{... | collective-permute-start | bytes 3649544 | tf_op jit(solution)/shard_map/ppermute | solution.py:562
  34.3 30.9 %collective-permute-start.6 = (bf16[528,1152]{1,0:T(8,128)(2,1)}, bf16[528,1152]{1,0:T(8,128)(2,1)}, u32[]{:S(2)}, u32[]{:S(2)}) collective-permute-start(bf16[528,1152]{1,0:T(8,128)(2,1)} %collective-permute-done.refs_0_), channel_id=1, source_target_pairs={{8,16},{16,8},{9,17},{17,9},{10,18},{18,10},{11,19},{19,11},{12,20... | collective-permute-start | bytes 3649544 | tf_op jit(solution)/shard_map/ppermute | solution.py:561
  36.3 8.2 %copy-start = (bf16[1,1152,768]{2,1,0:T(8,128)(2,1)S(1)}, bf16[1,1152,768]{2,1,0:T(8,128)(2,1)}, u32[]{:S(2)}) copy-start(bf16[1,1152,768]{2,1,0:T(8,128)(2,1)} %param.13) | copy-start | bytes 5308420
  36.3 8.2 %copy-start.7 = (bf16[1,768]{1,0:T(2,128)(2,1)S(1)}, bf16[1,768]{1,0:T(2,128)(2,1)}, u32[]{:S(2)}) copy-start(bf16[1,768]{1,0:T(2,128)(2,1)} %refs_2_.1) | copy-start | bytes 4612
  36.3 8.2 %copy-start.8 = (bf16[1,768]{1,0:T(2,128)(2,1)S(1)}, bf16[1,768]{1,0:T(2,128)(2,1)}, u32[]{:S(2)}) copy-start(bf16[1,768]{1,0:T(2,128)(2,1)} %refs_3_.1) | copy-start | bytes 4612
  40.9 24.3 %copy-start.6 = (bf16[528,1152]{1,0:T(8,128)(2,1)S(1)}, bf16[528,1152]{1,0:T(8,128)(2,1)}, u32[]{:S(2)}) copy-start(bf16[528,1152]{1,0:T(8,128)(2,1)} %copy-done.5) | copy-start | bytes 3649540
  40.9 32.0 %collective-permute-start.8 = (bf16[272,1152]{1,0:T(8,128)(2,1)S(1)}, bf16[272,1152]{1,0:T(8,128)(2,1)S(1)}, u32[]{:S(2)}, u32[]{:S(2)}) collective-permute-start(bf16[272,1152]{1,0:T(8,128)(2,1)S(1)} %get-tuple-element.58), channel_id=1, source_target_pairs={{0,2},{2,0},{4,6},{6,4},{1,3},{3,1},{5,7},{7,5},{8,10},{10,8},{12,... | collective-permute-start | bytes 1880072 | tf_op jit(solution)/shard_map/ppermute | solution.py:536
  42.6 30.3 %collective-permute-start.9 = (bf16[272,1152]{1,0:T(8,128)(2,1)S(1)}, bf16[272,1152]{1,0:T(8,128)(2,1)S(1)}, u32[]{:S(2)}, u32[]{:S(2)}) collective-permute-start(bf16[272,1152]{1,0:T(8,128)(2,1)S(1)} %get-tuple-element.59), channel_id=1, source_target_pairs={{0,4},{2,6},{4,0},{6,2},{1,5},{3,7},{5,1},{7,3},{8,12},{10,14},{12... | collective-permute-start | bytes 1880072 | tf_op jit(solution)/shard_map/ppermute | solution.py:536
  44.1 28.8 %collective-permute-start.10 = (bf16[272,1152]{1,0:T(8,128)(2,1)S(1)}, bf16[272,1152]{1,0:T(8,128)(2,1)S(1)}, u32[]{:S(2)}, u32[]{:S(2)}) collective-permute-start(bf16[272,1152]{1,0:T(8,128)(2,1)S(1)} %get-tuple-element.60), channel_id=1, source_target_pairs={{0,6},{2,4},{4,2},{6,0},{1,7},{3,5},{5,3},{7,1},{8,14},{10,12},{12... | collective-permute-start | bytes 1880072 | tf_op jit(solution)/shard_map/ppermute | solution.py:536
  65.2 30.7 %collective-permute-start.7 = (bf16[528,1152]{1,0:T(8,128)(2,1)S(1)}, bf16[528,1152]{1,0:T(8,128)(2,1)S(1)}, u32[]{:S(2)}, u32[]{:S(2)}) collective-permute-start(bf16[528,1152]{1,0:T(8,128)(2,1)S(1)} %copy-done.6), channel_id=1, source_target_pairs={{0,24},{24,0},{1,25},{25,1},{2,26},{26,2},{3,27},{27,3},{4,28},{28... | collective-permute-start | bytes 3649544 | tf_op jit(solution)/shard_map/ppermute | solution.py:573
  73.0 11.6 %collective-permute-start.11 = (bf16[144,1152]{1,0:T(8,128)(2,1)S(1)}, bf16[144,1152]{1,0:T(8,128)(2,1)S(1)}, u32[]{:S(2)}, u32[]{:S(2)}) collective-permute-start(bf16[144,1152]{1,0:T(8,128)(2,1)S(1)} %get-tuple-element.75), channel_id=1, source_target_pairs={{0,2},{2,0},{4,6},{6,4},{1,3},{3,1},{5,7},{7,5},{8,10},{10,8},{12,... | collective-permute-start | bytes 995336 | tf_op jit(solution)/shard_map/ppermute | solution.py:536
  74.5 14.3 %collective-permute-start.12 = (bf16[144,1152]{1,0:T(8,128)(2,1)S(1)}, bf16[144,1152]{1,0:T(8,128)(2,1)S(1)}, u32[]{:S(2)}, u32[]{:S(2)}) collective-permute-start(bf16[144,1152]{1,0:T(8,128)(2,1)S(1)} %get-tuple-element.76), channel_id=1, source_target_pairs={{0,4},{2,6},{4,0},{6,2},{1,5},{3,7},{5,1},{7,3},{8,12},{10,14},{12... | collective-permute-start | bytes 995336 | tf_op jit(solution)/shard_map/ppermute | solution.py:536
  76.0 12.7 %collective-permute-start.13 = (bf16[144,1152]{1,0:T(8,128)(2,1)S(1)}, bf16[144,1152]{1,0:T(8,128)(2,1)S(1)}, u32[]{:S(2)}, u32[]{:S(2)}) collective-permute-start(bf16[144,1152]{1,0:T(8,128)(2,1)S(1)} %get-tuple-element.77), channel_id=1, source_target_pairs={{0,6},{2,4},{4,2},{6,0},{1,7},{3,5},{5,3},{7,1},{8,14},{10,12},{12... | collective-permute-start | bytes 995336 | tf_op jit(solution)/shard_map/ppermute | solution.py:536
  100.0 3.8 %collective-permute-start.14 = (f32[584,768]{1,0:T(8,128)S(1)}, f32[584,768]{1,0:T(8,128)S(1)}, u32[]{:S(2)}, u32[]{:S(2)}) collective-permute-start(f32[584,768]{1,0:T(8,128)S(1)} %get-tuple-element.85), channel_id=1, source_target_pairs={{0,1},{1,0},{2,3},{3,2},{4,5},{5,4},{6,7},{7,6},{8,9},{9,8},{10,11... | collective-permute-start | bytes 5382152 | tf_op jit(solution)/shard_map/ppermute | solution.py:590
  100.1 3.7 %copy-start.3 = (f32[1,576,768]{2,1,0:T(8,128)S(1)}, f32[1,576,768]{2,1,0:T(8,128)}, u32[]{:S(2)}) copy-start(f32[1,576,768]{2,1,0:T(8,128)} %first_w.1) | copy-start | bytes 5308420
  100.1 3.7 %copy-start.4 = (f32[1,576,768]{2,1,0:T(8,128)S(1)}, f32[1,576,768]{2,1,0:T(8,128)}, u32[]{:S(2)}) copy-start(f32[1,576,768]{2,1,0:T(8,128)} %second_w.1) | copy-start | bytes 5308420
  100.1 3.7 %copy-start.9 = (f32[1,2,768]{2,1,0:T(2,128)S(1)}, f32[1,2,768]{2,1,0:T(2,128)}, u32[]{:S(2)}) copy-start(f32[1,2,768]{2,1,0:T(2,128)} %first_vec.1) | copy-start | bytes 18436
  107.1 2.5 %collective-permute-start.15 = (bf16[576,768]{1,0:T(8,128)(2,1)S(1)}, bf16[576,768]{1,0:T(8,128)(2,1)S(1)}, u32[]{:S(2)}, u32[]{:S(2)}) collective-permute-start(bf16[576,768]{1,0:T(8,128)(2,1)S(1)} %get-tuple-element.87), channel_id=1, source_target_pairs={{0,1},{1,0},{2,3},{3,2},{4,5},{5,4},{6,7},{7,6},{8,9},{9,8},{10,11... | collective-permute-start | bytes 2654216 | tf_op jit(solution)/shard_map/ppermute | solution.py:596
  (3 other events, 6.0 us)

commit v7 on v6

--- a/solution.py
+++ b/solution.py
@@ -12,7 +12,7 @@
 learn_rate = 0.001
 epsilon = 1e-08
 swap = [(0, 1), (1, 0)]
-PB, PC, LA, LB, LC, LF = (0, 10, 0, 40, 20, 0)
+PB, PC, LA, LB, LC, LF = (30, 10, 0, 40, 20, 0)
 bf16 = jnp.bfloat16
 MIB = 1024 * 1024
 ROOM = 60
@@ -310,7 +310,7 @@
         start = (vec_ref[0:1, :], vec_ref[1:2, :])
     else:
         start = (jnp.zeros((1, hid), f32), jnp.zeros((1, hid), f32))
-    grad_bias, grad_out = lax.fori_loop(0, rows_all // step, forward, start)
+    grad_bias, grad_out = lax.fori_loop(0, rows_all // step, forward, start, unroll=True)
 
     def product(first, size):
         piece = lax.dot_general(
@@ -434,51 +434,71 @@
     return new.astype(bf16), new_first, new_second
 
 
-def step_kernel(
-    at_ref, kept, got, kept_vec, got_vec, w, first_w, second_w, vec_old, first_vec, second_vec,
-    new_half, new_full, new_vec, new_first_w, new_second_w, new_first_vec, new_second_vec,
+def weights_kernel(at_ref, kept, got, w, first_w, second_w, new_half):
+    new, _, _ = adam(w[...].astype(f32), kept[...] + got[...], first_w[0], second_w[0])
+    new_half[...] = new
+
+
+def moments_kernel(
+    at_ref, kept, got, kept_vec, got_vec, half_rows, first_w, second_w, bias, out, first_vec, second_vec,
+    new_full, new_vec, new_first_w, new_second_w, new_first_vec, new_second_vec,
 ):
-    new, new_first, new_second = adam(
-        w[...].astype(f32), kept[...] + got[...], first_w[0], second_w[0]
-    )
-    new_half[...] = new
-    new_full[0] = new
-    new_first_w[0] = new_first
-    new_second_w[0] = new_second
+    grad = kept[...] + got[...]
+    new_full[0] = half_rows[...]
+    new_first_w[0] = beta_one * first_w[0] + (1.0 - beta_one) * grad
+    new_second_w[0] = beta_two * second_w[0] + (1.0 - beta_two) * grad * grad
 
     @pl.when(pl.program_id(0) == 0)
     def _():
-        grad = kept_vec[...] + got_vec[0:2, :]
-        fresh, fresh_first, fresh_second = adam(
-            vec_old[...].astype(f32), grad, first_vec[0], second_vec[0]
-        )
-        new_vec[0] = fresh
-        new_first_vec[0] = fresh_first
-        new_second_vec[0] = fresh_second
-
-
-def take_step(rep, kept, kept_vec, got, w_in, vec_old, first_w, second_w, first_vec, second_vec):
+        vec = kept_vec[...] + got_vec[0:2, :]
+        for row, old in enumerate((bias, out)):
+            fresh, fresh_first, fresh_second = adam(
+                old[...].astype(f32),
+                vec[row : row + 1],
+                first_vec[0, row : row + 1],
+                second_vec[0, row : row + 1],
+            )
+            new_vec[0, row : row + 1] = fresh
+            new_first_vec[0, row : row + 1] = fresh_first
+            new_second_vec[0, row : row + 1] = fresh_second
+
+
+def take_step(rep, kept, kept_vec, got, w_in, bias, out, first_w, second_w, first_vec, second_vec):
     feature, hid = w_in.shape
     half = feature // 2
-    tiles = max(n for n in range(1, 5) if half % (16 * n) == 0)
+    tiles = max(n for n in range(1, 3) if half % (16 * n) == 0)
     tile = half // tiles
     here = pl.BlockSpec((tile, hid), lambda i, at: (i, 0))
     there = pl.BlockSpec((tile, hid), lambda i, at: (at[0] * tiles + i, 0))
     tail = pl.BlockSpec((8, hid), lambda i, at: (half // 8, 0))
     moment = pl.BlockSpec((1, tile, hid), lambda i, at: (0, i, 0))
+    row = pl.BlockSpec((1, hid), lambda i, at: (0, 0))
     pair = pl.BlockSpec((2, hid), lambda i, at: (0, 0))
     pairs = pl.BlockSpec((1, 2, hid), lambda i, at: (0, 0, 0))
     full = pl.BlockSpec((1, tile, hid), lambda i, at: (0, at[0] * tiles + i, 0))
-    return pl.pallas_call(
-        step_kernel,
+    new_half = pl.pallas_call(
+        weights_kernel,
         grid_spec=pltpu.PrefetchScalarGridSpec(
             num_scalar_prefetch=1,
             grid=(tiles,),
-            in_specs=[here, here, pair, tail, there, moment, moment, pair, pairs, pairs],
-            out_specs=[here, full, pairs, moment, moment, pairs, pairs],
+            in_specs=[here, here, there, moment, moment],
+            out_specs=here,
+        ),
+        out_shape=sds((half, hid), bf16),
+        compiler_params=params(16),
+        cost_estimate=spent(2),
+        name="weights",
+    )(rep, kept, got, w_in, first_w, second_w)
+    other = lax.ppermute(new_half, "rep", swap)
+    new_full, *rest = pl.pallas_call(
+        moments_kernel,
+        grid_spec=pltpu.PrefetchScalarGridSpec(
+            num_scalar_prefetch=1,
+            grid=(tiles,),
+            in_specs=[here, here, pair, tail, here, moment, moment, row, row, pairs, pairs],
+            out_specs=[full, pairs, moment, moment, pairs, pairs],
         ),
         out_shape=(
-            sds((half, hid), bf16),
             sds((1, feature, hid), bf16),
             sds((1, 2, hid), bf16),
             sds((1, half, hid), f32),
@@ -487,8 +507,10 @@
             sds((1, 2, hid), f32),
         ),
         compiler_params=params(16),
-        name="step",
-    )(rep, kept, got, kept_vec, got, w_in, first_w, second_w, vec_old, first_vec, second_vec)
+        cost_estimate=spent(3),
+        name="moments",
+    )(rep, kept, got, kept_vec, got, new_half, first_w, second_w, bias, out, first_vec, second_vec)
+    return join(rep, other, new_full), *rest
 
 
 def join_kernel(at_ref, other_ref, full_ref, out_ref, sem):
@@ -542,8 +564,8 @@
         return found if real is None else [jnp.where(real, h, -1) for h in found]
 
     own = make_shard(embeddings.reshape(rows, feature), coverage, labels, owners)
+    inner = lax.ppermute(own, "dp", inner_pairs)
     outer = lax.ppermute(own, "dp", outer_pairs)
-    inner = lax.ppermute(own, "dp", inner_pairs)
     always = jnp.ones((), jnp.bool_)
     at_end = (z == 0) | (z == planes - 1)
 
@@ -557,9 +579,9 @@
     one = jnp.ones((), jnp.int32)
     first_spots = [(k, 0, 0) for k in range(heads)]
     middle = 1 - at_end.astype(jnp.int32)
-    outer, inner, far_sent = lax.optimization_barrier((outer, inner, far_sent))
+    inner, far_sent = lax.optimization_barrier((inner, far_sent))
+    next_out = lax.ppermute(inner, "dp", out_pairs)
     next_in = lax.ppermute(outer, "dp", inner_pairs)
-    next_out = lax.ppermute(inner, "dp", out_pairs)
     messages = pick(
         unit, per_block, [outer, inner, own], [(0, 0), (1, 2)], plane_heads(z) * 2,
         [always, jnp.logical_not(at_end)], PB,
@@ -589,12 +611,9 @@
     given, kept_vec, low = total
     got = lax.ppermute(given, "rep", swap)
     kept = keep(unit, spots, parts, rep, low, done[0])
-    vec_old = jnp.concatenate([bias_in, w_out])
-    new_half, new_full, new_vec, nfw, nsw, nfv, nsv = take_step(
-        rep, kept, kept_vec, got, w_in[0], vec_old, first_w, second_w, first_vec, second_vec
-    )
-    new_w_in = join(rep, lax.ppermute(new_half, "rep", swap), new_full)
-    return new_w_in, new_vec, nfw, nsw, nfv, nsv
+    return take_step(
+        rep, kept, kept_vec, got, w_in[0], bias_in, w_out, first_w, second_w, first_vec, second_vec
+    )
 
 
 def routed(

time: 111 us -> 107 us (0.964)
  Pallas kernels: 39.4 us -> 35.2 us
    pallas_call x4, Pallas kernels: 21.1 us -> 17 us  [learn(): pl.pallas_call(kernel, out_shape=outs, in_specs=[SMEM] + [HBM] * len(part...]
    ppermute x1, waiting for transfers between devices: 2.3 us -> 0.01 us  [take_step(): other = lax.ppermute(new_half, 'rep', swap)]
    ppermute x9, waiting for transfers between devices: 18.4 us -> 20.2 us  [exchange(): lax.ppermute(units[k], 'head', [(i, i ^ k) for i in range(heads)])]
    ppermute x1, starting transfers between devices: 3.09 us -> 4.87 us  [gathered(): outer = lax.ppermute(own, 'dp', outer_pairs)]
    ppermute x1, waiting for transfers between devices: 2.58 us -> 3.81 us  [gathered(): far_got = lax.ppermute(far_sent, 'dp', end_pairs)]
    ppermute x1, waiting for transfers between devices: 2.44 us -> 3.67 us  [gathered(): outer = lax.ppermute(own, 'dp', outer_pairs)]
    ppermute x1, waiting for transfers between devices: 16.2 us -> 15.1 us  [gathered(): next_out = lax.ppermute(inner, 'dp', out_pairs)]
    unnamed x22 -> x18, local copies, waits for them, and re-layouts: 2.35 us -> 1.33 us
  transfers between devices with their start and end apart: 16 -> 16, of which waited for: 8 -> 9; matrix products, arithmetic and copies ran while one was open for 0% -> 0% of each run, Pallas kernels for 26% -> 25%
where the time goes in v7:
time: 107 us
  waiting for transfers between devices  45.2 us (42%)
  Pallas kernels  35.2 us (33%)
  starting transfers between devices  24 us (22%)
  local copies, waits for them, and re-layouts  1.58 us (1%)
    ppermute x9, waiting for transfers between devices, exchange(): lax.ppermute(units[k], 'head', [(i, i ^ k) for i in range(heads)])  20.2 us
    pallas_call x4, Pallas kernels, learn(): pl.pallas_call(kernel, out_shape=outs, in_specs=[SMEM] + [HBM] * len(part...  17 us
    ppermute x1, waiting for transfers between devices, gathered(): next_out = lax.ppermute(inner, 'dp', out_pairs)  15.1 us
    ppermute x9, starting transfers between devices, exchange(): lax.ppermute(units[k], 'head', [(i, i ^ k) for i in range(heads)])  10.6 us
    pallas_call x3, Pallas kernels, pick(): pl.pallas_call(functools.partial(pick_kernel, unit, per_block, plan, len(...  9.38 us
    ppermute x1, starting transfers between devices, gathered(): outer = lax.ppermute(own, 'dp', outer_pairs)  4.87 us
    ppermute x1, starting transfers between devices, gathered(): far_got = lax.ppermute(far_sent, 'dp', end_pairs)  4.37 us
    ppermute x1, waiting for transfers between devices, gathered(): far_got = lax.ppermute(far_sent, 'dp', end_pairs)  3.81 us
  transfers between devices with their start and end apart: 16, of which 9 were waited for; matrix products, arithmetic and copies ran while one was open for 0% of the time, Pallas kernels for 25%

profile of v7, /device:TPU:0, one launch (start us, length us, event | category | flops | bytes accessed | tf_op | source)
XLA Modules:
  0.0 107.2 jit_solution(5889340578112936463)
XLA Ops:
  0.6 2.2 %shard.1.refs_0_.refs_2_ = bf16[528,1152]{1,0:T(8,128)(2,1)} custom-call(s32[2,64]{1,0:T(2,128)} %bitcast.22, s32[2,8,64]{2,1,0:T(8,128)} %bitcast.21, bf16[512,1152]{1,0:T(8,128)(2,1)} %bitcast.20), custom_call_target="tpu_custom_call" | custom-call | tf_op jit(solution)/shard_map/shard/pallas_call | solution.py:100
  2.8 1.7 %collective-permute-start = (bf16[528,1152]{1,0:T(8,128)(2,1)}, bf16[528,1152]{1,0:T(8,128)(2,1)}, u32[]{:S(2)}, u32[]{:S(2)}) collective-permute-start(bf16[528,1152]{1,0:T(8,128)(2,1)} %shard.1.refs_0_.refs_2_), channel_id=1, source_target_pairs={{8,16},{16,8},{9,17},{17,9},{10,18},{18,10},{11,19},{19,11},{12,20... | collective-permute-start | bytes 3649544 | tf_op jit(solution)/shard_map/ppermute | solution.py:567
  4.5 4.9 %collective-permute-start.5 = (bf16[528,1152]{1,0:T(8,128)(2,1)}, bf16[528,1152]{1,0:T(8,128)(2,1)}, u32[]{:S(2)}, u32[]{:S(2)}) collective-permute-start(bf16[528,1152]{1,0:T(8,128)(2,1)} %shard.1.refs_0_.refs_2_), channel_id=1, source_target_pairs={{0,8},{8,0},{16,24},{24,16},{1,9},{9,1},{17,25},{25,17},{2,10},{10... | collective-permute-start | bytes 3649544 | tf_op jit(solution)/shard_map/ppermute | solution.py:568
  10.8 2.3 %pick.3 = (bf16[144,1152]{1,0:T(8,128)(2,1)S(1)}, bf16[144,1152]{1,0:T(8,128)(2,1)S(1)}, bf16[144,1152]{1,0:T(8,128)(2,1)S(1)}, bf16[144,1152]{1,0:T(8,128)(2,1)S(1)}) custom-call(s32[5]{0:T(128)S(1)} %stack.63.at_ref, bf16[528,1152]{1,0:T(8,128)(2,1)S(1)} %copy-done.1), custom_call_target="tpu_custom_call" | custom-call | flops 1 | bytes 1 | tf_op jit(solution)/shard_map/pick/pallas_call | solution.py:184
  13.1 1.6 %collective-permute-start.1 = (bf16[144,1152]{1,0:T(8,128)(2,1)S(1)}, bf16[144,1152]{1,0:T(8,128)(2,1)S(1)}, u32[]{:S(2)}, u32[]{:S(2)}) collective-permute-start(bf16[144,1152]{1,0:T(8,128)(2,1)S(1)} %get-tuple-element.49), channel_id=1, source_target_pairs={{0,2},{2,0},{4,6},{6,4},{1,3},{3,1},{5,7},{7,5},{8,10},{10,8},{12,... | collective-permute-start | bytes 995336 | tf_op jit(solution)/shard_map/ppermute | solution.py:558
  14.6 1.5 %collective-permute-start.2 = (bf16[144,1152]{1,0:T(8,128)(2,1)S(1)}, bf16[144,1152]{1,0:T(8,128)(2,1)S(1)}, u32[]{:S(2)}, u32[]{:S(2)}) collective-permute-start(bf16[144,1152]{1,0:T(8,128)(2,1)S(1)} %get-tuple-element.50), channel_id=1, source_target_pairs={{0,4},{2,6},{4,0},{6,2},{1,5},{3,7},{5,1},{7,3},{8,12},{10,14},{12... | collective-permute-start | bytes 995336 | tf_op jit(solution)/shard_map/ppermute | solution.py:558
  17.0 6.9 %collective-permute-done.1.refs_1_ = bf16[144,1152]{1,0:T(8,128)(2,1)S(1)} collective-permute-done((bf16[144,1152]{1,0:T(8,128)(2,1)S(1)}, bf16[144,1152]{1,0:T(8,128)(2,1)S(1)}, u32[]{:S(2)}, u32[]{:S(2)}) %collective-permute-start.1) | collective-permute-done | bytes 331808 | tf_op jit(solution)/shard_map/ppermute | solution.py:558
  23.9 6.6 %collective-permute-done.2.refs_2_ = bf16[144,1152]{1,0:T(8,128)(2,1)S(1)} collective-permute-done((bf16[144,1152]{1,0:T(8,128)(2,1)S(1)}, bf16[144,1152]{1,0:T(8,128)(2,1)S(1)}, u32[]{:S(2)}, u32[]{:S(2)}) %collective-permute-start.2) | collective-permute-done | bytes 331808 | tf_op jit(solution)/shard_map/ppermute | solution.py:558
  32.5 3.7 %collective-permute-done.5.refs_0_ = bf16[528,1152]{1,0:T(8,128)(2,1)} collective-permute-done((bf16[528,1152]{1,0:T(8,128)(2,1)}, bf16[528,1152]{1,0:T(8,128)(2,1)}, u32[]{:S(2)}, u32[]{:S(2)}) %collective-permute-start.5) | collective-permute-done | bytes 1216544 | tf_op jit(solution)/shard_map/ppermute | solution.py:568
  36.9 4.6 %pick.4 = (bf16[272,1152]{1,0:T(8,128)(2,1)S(1)}, bf16[272,1152]{1,0:T(8,128)(2,1)S(1)}, bf16[272,1152]{1,0:T(8,128)(2,1)S(1)}, bf16[272,1152]{1,0:T(8,128)(2,1)S(1)}) custom-call(s32[10]{0:T(128)S(1)} %stack.72.at_ref, bf16[528,1152]{1,0:T(8,128)(2,1)} %collective-permute-done.5.refs_0_, bf16[528,1152]{1,0:T(8,128)(2,1)} %collective-permute-done.refs_1_, ...), custom_call_target="tpu_custom_call" | custom-call | flops 34500001792 | bytes 1 | tf_op jit(solution)/shard_map/pick/pallas_call | solution.py:184
  41.5 1.5 %collective-permute-start.8 = (bf16[272,1152]{1,0:T(8,128)(2,1)S(1)}, bf16[272,1152]{1,0:T(8,128)(2,1)S(1)}, u32[]{:S(2)}, u32[]{:S(2)}) collective-permute-start(bf16[272,1152]{1,0:T(8,128)(2,1)S(1)} %get-tuple-element.55), channel_id=1, source_target_pairs={{0,2},{2,0},{4,6},{6,4},{1,3},{3,1},{5,7},{7,5},{8,10},{10,8},{12,... | collective-permute-start | bytes 1880072 | tf_op jit(solution)/shard_map/ppermute | solution.py:558
  43.1 1.5 %collective-permute-start.9 = (bf16[272,1152]{1,0:T(8,128)(2,1)S(1)}, bf16[272,1152]{1,0:T(8,128)(2,1)S(1)}, u32[]{:S(2)}, u32[]{:S(2)}) collective-permute-start(bf16[272,1152]{1,0:T(8,128)(2,1)S(1)} %get-tuple-element.56), channel_id=1, source_target_pairs={{0,4},{2,6},{4,0},{6,2},{1,5},{3,7},{5,1},{7,3},{8,12},{10,14},{12... | collective-permute-start | bytes 1880072 | tf_op jit(solution)/shard_map/ppermute | solution.py:558
  45.1 3.8 %learn.4 = (f32[1152,768]{1,0:T(8,128)S(1)}, f32[2,768]{1,0:T(2,128)S(1)}) custom-call(s32[2]{0:T(128)S(1)} %pad_add_fusion.at_ref, bf16[144,1152]{1,0:T(8,128)(2,1)S(1)} %get-tuple-element.58.refs_0_, bf16[144,1152]{1,0:T(8,128)(2,1)S(1)} %collective-permute-done.1.refs_1_, bf16[144,1152]{1,0:T(8,128)(2,1)S(1)} %collective-permute-done.2.refs_2_, ...), custom_call_target="tpu_custom_call" | custom-call | flops 1 | bytes 1 | tf_op jit(solution)/shard_map/learn/pallas_call | solution.py:412
  48.8 15.1 %collective-permute-done.4.refs_1_ = bf16[528,1152]{1,0:T(8,128)(2,1)S(1)} collective-permute-done((bf16[528,1152]{1,0:T(8,128)(2,1)}, bf16[528,1152]{1,0:T(8,128)(2,1)S(1)}, u32[]{:S(2)}, u32[]{:S(2)}) %collective-permute-start.4) | collective-permute-done | bytes 1216544 | tf_op jit(solution)/shard_map/ppermute | solution.py:583
  63.9 4.4 %collective-permute-start.7 = (bf16[528,1152]{1,0:T(8,128)(2,1)S(1)}, bf16[528,1152]{1,0:T(8,128)(2,1)S(1)}, u32[]{:S(2)}, u32[]{:S(2)}) collective-permute-start(bf16[528,1152]{1,0:T(8,128)(2,1)S(1)} %pack.1), channel_id=1, source_target_pairs={{0,24},{24,0},{1,25},{25,1},{2,26},{26,2},{3,27},{27,3},{4,28},{28... | collective-permute-start | bytes 3649544 | tf_op jit(solution)/shard_map/ppermute | solution.py:595
  68.3 2.5 %pick.5 = (bf16[144,1152]{1,0:T(8,128)(2,1)S(1)}, bf16[144,1152]{1,0:T(8,128)(2,1)S(1)}, bf16[144,1152]{1,0:T(8,128)(2,1)S(1)}, bf16[144,1152]{1,0:T(8,128)(2,1)S(1)}) custom-call(s32[5]{0:T(128)S(1)} %stack.74.at_ref, bf16[528,1152]{1,0:T(8,128)(2,1)S(1)} %collective-permute-done.6.refs_0_, bf16[528,1152]{1,0:T(8,128)(2,1)S(1)} %collective-permute-done.4.refs_1_), custom_call_target="tpu_custom_call" | custom-call | flops 11500000256 | bytes 1 | tf_op jit(solution)/shard_map/pick/pallas_call | solution.py:184
  72.4 1.5 %collective-permute-start.12 = (bf16[144,1152]{1,0:T(8,128)(2,1)S(1)}, bf16[144,1152]{1,0:T(8,128)(2,1)S(1)}, u32[]{:S(2)}, u32[]{:S(2)}) collective-permute-start(bf16[144,1152]{1,0:T(8,128)(2,1)S(1)} %get-tuple-element.73), channel_id=1, source_target_pairs={{0,4},{2,6},{4,0},{6,2},{1,5},{3,7},{5,1},{7,3},{8,12},{10,14},{12... | collective-permute-start | bytes 995336 | tf_op jit(solution)/shard_map/ppermute | solution.py:558
  74.7 6.0 %learn.5 = (f32[1152,768]{1,0:T(8,128)S(1)}, f32[2,768]{1,0:T(2,128)S(1)}) custom-call(s32[2]{0:T(128)S(1)} %pad_add_fusion.1.at_ref, bf16[272,1152]{1,0:T(8,128)(2,1)S(1)} %get-tuple-element.54.refs_0_, bf16[272,1152]{1,0:T(8,128)(2,1)S(1)} %collective-permute-done.8.refs_1_, bf16[272,1152]{1,0:T(8,128)(2,1)S(1)} %collective-permute-done.9.refs_2_, ...), custom_call_target="tpu_custom_call" | custom-call | flops 46000001024 | bytes 1 | tf_op jit(solution)/shard_map/learn/pallas_call | solution.py:412
  81.9 5.1 %collective-permute-done.12.refs_2_ = bf16[144,1152]{1,0:T(8,128)(2,1)S(1)} collective-permute-done((bf16[144,1152]{1,0:T(8,128)(2,1)S(1)}, bf16[144,1152]{1,0:T(8,128)(2,1)S(1)}, u32[]{:S(2)}, u32[]{:S(2)}) %collective-permute-start.12) | collective-permute-done | bytes 331808 | tf_op jit(solution)/shard_map/ppermute | solution.py:558
  87.0 3.7 %learn.6 = (f32[1152,768]{1,0:T(8,128)S(1)}, f32[2,768]{1,0:T(2,128)S(1)}) custom-call(s32[2]{0:T(128)S(1)} %pad_add_fusion.1.at_ref, bf16[144,1152]{1,0:T(8,128)(2,1)S(1)} %get-tuple-element.71.refs_0_, bf16[144,1152]{1,0:T(8,128)(2,1)S(1)} %collective-permute-done.11.refs_1_, bf16[144,1152]{1,0:T(8,128)(2,1)S(1)} %collective-permute-done.12.refs_2_, ...), custom_call_target="tpu_custom_call" | custom-call | flops 23000000512 | bytes 1 | tf_op jit(solution)/shard_map/learn/pallas_call | solution.py:412
  90.8 3.8 %collective-permute-done.7.refs_0_ = bf16[528,1152]{1,0:T(8,128)(2,1)S(1)} collective-permute-done((bf16[528,1152]{1,0:T(8,128)(2,1)S(1)}, bf16[528,1152]{1,0:T(8,128)(2,1)S(1)}, u32[]{:S(2)}, u32[]{:S(2)}) %collective-permute-start.7) | collective-permute-done | bytes 1216544 | tf_op jit(solution)/shard_map/ppermute | solution.py:595
  94.6 3.5 %learn.7 = (f32[584,768]{1,0:T(8,128)S(1)}, f32[2,768]{1,0:T(2,128)S(1)}, bf16[512,768]{1,0:T(8,128)(2,1)S(1)}) custom-call(s32[2]{0:T(128)S(1)} %pad_add_fusion.1.at_ref, bf16[528,1152]{1,0:T(8,128)(2,1)S(1)} %collective-permute-done.7.refs_0_, bf16[1152,768]{1,0:T(8,128)(2,1)S(1)} %bitcast.18, bf16[1,768]{1,0:T(2,128)(2,1)S(1)} %copy-done.5, ...), custom_call_target="tpu_custom_call" | custom-call | flops 1 | bytes 1 | tf_op jit(solution)/shard_map/learn/pallas_call | solution.py:412
  99.4 2.5 %collective-permute-done.14.got.got_vec = f32[584,768]{1,0:T(8,128)S(1)} collective-permute-done((f32[584,768]{1,0:T(8,128)S(1)}, f32[584,768]{1,0:T(8,128)S(1)}, u32[]{:S(2)}, u32[]{:S(2)}) %collective-permute-start.14) | collective-permute-done | bytes 1794080 | tf_op jit(solution)/shard_map/ppermute | solution.py:612
  103.5 2.6 %moments.1 = (bf16[1,1152,768]{2,1,0:T(8,128)(2,1)}, bf16[1,2,768]{2,1,0:T(2,128)(2,1)}, f32[1,576,768]{2,1,0:T(8,128)}, f32[1,576,768]{2,1,0:T(8,128)}, f32[1,2,768]{2,1,0:T(2,128)}, /*index=5*/f32[1,2,768]{2,1,0:T(2,128)}) custom-call(s32[1]{0:T(128)} %bitcast.at_ref, f32[576,768]{1,0:T(8,128)S(1)} %keep.1.kept, ...), custom_call_target="tpu_custom_call" | custom-call | flops 3450000128 | bytes 1 | tf_op jit(solution)/shard_map/moments/pallas_call | solution.py:493
  (44 shorter events, 12.8 us)
Async XLA Ops:
  2.8 28.3 %collective-permute-start = (bf16[528,1152]{1,0:T(8,128)(2,1)}, bf16[528,1152]{1,0:T(8,128)(2,1)}, u32[]{:S(2)}, u32[]{:S(2)}) collective-permute-start(bf16[528,1152]{1,0:T(8,128)(2,1)} %shard.1.refs_0_.refs_2_), channel_id=1, source_target_pairs={{8,16},{16,8},{9,17},{17,9},{10,18},{18,10},{11,19},{19,11},{12,20... | collective-permute-start | bytes 3649544 | tf_op jit(solution)/shard_map/ppermute | solution.py:567
  4.5 31.7 %collective-permute-start.5 = (bf16[528,1152]{1,0:T(8,128)(2,1)}, bf16[528,1152]{1,0:T(8,128)(2,1)}, u32[]{:S(2)}, u32[]{:S(2)}) collective-permute-start(bf16[528,1152]{1,0:T(8,128)(2,1)} %shard.1.refs_0_.refs_2_), channel_id=1, source_target_pairs={{0,8},{8,0},{16,24},{24,16},{1,9},{9,1},{17,25},{25,17},{2,10},{10... | collective-permute-start | bytes 3649544 | tf_op jit(solution)/shard_map/ppermute | solution.py:568
  10.8 26.2 %copy-start.2 = (bf16[528,1152]{1,0:T(8,128)(2,1)S(1)}, bf16[528,1152]{1,0:T(8,128)(2,1)}, u32[]{:S(2)}) copy-start(bf16[528,1152]{1,0:T(8,128)(2,1)} %shard.1.refs_0_.refs_2_) | copy-start | bytes 3649540
  13.1 10.8 %collective-permute-start.1 = (bf16[144,1152]{1,0:T(8,128)(2,1)S(1)}, bf16[144,1152]{1,0:T(8,128)(2,1)S(1)}, u32[]{:S(2)}, u32[]{:S(2)}) collective-permute-start(bf16[144,1152]{1,0:T(8,128)(2,1)S(1)} %get-tuple-element.49), channel_id=1, source_target_pairs={{0,2},{2,0},{4,6},{6,4},{1,3},{3,1},{5,7},{7,5},{8,10},{10,8},{12,... | collective-permute-start | bytes 995336 | tf_op jit(solution)/shard_map/ppermute | solution.py:558
  14.6 15.8 %collective-permute-start.2 = (bf16[144,1152]{1,0:T(8,128)(2,1)S(1)}, bf16[144,1152]{1,0:T(8,128)(2,1)S(1)}, u32[]{:S(2)}, u32[]{:S(2)}) collective-permute-start(bf16[144,1152]{1,0:T(8,128)(2,1)S(1)} %get-tuple-element.50), channel_id=1, source_target_pairs={{0,4},{2,6},{4,0},{6,2},{1,5},{3,7},{5,1},{7,3},{8,12},{10,14},{12... | collective-permute-start | bytes 995336 | tf_op jit(solution)/shard_map/ppermute | solution.py:558
  16.2 14.3 %collective-permute-start.3 = (bf16[144,1152]{1,0:T(8,128)(2,1)S(1)}, bf16[144,1152]{1,0:T(8,128)(2,1)S(1)}, u32[]{:S(2)}, u32[]{:S(2)}) collective-permute-start(bf16[144,1152]{1,0:T(8,128)(2,1)S(1)} %get-tuple-element.51), channel_id=1, source_target_pairs={{0,6},{2,4},{4,2},{6,0},{1,7},{3,5},{5,3},{7,1},{8,14},{10,12},{12... | collective-permute-start | bytes 995336 | tf_op jit(solution)/shard_map/ppermute | solution.py:558
  31.0 14.0 %copy-start = (bf16[1,1152,768]{2,1,0:T(8,128)(2,1)S(1)}, bf16[1,1152,768]{2,1,0:T(8,128)(2,1)}, u32[]{:S(2)}) copy-start(bf16[1,1152,768]{2,1,0:T(8,128)(2,1)} %param.13) | copy-start | bytes 5308420
  31.0 14.0 %copy-start.5 = (bf16[1,768]{1,0:T(2,128)(2,1)S(1)}, bf16[1,768]{1,0:T(2,128)(2,1)}, u32[]{:S(2)}) copy-start(bf16[1,768]{1,0:T(2,128)(2,1)} %bias.1) | copy-start | bytes 4612
  31.1 14.0 %copy-start.6 = (bf16[1,768]{1,0:T(2,128)(2,1)S(1)}, bf16[1,768]{1,0:T(2,128)(2,1)}, u32[]{:S(2)}) copy-start(bf16[1,768]{1,0:T(2,128)(2,1)} %out.1) | copy-start | bytes 4612
  31.1 32.8 %collective-permute-start.4 = (bf16[528,1152]{1,0:T(8,128)(2,1)}, bf16[528,1152]{1,0:T(8,128)(2,1)S(1)}, u32[]{:S(2)}, u32[]{:S(2)}) collective-permute-start(bf16[528,1152]{1,0:T(8,128)(2,1)} %collective-permute-done.refs_1_), channel_id=1, source_target_pairs={{8,0},{16,24},{9,1},{17,25},{10,2},{18,26},{11,3},{19,27},{12,4},{... | collective-permute-start | bytes 3649544 | tf_op jit(solution)/shard_map/ppermute | solution.py:583
  36.2 12.6 %collective-permute-start.6 = (bf16[528,1152]{1,0:T(8,128)(2,1)}, bf16[528,1152]{1,0:T(8,128)(2,1)S(1)}, u32[]{:S(2)}, u32[]{:S(2)}) collective-permute-start(bf16[528,1152]{1,0:T(8,128)(2,1)} %collective-permute-done.5.refs_0_), channel_id=1, source_target_pairs={{8,16},{16,8},{9,17},{17,9},{10,18},{18,10},{11,19},{19,11},{12,20... | collective-permute-start | bytes 3649544 | tf_op jit(solution)/shard_map/ppermute | solution.py:584
  41.5 29.3 %collective-permute-start.8 = (bf16[272,1152]{1,0:T(8,128)(2,1)S(1)}, bf16[272,1152]{1,0:T(8,128)(2,1)S(1)}, u32[]{:S(2)}, u32[]{:S(2)}) collective-permute-start(bf16[272,1152]{1,0:T(8,128)(2,1)S(1)} %get-tuple-element.55), channel_id=1, source_target_pairs={{0,2},{2,0},{4,6},{6,4},{1,3},{3,1},{5,7},{7,5},{8,10},{10,8},{12,... | collective-permute-start | bytes 1880072 | tf_op jit(solution)/shard_map/ppermute | solution.py:558
  43.1 28.1 %collective-permute-start.9 = (bf16[272,1152]{1,0:T(8,128)(2,1)S(1)}, bf16[272,1152]{1,0:T(8,128)(2,1)S(1)}, u32[]{:S(2)}, u32[]{:S(2)}) collective-permute-start(bf16[272,1152]{1,0:T(8,128)(2,1)S(1)} %get-tuple-element.56), channel_id=1, source_target_pairs={{0,4},{2,6},{4,0},{6,2},{1,5},{3,7},{5,1},{7,3},{8,12},{10,14},{12... | collective-permute-start | bytes 1880072 | tf_op jit(solution)/shard_map/ppermute | solution.py:558
  44.6 26.6 %collective-permute-start.10 = (bf16[272,1152]{1,0:T(8,128)(2,1)S(1)}, bf16[272,1152]{1,0:T(8,128)(2,1)S(1)}, u32[]{:S(2)}, u32[]{:S(2)}) collective-permute-start(bf16[272,1152]{1,0:T(8,128)(2,1)S(1)} %get-tuple-element.57), channel_id=1, source_target_pairs={{0,6},{2,4},{4,2},{6,0},{1,7},{3,5},{5,3},{7,1},{8,14},{10,12},{12... | collective-permute-start | bytes 1880072 | tf_op jit(solution)/shard_map/ppermute | solution.py:558
  63.9 30.7 %collective-permute-start.7 = (bf16[528,1152]{1,0:T(8,128)(2,1)S(1)}, bf16[528,1152]{1,0:T(8,128)(2,1)S(1)}, u32[]{:S(2)}, u32[]{:S(2)}) collective-permute-start(bf16[528,1152]{1,0:T(8,128)(2,1)S(1)} %pack.1), channel_id=1, source_target_pairs={{0,24},{24,0},{1,25},{25,1},{2,26},{26,2},{3,27},{27,3},{4,28},{28... | collective-permute-start | bytes 3649544 | tf_op jit(solution)/shard_map/ppermute | solution.py:595
  71.2 10.7 %collective-permute-start.11 = (bf16[144,1152]{1,0:T(8,128)(2,1)S(1)}, bf16[144,1152]{1,0:T(8,128)(2,1)S(1)}, u32[]{:S(2)}, u32[]{:S(2)}) collective-permute-start(bf16[144,1152]{1,0:T(8,128)(2,1)S(1)} %get-tuple-element.72), channel_id=1, source_target_pairs={{0,2},{2,0},{4,6},{6,4},{1,3},{3,1},{5,7},{7,5},{8,10},{10,8},{12,... | collective-permute-start | bytes 995336 | tf_op jit(solution)/shard_map/ppermute | solution.py:558
  72.4 14.6 %collective-permute-start.12 = (bf16[144,1152]{1,0:T(8,128)(2,1)S(1)}, bf16[144,1152]{1,0:T(8,128)(2,1)S(1)}, u32[]{:S(2)}, u32[]{:S(2)}) collective-permute-start(bf16[144,1152]{1,0:T(8,128)(2,1)S(1)} %get-tuple-element.73), channel_id=1, source_target_pairs={{0,4},{2,6},{4,0},{6,2},{1,5},{3,7},{5,1},{7,3},{8,12},{10,14},{12... | collective-permute-start | bytes 995336 | tf_op jit(solution)/shard_map/ppermute | solution.py:558
  73.9 13.1 %collective-permute-start.13 = (bf16[144,1152]{1,0:T(8,128)(2,1)S(1)}, bf16[144,1152]{1,0:T(8,128)(2,1)S(1)}, u32[]{:S(2)}, u32[]{:S(2)}) collective-permute-start(bf16[144,1152]{1,0:T(8,128)(2,1)S(1)} %get-tuple-element.74), channel_id=1, source_target_pairs={{0,6},{2,4},{4,2},{6,0},{1,7},{3,5},{5,3},{7,1},{8,14},{10,12},{12... | collective-permute-start | bytes 995336 | tf_op jit(solution)/shard_map/ppermute | solution.py:558
  98.1 3.8 %collective-permute-start.14 = (f32[584,768]{1,0:T(8,128)S(1)}, f32[584,768]{1,0:T(8,128)S(1)}, u32[]{:S(2)}, u32[]{:S(2)}) collective-permute-start(f32[584,768]{1,0:T(8,128)S(1)} %get-tuple-element.82), channel_id=1, source_target_pairs={{0,1},{1,0},{2,3},{3,2},{4,5},{5,4},{6,7},{7,6},{8,9},{9,8},{10,11... | collective-permute-start | bytes 5382152 | tf_op jit(solution)/shard_map/ppermute | solution.py:612
  98.2 3.7 %copy-start.3 = (f32[1,576,768]{2,1,0:T(8,128)S(1)}, f32[1,576,768]{2,1,0:T(8,128)}, u32[]{:S(2)}) copy-start(f32[1,576,768]{2,1,0:T(8,128)} %first_w.3) | copy-start | bytes 5308420
  98.2 3.7 %copy-start.4 = (f32[1,576,768]{2,1,0:T(8,128)S(1)}, f32[1,576,768]{2,1,0:T(8,128)}, u32[]{:S(2)}) copy-start(f32[1,576,768]{2,1,0:T(8,128)} %second_w.3) | copy-start | bytes 5308420
  99.4 4.0 %copy-start.7 = (f32[1,2,768]{2,1,0:T(2,128)S(1)}, f32[1,2,768]{2,1,0:T(2,128)}, u32[]{:S(2)}) copy-start(f32[1,2,768]{2,1,0:T(2,128)} %first_vec.1) | copy-start | bytes 18436
  99.4 4.0 %copy-start.8 = (f32[1,2,768]{2,1,0:T(2,128)S(1)}, f32[1,2,768]{2,1,0:T(2,128)}, u32[]{:S(2)}) copy-start(f32[1,2,768]{2,1,0:T(2,128)} %second_vec.1) | copy-start | bytes 18436
  103.2 2.8 %collective-permute-start.15 = (bf16[576,768]{1,0:T(8,128)(2,1)S(1)}, bf16[576,768]{1,0:T(8,128)(2,1)S(1)}, u32[]{:S(2)}, u32[]{:S(2)}) collective-permute-start(bf16[576,768]{1,0:T(8,128)(2,1)S(1)} %weights.1.half_rows), channel_id=1, source_target_pairs={{0,1},{1,0},{2,3},{3,2},{4,5},{5,4},{6,7},{7,6},{8,9},{9,8},{10,11... | collective-permute-start | bytes 2654216 | tf_op jit(solution)/shard_map/ppermute | solution.py:492
  (1 other events, 1.3 us)

commit v8 on v7

--- a/solution.py
+++ b/solution.py
@@ -12,7 +12,7 @@
 learn_rate = 0.001
 epsilon = 1e-08
 swap = [(0, 1), (1, 0)]
-PB, PC, LA, LB, LC, LF = (30, 10, 0, 40, 20, 0)
+PB, PC, LA, LB, LC, LF = (30, 5, 0, 5, 0, 0)
 bf16 = jnp.bfloat16
 MIB = 1024 * 1024
 ROOM = 60
@@ -246,18 +246,20 @@
     )(*parts)
 
 
-def learn_kernel(unit, spots, n_parts, last, with_total, half_rows, at_ref, *refs):
+def learn_kernel(unit, spots, n_parts, mode, with_total, half_rows, at_ref, *refs):
     parts, refs = refs[:n_parts], refs[n_parts:]
     w_ref, bias_ref, out_ref, refs = refs[0], refs[1], refs[2], refs[3:]
     if with_total:
         total_ref, vec_ref, refs = refs[0], refs[1], refs[2:]
-    if last:
-        given_ref, new_vec_ref, low_ref, refs = refs[0], refs[1], refs[2], refs[3:]
-        rows_ref, wide_ref, mark_ref, target_ref, sems = refs
+    if mode == "rows":
+        low_ref, new_vec_ref, refs = refs[0], refs[1], refs[2:]
+        rows_ref, mark_ref, target_ref, sems = refs
+    elif mode == "halves":
+        kept_ref, given_ref, new_vec_ref, refs = refs[0], refs[1], refs[2], refs[3:]
+        rows_ref, low_ref, mark_ref, target_ref, sems = refs
     else:
         new_total_ref, new_vec_ref, refs = refs[0], refs[1], refs[2:]
         rows_ref, low_ref, mark_ref, target_ref, sems = refs
-    low_cut = half_rows // 128 * 128
     rows_all, feature = rows_ref.shape
     loads = []
     for i in range(n_parts):
@@ -323,34 +325,33 @@
             piece = piece + total_ref[first : first + size, :]
         return piece
 
+    new_vec_ref[...] = jnp.zeros(new_vec_ref.shape, f32)
+    new_vec_ref[0:1, :] = grad_bias
+    new_vec_ref[1:2, :] = grad_out
+    if mode == "rows":
+        return
     tile = 128 * max(n for n in range(1, 5) if feature % (128 * n) == 0)
-    if not last:
+    if mode == "total":
         for first in range(0, feature, tile):
             new_total_ref[first : first + tile, :] = product(first, tile)
-        new_vec_ref[0:1, :] = grad_bias
-        new_vec_ref[1:2, :] = grad_out
         return
-    first = pl.multiple_of((1 - at_ref[0]) * low_cut, 128)
-    skip = pl.multiple_of((1 - at_ref[0]) * (half_rows - low_cut), 8)
-    wide_ref[...] = lax.dot_general(
-        rows_ref[:, pl.ds(first, feature - low_cut)],
-        low_ref[...],
-        (((0,), (0,)), ((), ())),
-        preferred_element_type=f32,
-    )
-    other = pl.multiple_of((1 - at_ref[0]) * half_rows, 8)
-    given_ref[0:half_rows, :] = (
-        wide_ref[pl.ds(skip, half_rows), :] + total_ref[pl.ds(other, half_rows), :]
-    )
-    given_ref[half_rows : half_rows + 8, :] = jnp.zeros((8, hid), f32)
-    given_ref[half_rows : half_rows + 1, :] = grad_bias
-    given_ref[half_rows + 1 : half_rows + 2, :] = grad_out
-    new_vec_ref[0:1, :] = grad_bias
-    new_vec_ref[1:2, :] = grad_out
+    given_ref[half_rows:, :] = new_vec_ref[...]
+    for first in range(0, feature, tile):
+        piece = product(first, tile)
+        cut = min(max(half_rows - first, 0), tile)
+        for core in range(2):
+            low_half, high_half = (kept_ref, given_ref) if core == 0 else (given_ref, kept_ref)
+
+            @pl.when(at_ref[0] == core)
+            def _():
+                if cut > 0:
+                    low_half[first : first + cut, :] = piece[:cut]
+                if cut < tile:
+                    high_half[first + cut - half_rows : first + tile - half_rows, :] = piece[cut:]
 
 
 def keep_kernel(half_rows, low_cut, unit, spots, n_parts, at_ref, *refs):
-    parts, (low_ref, total_ref, out_ref, rows_ref, wide_ref, sems) = refs[:n_parts], refs[n_parts:]
+    parts, (low_ref, kept_ref, out_ref, rows_ref, wide_ref, sems) = refs[:n_parts], refs[n_parts:]
     feature = rows_ref.shape[1]
     loads = []
     for u, (part, at, _) in enumerate(spots):
@@ -371,13 +372,12 @@
         (((0,), (0,)), ((), ())),
         preferred_element_type=f32,
     )
-    own = pl.multiple_of(at_ref[0] * half_rows, 8)
-    out_ref[...] = wide_ref[pl.ds(skip, half_rows), :] + total_ref[pl.ds(own, half_rows), :]
-
-
-def keep(unit, spots, parts, at, low, total):
-    feature, hid = total.shape
-    half = feature // 2
+    out_ref[...] = wide_ref[pl.ds(skip, half_rows), :] + kept_ref[...]
+
+
+def keep(unit, spots, parts, at, low, kept):
+    feature = parts[0].shape[1]
+    half, hid = kept.shape
     low_cut = half // 128 * 128
     return pl.pallas_call(
         functools.partial(keep_kernel, half, low_cut, unit, spots, len(parts)),
@@ -392,22 +392,23 @@
         compiler_params=params(16),
         cost_estimate=spent(2),
         name="keep",
-    )(at, *parts, low, total)
-
-
-def learn(unit, spots, parts, at, w, bias, out, total, cost, last):
+    )(at, *parts, low, kept)
+
+
+def learn(unit, spots, parts, at, w, bias, out, total, cost, mode):
     feature, hid = w.shape
     rows_all = len(spots) * unit
     half = feature // 2
-    if last:
-        outs = (sds((half + 8, hid), f32), sds((2, hid), f32), sds((rows_all, hid), bf16))
-        work = pltpu.VMEM((feature - half // 128 * 128, hid), f32)
+    work = (pltpu.VMEM((rows_all, hid), bf16),)
+    if mode == "rows":
+        outs, work = (sds((rows_all, hid), bf16), sds((8, hid), f32)), ()
+    elif mode == "halves":
+        outs = (sds((half, hid), f32), sds((half + 8, hid), f32), sds((8, hid), f32))
     else:
-        outs = (sds((feature, hid), f32), sds((2, hid), f32))
-        work = pltpu.VMEM((rows_all, hid), bf16)
+        outs = (sds((feature, hid), f32), sds((8, hid), f32))
     extra = () if total is None else total
     kernel = functools.partial(
-        learn_kernel, unit, spots, len(parts), last, total is not None, half
+        learn_kernel, unit, spots, len(parts), mode, total is not None, half
     )
     return pl.pallas_call(
         kernel,
@@ -416,7 +417,7 @@
         out_specs=(VMEM,) * len(outs),
         scratch_shapes=[
             pltpu.VMEM((rows_all, feature), bf16),
-            work,
+            *work,
             pltpu.VMEM((len(parts), 16, feature), bf16),
             pltpu.VMEM((rows_all, 1), f32),
             pltpu.SemaphoreType.DMA((2, max(len(parts), len(spots)))),
@@ -434,23 +435,43 @@
     return new.astype(bf16), new_first, new_second
 
 
-def weights_kernel(at_ref, kept, got, w, first_w, second_w, new_half):
-    new, _, _ = adam(w[...].astype(f32), kept[...] + got[...], first_w[0], second_w[0])
-    new_half[...] = new
+def weights_kernel(
+    low_cut, n_tiles, at_ref, rows_ref, low_ref, kept, got, w, first_w, second_w, new_half, grad_ref, wide_ref
+):
+    half = kept.shape[0]
+    first = pl.multiple_of(at_ref[0] * low_cut, 128)
+    skip = pl.multiple_of(at_ref[0] * (half - low_cut), 8)
+    own = pl.multiple_of(at_ref[0] * half, 16)
+    wide_ref[...] = lax.dot_general(
+        rows_ref[0 : low_ref.shape[0], pl.ds(first, rows_ref.shape[1] - low_cut)],
+        low_ref[...],
+        (((0,), (0,)), ((), ())),
+        preferred_element_type=f32,
+    )
+    tile = half // n_tiles
+    for i in range(n_tiles):
+        span = pl.ds(i * tile, tile)
+        there = pl.ds(pl.multiple_of(own + i * tile, 16), tile)
+        there_wide = pl.ds(pl.multiple_of(skip + i * tile, 8), tile)
+        grad = kept[span, :] + got[span, :] + wide_ref[there_wide, :]
+        new, _, _ = adam(w[there, :].astype(f32), grad, first_w[0, span, :], second_w[0, span, :])
+        new_half[span, :] = new
+        grad_ref[span, :] = grad
 
 
 def moments_kernel(
-    at_ref, kept, got, kept_vec, got_vec, half_rows, first_w, second_w, bias, out, first_vec, second_vec,
+    at_ref, grad_ref, vec_near, vec_far, vec_other, got_vec, half_rows, first_w, second_w, bias, out,
+    first_vec, second_vec,
     new_full, new_vec, new_first_w, new_second_w, new_first_vec, new_second_vec,
 ):
-    grad = kept[...] + got[...]
+    grad = grad_ref[...]
     new_full[0] = half_rows[...]
     new_first_w[0] = beta_one * first_w[0] + (1.0 - beta_one) * grad
     new_second_w[0] = beta_two * second_w[0] + (1.0 - beta_two) * grad * grad
 
     @pl.when(pl.program_id(0) == 0)
     def _():
-        vec = kept_vec[...] + got_vec[0:2, :]
+        vec = (vec_near[0:2, :] + vec_far[0:2, :]) + (got_vec[0:2, :] + vec_other[0:2, :])
         for row, old in enumerate((bias, out)):
             fresh, fresh_first, fresh_second = adam(
                 old[...].astype(f32),
@@ -463,39 +484,38 @@
             new_second_vec[0, row : row + 1] = fresh_second
 
 
-def take_step(rep, kept, kept_vec, got, w_in, bias, out, first_w, second_w, first_vec, second_vec):
+def take_step(
+    rep, rows, low, kept, got, vecs, w_in, bias, out, first_w, second_w, first_vec, second_vec
+):
     feature, hid = w_in.shape
     half = feature // 2
+    low_cut = half // 128 * 128
     tiles = max(n for n in range(1, 3) if half % (16 * n) == 0)
     tile = half // tiles
     here = pl.BlockSpec((tile, hid), lambda i, at: (i, 0))
-    there = pl.BlockSpec((tile, hid), lambda i, at: (at[0] * tiles + i, 0))
     tail = pl.BlockSpec((8, hid), lambda i, at: (half // 8, 0))
+    top = pl.BlockSpec((8, hid), lambda i, at: (0, 0))
     moment = pl.BlockSpec((1, tile, hid), lambda i, at: (0, i, 0))
     row = pl.BlockSpec((1, hid), lambda i, at: (0, 0))
-    pair = pl.BlockSpec((2, hid), lambda i, at: (0, 0))
     pairs = pl.BlockSpec((1, 2, hid), lambda i, at: (0, 0, 0))
     full = pl.BlockSpec((1, tile, hid), lambda i, at: (0, at[0] * tiles + i, 0))
-    new_half = pl.pallas_call(
-        weights_kernel,
-        grid_spec=pltpu.PrefetchScalarGridSpec(
-            num_scalar_prefetch=1,
-            grid=(tiles,),
-            in_specs=[here, here, there, moment, moment],
-            out_specs=here,
-        ),
-        out_shape=sds((half, hid), bf16),
+    new_half, grad = pl.pallas_call(
+        functools.partial(weights_kernel, low_cut, 2 * tiles),
+        in_specs=[SMEM] + [VMEM] * 7,
+        out_specs=[VMEM, VMEM],
+        out_shape=(sds((half, hid), bf16), sds((half, hid), f32)),
+        scratch_shapes=[pltpu.VMEM((feature - low_cut, hid), f32)],
         compiler_params=params(16),
         cost_estimate=spent(2),
         name="weights",
-    )(rep, kept, got, w_in, first_w, second_w)
+    )(rep, rows, low, kept, got, w_in, first_w, second_w)
     other = lax.ppermute(new_half, "rep", swap)
     new_full, *rest = pl.pallas_call(
         moments_kernel,
         grid_spec=pltpu.PrefetchScalarGridSpec(
             num_scalar_prefetch=1,
             grid=(tiles,),
-            in_specs=[here, here, pair, tail, here, moment, moment, row, row, pairs, pairs],
+            in_specs=[here, top, top, top, tail, here, moment, moment, row, row, pairs, pairs],
             out_specs=[full, pairs, moment, moment, pairs, pairs],
         ),
         out_shape=(
@@ -509,7 +529,7 @@
         compiler_params=params(16),
         cost_estimate=spent(3),
         name="moments",
-    )(rep, kept, got, kept_vec, got, new_half, first_w, second_w, bias, out, first_vec, second_vec)
+    )(rep, grad, *vecs, got, new_half, first_w, second_w, bias, out, first_vec, second_vec)
     return join(rep, other, new_full), *rest
 
 
@@ -569,9 +589,9 @@
     always = jnp.ones((), jnp.bool_)
     at_end = (z == 0) | (z == planes - 1)
 
-    def add(total, parts, spots, real, cost, last=False):
+    def add(total, parts, spots, real, cost, mode="total"):
         scalars = jnp.stack([rep[0], real]).astype(jnp.int32)
-        return learn(unit, spots, parts, scalars, w_in[0], bias_in, w_out, total, cost, last)
+        return learn(unit, spots, parts, scalars, w_in[0], bias_in, w_out, total, cost, mode)
 
     first_heads = plane_heads(jnp.where(at_end, planes - 1 - z, z))
     first_units = exchange(pick(unit, per_block, [own], [(0, 0)], first_heads, [always], 0))
@@ -602,17 +622,21 @@
         (near, [(k, g * unit, g) for k in range(heads) for g in range(2)]),
         (exchange(messages), [(k, 0, 0) for k in range(heads)]),
     ]
-    rest.append(([far_got], [(0, k * unit, k) for k in range(heads)]))
-
     for at, (parts, spots) in enumerate(rest):
-        cost = (LB, LC, LF)[min(at, 2)]
         last = at == len(rest) - 1
-        done, total = total, add(total, parts, spots, one, cost, last)
-    given, kept_vec, low = total
+        total = add(total, parts, spots, one, (LB, LC)[min(at, 1)], "halves" if last else "total")
+    kept, given, vec_near = total
     got = lax.ppermute(given, "rep", swap)
-    kept = keep(unit, spots, parts, rep, low, done[0])
+    far_other = lax.ppermute(far_got, "rep", swap)
+    spots = [(0, k * unit, k) for k in range(heads)]
+    low, vec_far = add(None, [far_got], spots, one, LF, "rows")
+    low_other = lax.ppermute(low, "rep", swap)
+    vec_other = lax.ppermute(vec_far, "rep", swap)
+    low_other, vec_other = lax.optimization_barrier((low_other, vec_other))
+    kept = keep(unit, spots, [far_got], rep, low, kept)
     return take_step(
-        rep, kept, kept_vec, got, w_in[0], bias_in, w_out, first_w, second_w, first_vec, second_vec
+        rep, far_other, low_other, kept, got, [vec_near, vec_far, vec_other], w_in[0], bias_in, w_out,
+        first_w, second_w, first_vec, second_vec,
     )
 
 

time: 107 us -> 107 us (level)
  waiting for transfers between devices: 45.2 us -> 42.2 us
  Pallas kernels: 35.2 us -> 36.9 us
    ppermute x1, waiting for transfers between devices: 2.46 us -> 0.01 us  [gathered(): got = lax.ppermute(given, 'rep', swap)]
    pallas_call x1, Pallas kernels: 1.32 us -> 2.85 us  [take_step(): pl.pallas_call(functools.partial(weights_kernel, low_cut, 2 * tiles), in_...]
    ppermute x1, waiting for transfers between devices: 3.81 us -> 2.64 us  [gathered(): far_got = lax.ppermute(far_sent, 'dp', end_pairs)]
  transfers between devices with their start and end apart: 16 -> 19, of which waited for: 9 -> 9; matrix products, arithmetic and copies ran while one was open for 0% -> 0% of each run, Pallas kernels for 25% -> 29%
where the time goes in v8:
time: 107 us
  waiting for transfers between devices  42.2 us (39%)
  Pallas kernels  36.9 us (34%)
  starting transfers between devices  24.9 us (23%)
  local copies, waits for them, and re-layouts  1.69 us (2%)
    ppermute x9, waiting for transfers between devices, exchange(): lax.ppermute(units[k], 'head', [(i, i ^ k) for i in range(heads)])  20.3 us
    pallas_call x4, Pallas kernels, learn(): pl.pallas_call(kernel, out_shape=outs, in_specs=[SMEM] + [HBM] * len(part...  17.3 us
    ppermute x1, waiting for transfers between devices, gathered(): next_out = lax.ppermute(inner, 'dp', out_pairs)  15 us
    ppermute x9, starting transfers between devices, exchange(): lax.ppermute(units[k], 'head', [(i, i ^ k) for i in range(heads)])  10.6 us
    pallas_call x3, Pallas kernels, pick(): pl.pallas_call(functools.partial(pick_kernel, unit, per_block, plan, len(...  9.38 us
    ppermute x1, starting transfers between devices, gathered(): outer = lax.ppermute(own, 'dp', outer_pairs)  4.89 us
    ppermute x1, starting transfers between devices, gathered(): far_got = lax.ppermute(far_sent, 'dp', end_pairs)  4.37 us
    ppermute x1, waiting for transfers between devices, gathered(): outer = lax.ppermute(own, 'dp', outer_pairs)  3.67 us
  transfers between devices with their start and end apart: 19, of which 9 were waited for; matrix products, arithmetic and copies ran while one was open for 0% of the time, Pallas kernels for 29%

profile of v8, /device:TPU:0, one launch (start us, length us, event | category | flops | bytes accessed | tf_op | source)
XLA Modules:
  0.0 106.9 jit_solution(8372049892920238535)
XLA Ops:
  0.6 2.2 %shard.1.refs_0_.refs_2_ = bf16[528,1152]{1,0:T(8,128)(2,1)} custom-call(s32[2,64]{1,0:T(2,128)} %bitcast.22, s32[2,8,64]{2,1,0:T(8,128)} %bitcast.21, bf16[512,1152]{1,0:T(8,128)(2,1)} %bitcast.20), custom_call_target="tpu_custom_call" | custom-call | tf_op jit(solution)/shard_map/shard/pallas_call | solution.py:100
  2.8 1.7 %collective-permute-start = (bf16[528,1152]{1,0:T(8,128)(2,1)}, bf16[528,1152]{1,0:T(8,128)(2,1)}, u32[]{:S(2)}, u32[]{:S(2)}) collective-permute-start(bf16[528,1152]{1,0:T(8,128)(2,1)} %shard.1.refs_0_.refs_2_), channel_id=1, source_target_pairs={{8,16},{16,8},{9,17},{17,9},{10,18},{18,10},{11,19},{19,11},{12,20... | collective-permute-start | bytes 3649544 | tf_op jit(solution)/shard_map/ppermute | solution.py:587
  4.5 4.9 %collective-permute-start.5 = (bf16[528,1152]{1,0:T(8,128)(2,1)}, bf16[528,1152]{1,0:T(8,128)(2,1)}, u32[]{:S(2)}, u32[]{:S(2)}) collective-permute-start(bf16[528,1152]{1,0:T(8,128)(2,1)} %shard.1.refs_0_.refs_2_), channel_id=1, source_target_pairs={{0,8},{8,0},{16,24},{24,16},{1,9},{9,1},{17,25},{25,17},{2,10},{10... | collective-permute-start | bytes 3649544 | tf_op jit(solution)/shard_map/ppermute | solution.py:588
  10.8 2.3 %pick.3 = (bf16[144,1152]{1,0:T(8,128)(2,1)S(1)}, bf16[144,1152]{1,0:T(8,128)(2,1)S(1)}, bf16[144,1152]{1,0:T(8,128)(2,1)S(1)}, bf16[144,1152]{1,0:T(8,128)(2,1)S(1)}) custom-call(s32[5]{0:T(128)S(1)} %stack.63.at_ref, bf16[528,1152]{1,0:T(8,128)(2,1)S(1)} %copy-done.1), custom_call_target="tpu_custom_call" | custom-call | flops 1 | bytes 1 | tf_op jit(solution)/shard_map/pick/pallas_call | solution.py:184
  13.1 1.6 %collective-permute-start.1 = (bf16[144,1152]{1,0:T(8,128)(2,1)S(1)}, bf16[144,1152]{1,0:T(8,128)(2,1)S(1)}, u32[]{:S(2)}, u32[]{:S(2)}) collective-permute-start(bf16[144,1152]{1,0:T(8,128)(2,1)S(1)} %get-tuple-element.53), channel_id=1, source_target_pairs={{0,2},{2,0},{4,6},{6,4},{1,3},{3,1},{5,7},{7,5},{8,10},{10,8},{12,... | collective-permute-start | bytes 995336 | tf_op jit(solution)/shard_map/ppermute | solution.py:578
  14.6 1.5 %collective-permute-start.2 = (bf16[144,1152]{1,0:T(8,128)(2,1)S(1)}, bf16[144,1152]{1,0:T(8,128)(2,1)S(1)}, u32[]{:S(2)}, u32[]{:S(2)}) collective-permute-start(bf16[144,1152]{1,0:T(8,128)(2,1)S(1)} %get-tuple-element.54), channel_id=1, source_target_pairs={{0,4},{2,6},{4,0},{6,2},{1,5},{3,7},{5,1},{7,3},{8,12},{10,14},{12... | collective-permute-start | bytes 995336 | tf_op jit(solution)/shard_map/ppermute | solution.py:578
  16.9 7.0 %collective-permute-done.1.refs_1_ = bf16[144,1152]{1,0:T(8,128)(2,1)S(1)} collective-permute-done((bf16[144,1152]{1,0:T(8,128)(2,1)S(1)}, bf16[144,1152]{1,0:T(8,128)(2,1)S(1)}, u32[]{:S(2)}, u32[]{:S(2)}) %collective-permute-start.1) | collective-permute-done | bytes 331808 | tf_op jit(solution)/shard_map/ppermute | solution.py:578
  23.9 6.6 %collective-permute-done.2.refs_2_ = bf16[144,1152]{1,0:T(8,128)(2,1)S(1)} collective-permute-done((bf16[144,1152]{1,0:T(8,128)(2,1)S(1)}, bf16[144,1152]{1,0:T(8,128)(2,1)S(1)}, u32[]{:S(2)}, u32[]{:S(2)}) %collective-permute-start.2) | collective-permute-done | bytes 331808 | tf_op jit(solution)/shard_map/ppermute | solution.py:578
  32.5 3.7 %collective-permute-done.5.refs_0_ = bf16[528,1152]{1,0:T(8,128)(2,1)} collective-permute-done((bf16[528,1152]{1,0:T(8,128)(2,1)}, bf16[528,1152]{1,0:T(8,128)(2,1)}, u32[]{:S(2)}, u32[]{:S(2)}) %collective-permute-start.5) | collective-permute-done | bytes 1216544 | tf_op jit(solution)/shard_map/ppermute | solution.py:588
  36.9 4.6 %pick.4 = (bf16[272,1152]{1,0:T(8,128)(2,1)S(1)}, bf16[272,1152]{1,0:T(8,128)(2,1)S(1)}, bf16[272,1152]{1,0:T(8,128)(2,1)S(1)}, bf16[272,1152]{1,0:T(8,128)(2,1)S(1)}) custom-call(s32[10]{0:T(128)S(1)} %stack.72.at_ref, bf16[528,1152]{1,0:T(8,128)(2,1)} %collective-permute-done.5.refs_0_, bf16[528,1152]{1,0:T(8,128)(2,1)} %collective-permute-done.refs_1_, ...), custom_call_target="tpu_custom_call" | custom-call | flops 34500001792 | bytes 1 | tf_op jit(solution)/shard_map/pick/pallas_call | solution.py:184
  41.5 1.5 %collective-permute-start.11 = (bf16[272,1152]{1,0:T(8,128)(2,1)S(1)}, bf16[272,1152]{1,0:T(8,128)(2,1)S(1)}, u32[]{:S(2)}, u32[]{:S(2)}) collective-permute-start(bf16[272,1152]{1,0:T(8,128)(2,1)S(1)} %get-tuple-element.59), channel_id=1, source_target_pairs={{0,2},{2,0},{4,6},{6,4},{1,3},{3,1},{5,7},{7,5},{8,10},{10,8},{12,... | collective-permute-start | bytes 1880072 | tf_op jit(solution)/shard_map/ppermute | solution.py:578
  43.1 1.5 %collective-permute-start.12 = (bf16[272,1152]{1,0:T(8,128)(2,1)S(1)}, bf16[272,1152]{1,0:T(8,128)(2,1)S(1)}, u32[]{:S(2)}, u32[]{:S(2)}) collective-permute-start(bf16[272,1152]{1,0:T(8,128)(2,1)S(1)} %get-tuple-element.60), channel_id=1, source_target_pairs={{0,4},{2,6},{4,0},{6,2},{1,5},{3,7},{5,1},{7,3},{8,12},{10,14},{12... | collective-permute-start | bytes 1880072 | tf_op jit(solution)/shard_map/ppermute | solution.py:578
  45.1 3.7 %learn.4 = (f32[1152,768]{1,0:T(8,128)S(1)}, f32[8,768]{1,0:T(8,128)S(1)}) custom-call(s32[2]{0:T(128)S(1)} %pad_add_fusion.at_ref, bf16[144,1152]{1,0:T(8,128)(2,1)S(1)} %get-tuple-element.62.refs_0_, bf16[144,1152]{1,0:T(8,128)(2,1)S(1)} %collective-permute-done.1.refs_1_, bf16[144,1152]{1,0:T(8,128)(2,1)S(1)} %collective-permute-done.2.refs_2_, ...), custom_call_target="tpu_custom_call" | custom-call | flops 1 | bytes 1 | tf_op jit(solution)/shard_map/learn/pallas_call | solution.py:413
  48.9 15.0 %collective-permute-done.4.refs_1_ = bf16[528,1152]{1,0:T(8,128)(2,1)S(1)} collective-permute-done((bf16[528,1152]{1,0:T(8,128)(2,1)}, bf16[528,1152]{1,0:T(8,128)(2,1)S(1)}, u32[]{:S(2)}, u32[]{:S(2)}) %collective-permute-start.4) | collective-permute-done | bytes 1216544 | tf_op jit(solution)/shard_map/ppermute | solution.py:603
  63.9 4.4 %collective-permute-start.7 = (bf16[528,1152]{1,0:T(8,128)(2,1)S(1)}, bf16[528,1152]{1,0:T(8,128)(2,1)S(1)}, u32[]{:S(2)}, u32[]{:S(2)}) collective-permute-start(bf16[528,1152]{1,0:T(8,128)(2,1)S(1)} %pack.1), channel_id=1, source_target_pairs={{0,24},{24,0},{1,25},{25,1},{2,26},{26,2},{3,27},{27,3},{4,28},{28... | collective-permute-start | bytes 3649544 | tf_op jit(solution)/shard_map/ppermute | solution.py:615
  68.3 2.5 %pick.5 = (bf16[144,1152]{1,0:T(8,128)(2,1)S(1)}, bf16[144,1152]{1,0:T(8,128)(2,1)S(1)}, bf16[144,1152]{1,0:T(8,128)(2,1)S(1)}, bf16[144,1152]{1,0:T(8,128)(2,1)S(1)}) custom-call(s32[5]{0:T(128)S(1)} %stack.74.at_ref, bf16[528,1152]{1,0:T(8,128)(2,1)S(1)} %collective-permute-done.6.refs_0_, bf16[528,1152]{1,0:T(8,128)(2,1)S(1)} %collective-permute-done.4.refs_1_), custom_call_target="tpu_custom_call" | custom-call | flops 5750000128 | bytes 1 | tf_op jit(solution)/shard_map/pick/pallas_call | solution.py:184
  72.4 1.5 %collective-permute-start.15 = (bf16[144,1152]{1,0:T(8,128)(2,1)S(1)}, bf16[144,1152]{1,0:T(8,128)(2,1)S(1)}, u32[]{:S(2)}, u32[]{:S(2)}) collective-permute-start(bf16[144,1152]{1,0:T(8,128)(2,1)S(1)} %get-tuple-element.80), channel_id=1, source_target_pairs={{0,4},{2,6},{4,0},{6,2},{1,5},{3,7},{5,1},{7,3},{8,12},{10,14},{12... | collective-permute-start | bytes 995336 | tf_op jit(solution)/shard_map/ppermute | solution.py:578
  74.7 6.0 %learn.6 = (f32[1152,768]{1,0:T(8,128)S(1)}, f32[8,768]{1,0:T(8,128)S(1)}) custom-call(s32[2]{0:T(128)S(1)} %pad_add_fusion.1.at_ref, bf16[272,1152]{1,0:T(8,128)(2,1)S(1)} %get-tuple-element.58.refs_0_, bf16[272,1152]{1,0:T(8,128)(2,1)S(1)} %collective-permute-done.11.refs_1_, bf16[272,1152]{1,0:T(8,128)(2,1)S(1)} %collective-permute-done.12.refs_2_, ...), custom_call_target="tpu_custom_call" | custom-call | flops 5750000128 | bytes 1 | tf_op jit(solution)/shard_map/learn/pallas_call | solution.py:413
  81.9 5.1 %collective-permute-done.15.refs_2_ = bf16[144,1152]{1,0:T(8,128)(2,1)S(1)} collective-permute-done((bf16[144,1152]{1,0:T(8,128)(2,1)S(1)}, bf16[144,1152]{1,0:T(8,128)(2,1)S(1)}, u32[]{:S(2)}, u32[]{:S(2)}) %collective-permute-start.15) | collective-permute-done | bytes 331808 | tf_op jit(solution)/shard_map/ppermute | solution.py:578
  87.0 4.8 %learn.7 = (f32[576,768]{1,0:T(8,128)S(1)}, f32[584,768]{1,0:T(8,128)S(1)}, f32[8,768]{1,0:T(8,128)S(1)}) custom-call(s32[2]{0:T(128)S(1)} %pad_add_fusion.1.at_ref, bf16[144,1152]{1,0:T(8,128)(2,1)S(1)} %get-tuple-element.78.refs_0_, bf16[144,1152]{1,0:T(8,128)(2,1)S(1)} %collective-permute-done.14.refs_1_, ...), custom_call_target="tpu_custom_call" | custom-call | flops 1 | bytes 1 | tf_op jit(solution)/shard_map/learn/pallas_call | solution.py:413
  91.9 2.6 %collective-permute-done.7.refs_0_ = bf16[528,1152]{1,0:T(8,128)(2,1)S(1)} collective-permute-done((bf16[528,1152]{1,0:T(8,128)(2,1)S(1)}, bf16[528,1152]{1,0:T(8,128)(2,1)S(1)}, u32[]{:S(2)}, u32[]{:S(2)}) %collective-permute-start.7) | collective-permute-done | bytes 1216544 | tf_op jit(solution)/shard_map/ppermute | solution.py:615
  94.6 2.7 %learn.5 = (bf16[512,768]{1,0:T(8,128)(2,1)S(1)}, f32[8,768]{1,0:T(8,128)S(1)}) custom-call(s32[2]{0:T(128)S(1)} %pad_add_fusion.1.at_ref, bf16[528,1152]{1,0:T(8,128)(2,1)S(1)} %collective-permute-done.7.refs_0_, bf16[1152,768]{1,0:T(8,128)(2,1)S(1)} %bitcast.18, bf16[1,768]{1,0:T(2,128)(2,1)S(1)} %copy-done.5, bf16[1,768]{1,0:T(2,128)(2,1)S(1)} %copy-done.6), custom_call_target="tpu_custom_call" | custom-call | flops 1 | bytes 1 | tf_op jit(solution)/shard_map/learn/pallas_call | solution.py:413
  100.0 2.8 %weights.1 = (bf16[576,768]{1,0:T(8,128)(2,1)S(1)}, f32[576,768]{1,0:T(8,128)S(1)}) custom-call(s32[1]{0:T(128)} %bitcast.at_ref, bf16[528,1152]{1,0:T(8,128)(2,1)S(1)} %collective-permute-done.8.rows_ref, bf16[512,768]{1,0:T(8,128)(2,1)S(1)} %collective-permute-done.9.low_ref, f32[576,768]{1,0:T(8,128)S(1)} %keep.1.kept, ...), custom_call_target="tpu_custom_call" | custom-call | flops 2300000000 | bytes 1 | tf_op jit(solution)/shard_map/weights/pallas_call | solution.py:502
  103.3 2.5 %moments.1 = (bf16[1,1152,768]{2,1,0:T(8,128)(2,1)}, bf16[1,2,768]{2,1,0:T(2,128)(2,1)}, f32[1,576,768]{2,1,0:T(8,128)}, f32[1,576,768]{2,1,0:T(8,128)}, f32[1,2,768]{2,1,0:T(2,128)}, /*index=5*/f32[1,2,768]{2,1,0:T(2,128)}) custom-call(s32[1]{0:T(128)} %bitcast.at_ref, f32[576,768]{1,0:T(8,128)S(1)} %get-tuple-element.89.grad_ref, ...), custom_call_target="tpu_custom_call" | custom-call | flops 3450000128 | bytes 1 | tf_op jit(solution)/shard_map/moments/pallas_call | solution.py:513
  (50 shorter events, 13.2 us)
Async XLA Ops:
  2.8 28.3 %collective-permute-start = (bf16[528,1152]{1,0:T(8,128)(2,1)}, bf16[528,1152]{1,0:T(8,128)(2,1)}, u32[]{:S(2)}, u32[]{:S(2)}) collective-permute-start(bf16[528,1152]{1,0:T(8,128)(2,1)} %shard.1.refs_0_.refs_2_), channel_id=1, source_target_pairs={{8,16},{16,8},{9,17},{17,9},{10,18},{18,10},{11,19},{19,11},{12,20... | collective-permute-start | bytes 3649544 | tf_op jit(solution)/shard_map/ppermute | solution.py:587
  4.5 31.7 %collective-permute-start.5 = (bf16[528,1152]{1,0:T(8,128)(2,1)}, bf16[528,1152]{1,0:T(8,128)(2,1)}, u32[]{:S(2)}, u32[]{:S(2)}) collective-permute-start(bf16[528,1152]{1,0:T(8,128)(2,1)} %shard.1.refs_0_.refs_2_), channel_id=1, source_target_pairs={{0,8},{8,0},{16,24},{24,16},{1,9},{9,1},{17,25},{25,17},{2,10},{10... | collective-permute-start | bytes 3649544 | tf_op jit(solution)/shard_map/ppermute | solution.py:588
  10.8 26.2 %copy-start.2 = (bf16[528,1152]{1,0:T(8,128)(2,1)S(1)}, bf16[528,1152]{1,0:T(8,128)(2,1)}, u32[]{:S(2)}) copy-start(bf16[528,1152]{1,0:T(8,128)(2,1)} %shard.1.refs_0_.refs_2_) | copy-start | bytes 3649540
  13.1 10.8 %collective-permute-start.1 = (bf16[144,1152]{1,0:T(8,128)(2,1)S(1)}, bf16[144,1152]{1,0:T(8,128)(2,1)S(1)}, u32[]{:S(2)}, u32[]{:S(2)}) collective-permute-start(bf16[144,1152]{1,0:T(8,128)(2,1)S(1)} %get-tuple-element.53), channel_id=1, source_target_pairs={{0,2},{2,0},{4,6},{6,4},{1,3},{3,1},{5,7},{7,5},{8,10},{10,8},{12,... | collective-permute-start | bytes 995336 | tf_op jit(solution)/shard_map/ppermute | solution.py:578
  14.6 15.8 %collective-permute-start.2 = (bf16[144,1152]{1,0:T(8,128)(2,1)S(1)}, bf16[144,1152]{1,0:T(8,128)(2,1)S(1)}, u32[]{:S(2)}, u32[]{:S(2)}) collective-permute-start(bf16[144,1152]{1,0:T(8,128)(2,1)S(1)} %get-tuple-element.54), channel_id=1, source_target_pairs={{0,4},{2,6},{4,0},{6,2},{1,5},{3,7},{5,1},{7,3},{8,12},{10,14},{12... | collective-permute-start | bytes 995336 | tf_op jit(solution)/shard_map/ppermute | solution.py:578
  16.2 14.3 %collective-permute-start.3 = (bf16[144,1152]{1,0:T(8,128)(2,1)S(1)}, bf16[144,1152]{1,0:T(8,128)(2,1)S(1)}, u32[]{:S(2)}, u32[]{:S(2)}) collective-permute-start(bf16[144,1152]{1,0:T(8,128)(2,1)S(1)} %get-tuple-element.55), channel_id=1, source_target_pairs={{0,6},{2,4},{4,2},{6,0},{1,7},{3,5},{5,3},{7,1},{8,14},{10,12},{12... | collective-permute-start | bytes 995336 | tf_op jit(solution)/shard_map/ppermute | solution.py:578
  31.0 14.1 %copy-start = (bf16[1,1152,768]{2,1,0:T(8,128)(2,1)S(1)}, bf16[1,1152,768]{2,1,0:T(8,128)(2,1)}, u32[]{:S(2)}) copy-start(bf16[1,1152,768]{2,1,0:T(8,128)(2,1)} %param.13) | copy-start | bytes 5308420
  31.0 14.1 %copy-start.5 = (bf16[1,768]{1,0:T(2,128)(2,1)S(1)}, bf16[1,768]{1,0:T(2,128)(2,1)}, u32[]{:S(2)}) copy-start(bf16[1,768]{1,0:T(2,128)(2,1)} %bias.1) | copy-start | bytes 4612
  31.1 14.1 %copy-start.6 = (bf16[1,768]{1,0:T(2,128)(2,1)S(1)}, bf16[1,768]{1,0:T(2,128)(2,1)}, u32[]{:S(2)}) copy-start(bf16[1,768]{1,0:T(2,128)(2,1)} %out.1) | copy-start | bytes 4612
  31.1 32.8 %collective-permute-start.4 = (bf16[528,1152]{1,0:T(8,128)(2,1)}, bf16[528,1152]{1,0:T(8,128)(2,1)S(1)}, u32[]{:S(2)}, u32[]{:S(2)}) collective-permute-start(bf16[528,1152]{1,0:T(8,128)(2,1)} %collective-permute-done.refs_1_), channel_id=1, source_target_pairs={{8,0},{16,24},{9,1},{17,25},{10,2},{18,26},{11,3},{19,27},{12,4},{... | collective-permute-start | bytes 3649544 | tf_op jit(solution)/shard_map/ppermute | solution.py:603
  36.2 27.7 %collective-permute-start.6 = (bf16[528,1152]{1,0:T(8,128)(2,1)}, bf16[528,1152]{1,0:T(8,128)(2,1)S(1)}, u32[]{:S(2)}, u32[]{:S(2)}) collective-permute-start(bf16[528,1152]{1,0:T(8,128)(2,1)} %collective-permute-done.5.refs_0_), channel_id=1, source_target_pairs={{8,16},{16,8},{9,17},{17,9},{10,18},{18,10},{11,19},{19,11},{12,20... | collective-permute-start | bytes 3649544 | tf_op jit(solution)/shard_map/ppermute | solution.py:604
  41.5 29.3 %collective-permute-start.11 = (bf16[272,1152]{1,0:T(8,128)(2,1)S(1)}, bf16[272,1152]{1,0:T(8,128)(2,1)S(1)}, u32[]{:S(2)}, u32[]{:S(2)}) collective-permute-start(bf16[272,1152]{1,0:T(8,128)(2,1)S(1)} %get-tuple-element.59), channel_id=1, source_target_pairs={{0,2},{2,0},{4,6},{6,4},{1,3},{3,1},{5,7},{7,5},{8,10},{10,8},{12,... | collective-permute-start | bytes 1880072 | tf_op jit(solution)/shard_map/ppermute | solution.py:578
  43.1 28.1 %collective-permute-start.12 = (bf16[272,1152]{1,0:T(8,128)(2,1)S(1)}, bf16[272,1152]{1,0:T(8,128)(2,1)S(1)}, u32[]{:S(2)}, u32[]{:S(2)}) collective-permute-start(bf16[272,1152]{1,0:T(8,128)(2,1)S(1)} %get-tuple-element.60), channel_id=1, source_target_pairs={{0,4},{2,6},{4,0},{6,2},{1,5},{3,7},{5,1},{7,3},{8,12},{10,14},{12... | collective-permute-start | bytes 1880072 | tf_op jit(solution)/shard_map/ppermute | solution.py:578
  44.6 26.6 %collective-permute-start.13 = (bf16[272,1152]{1,0:T(8,128)(2,1)S(1)}, bf16[272,1152]{1,0:T(8,128)(2,1)S(1)}, u32[]{:S(2)}, u32[]{:S(2)}) collective-permute-start(bf16[272,1152]{1,0:T(8,128)(2,1)S(1)} %get-tuple-element.61), channel_id=1, source_target_pairs={{0,6},{2,4},{4,2},{6,0},{1,7},{3,5},{5,3},{7,1},{8,14},{10,12},{12... | collective-permute-start | bytes 1880072 | tf_op jit(solution)/shard_map/ppermute | solution.py:578
  63.9 30.7 %collective-permute-start.7 = (bf16[528,1152]{1,0:T(8,128)(2,1)S(1)}, bf16[528,1152]{1,0:T(8,128)(2,1)S(1)}, u32[]{:S(2)}, u32[]{:S(2)}) collective-permute-start(bf16[528,1152]{1,0:T(8,128)(2,1)S(1)} %pack.1), channel_id=1, source_target_pairs={{0,24},{24,0},{1,25},{25,1},{2,26},{26,2},{3,27},{27,3},{4,28},{28... | collective-permute-start | bytes 3649544 | tf_op jit(solution)/shard_map/ppermute | solution.py:615
  71.2 10.7 %collective-permute-start.14 = (bf16[144,1152]{1,0:T(8,128)(2,1)S(1)}, bf16[144,1152]{1,0:T(8,128)(2,1)S(1)}, u32[]{:S(2)}, u32[]{:S(2)}) collective-permute-start(bf16[144,1152]{1,0:T(8,128)(2,1)S(1)} %get-tuple-element.79), channel_id=1, source_target_pairs={{0,2},{2,0},{4,6},{6,4},{1,3},{3,1},{5,7},{7,5},{8,10},{10,8},{12,... | collective-permute-start | bytes 995336 | tf_op jit(solution)/shard_map/ppermute | solution.py:578
  72.4 14.6 %collective-permute-start.15 = (bf16[144,1152]{1,0:T(8,128)(2,1)S(1)}, bf16[144,1152]{1,0:T(8,128)(2,1)S(1)}, u32[]{:S(2)}, u32[]{:S(2)}) collective-permute-start(bf16[144,1152]{1,0:T(8,128)(2,1)S(1)} %get-tuple-element.80), channel_id=1, source_target_pairs={{0,4},{2,6},{4,0},{6,2},{1,5},{3,7},{5,1},{7,3},{8,12},{10,14},{12... | collective-permute-start | bytes 995336 | tf_op jit(solution)/shard_map/ppermute | solution.py:578
  73.9 13.1 %collective-permute-start.16 = (bf16[144,1152]{1,0:T(8,128)(2,1)S(1)}, bf16[144,1152]{1,0:T(8,128)(2,1)S(1)}, u32[]{:S(2)}, u32[]{:S(2)}) collective-permute-start(bf16[144,1152]{1,0:T(8,128)(2,1)S(1)} %get-tuple-element.81), channel_id=1, source_target_pairs={{0,6},{2,4},{4,2},{6,0},{1,7},{3,5},{5,3},{7,1},{8,14},{10,12},{12... | collective-permute-start | bytes 995336 | tf_op jit(solution)/shard_map/ppermute | solution.py:578
  91.8 8.0 %collective-permute-start.17 = (f32[584,768]{1,0:T(8,128)S(1)}, f32[584,768]{1,0:T(8,128)S(1)}, u32[]{:S(2)}, u32[]{:S(2)}) collective-permute-start(f32[584,768]{1,0:T(8,128)S(1)} %get-tuple-element.87), channel_id=1, source_target_pairs={{0,1},{1,0},{2,3},{3,2},{4,5},{5,4},{6,7},{7,6},{8,9},{9,8},{10,11... | collective-permute-start | bytes 5382152 | tf_op jit(solution)/shard_map/ppermute | solution.py:629
  94.6 5.3 %collective-permute-start.8 = (bf16[528,1152]{1,0:T(8,128)(2,1)S(1)}, bf16[528,1152]{1,0:T(8,128)(2,1)S(1)}, u32[]{:S(2)}, u32[]{:S(2)}) collective-permute-start(bf16[528,1152]{1,0:T(8,128)(2,1)S(1)} %collective-permute-done.7.refs_0_), channel_id=1, source_target_pairs={{0,1},{1,0},{2,3},{3,2},{4,5},{5,4},{6,7},{7,6},{8,9},{9,8},{10,11... | collective-permute-start | bytes 3649544 | tf_op jit(solution)/shard_map/ppermute | solution.py:630
  97.3 2.5 %collective-permute-start.9 = (bf16[512,768]{1,0:T(8,128)(2,1)S(1)}, bf16[512,768]{1,0:T(8,128)(2,1)S(1)}, u32[]{:S(2)}, u32[]{:S(2)}) collective-permute-start(bf16[512,768]{1,0:T(8,128)(2,1)S(1)} %get-tuple-element.69.refs_1_), channel_id=1, source_target_pairs={{0,1},{1,0},{2,3},{3,2},{4,5},{5,4},{6,7},{7,6},{8,9},{9,8},{10,11... | collective-permute-start | bytes 2359304 | tf_op jit(solution)/shard_map/ppermute | solution.py:633
  97.9 1.9 %collective-permute-start.10 = (f32[8,768]{1,0:T(8,128)S(1)}, f32[8,768]{1,0:T(8,128)S(1)}, u32[]{:S(2)}, u32[]{:S(2)}) collective-permute-start(f32[8,768]{1,0:T(8,128)S(1)} %get-tuple-element.70.vec_far), channel_id=1, source_target_pairs={{0,1},{1,0},{2,3},{3,2},{4,5},{5,4},{6,7},{7,6},{8,9},{9,8},{10,11... | collective-permute-start | bytes 73736 | tf_op jit(solution)/shard_map/ppermute | solution.py:634
  99.2 4.1 %copy-start.7 = (f32[1,2,768]{2,1,0:T(2,128)S(1)}, f32[1,2,768]{2,1,0:T(2,128)}, u32[]{:S(2)}) copy-start(f32[1,2,768]{2,1,0:T(2,128)} %first_vec.1) | copy-start | bytes 18436
  102.8 3.0 %collective-permute-start.18 = (bf16[576,768]{1,0:T(8,128)(2,1)S(1)}, bf16[576,768]{1,0:T(8,128)(2,1)S(1)}, u32[]{:S(2)}, u32[]{:S(2)}) collective-permute-start(bf16[576,768]{1,0:T(8,128)(2,1)S(1)} %get-tuple-element.88.half_rows), channel_id=1, source_target_pairs={{0,1},{1,0},{2,3},{3,2},{4,5},{5,4},{6,7},{7,6},{8,9},{9,8},{10,11... | collective-permute-start | bytes 2654216 | tf_op jit(solution)/shard_map/ppermute | solution.py:512
  (4 other events, 9.3 us)

commit v9 on v8

--- a/solution.py
+++ b/solution.py
@@ -500,7 +500,7 @@
     pairs = pl.BlockSpec((1, 2, hid), lambda i, at: (0, 0, 0))
     full = pl.BlockSpec((1, tile, hid), lambda i, at: (0, at[0] * tiles + i, 0))
     new_half, grad = pl.pallas_call(
-        functools.partial(weights_kernel, low_cut, 2 * tiles),
+        functools.partial(weights_kernel, low_cut, 1),
         in_specs=[SMEM] + [VMEM] * 7,
         out_specs=[VMEM, VMEM],
         out_shape=(sds((half, hid), bf16), sds((half, hid), f32)),

time: 107 us -> 108 us (level)
  no operation moved by 1% of the time
where the time goes in v9:
time: 108 us; the launch traced here: 107 us
  waiting for transfers between devices  42.2 us (39%)
  Pallas kernels  37.4 us (35%)
  starting transfers between devices  24.9 us (23%)
  local copies, waits for them, and re-layouts  1.69 us (2%)
    ppermute x9, waiting for transfers between devices, exchange(): lax.ppermute(units[k], 'head', [(i, i ^ k) for i in range(heads)])  20.3 us
    pallas_call x4, Pallas kernels, learn(): pl.pallas_call(kernel, out_shape=outs, in_specs=[SMEM] + [HBM] * len(part...  17.3 us
    ppermute x1, waiting for transfers between devices, gathered(): next_out = lax.ppermute(inner, 'dp', out_pairs)  15 us
    ppermute x9, starting transfers between devices, exchange(): lax.ppermute(units[k], 'head', [(i, i ^ k) for i in range(heads)])  10.6 us
    pallas_call x3, Pallas kernels, pick(): pl.pallas_call(functools.partial(pick_kernel, unit, per_block, plan, len(...  9.38 us
    ppermute x1, starting transfers between devices, gathered(): outer = lax.ppermute(own, 'dp', outer_pairs)  4.89 us
    ppermute x1, starting transfers between devices, gathered(): far_got = lax.ppermute(far_sent, 'dp', end_pairs)  4.37 us
    ppermute x1, waiting for transfers between devices, gathered(): outer = lax.ppermute(own, 'dp', outer_pairs)  3.67 us
  transfers between devices with their start and end apart: 19, of which 9 were waited for; matrix products, arithmetic and copies ran while one was open for 0% of the time, Pallas kernels for 29%

profile of v9, /device:TPU:0, one launch (start us, length us, event | category | flops | bytes accessed | tf_op | source)
XLA Modules:
  0.0 107.4 jit_solution(11614289518741379321)
XLA Ops:
  0.6 2.2 %shard.1.refs_0_.refs_2_ = bf16[528,1152]{1,0:T(8,128)(2,1)} custom-call(s32[2,64]{1,0:T(2,128)} %bitcast.22, s32[2,8,64]{2,1,0:T(8,128)} %bitcast.21, bf16[512,1152]{1,0:T(8,128)(2,1)} %bitcast.20), custom_call_target="tpu_custom_call" | custom-call | tf_op jit(solution)/shard_map/shard/pallas_call | solution.py:100
  2.8 1.7 %collective-permute-start = (bf16[528,1152]{1,0:T(8,128)(2,1)}, bf16[528,1152]{1,0:T(8,128)(2,1)}, u32[]{:S(2)}, u32[]{:S(2)}) collective-permute-start(bf16[528,1152]{1,0:T(8,128)(2,1)} %shard.1.refs_0_.refs_2_), channel_id=1, source_target_pairs={{8,16},{16,8},{9,17},{17,9},{10,18},{18,10},{11,19},{19,11},{12,20... | collective-permute-start | bytes 3649544 | tf_op jit(solution)/shard_map/ppermute | solution.py:587
  4.5 4.9 %collective-permute-start.5 = (bf16[528,1152]{1,0:T(8,128)(2,1)}, bf16[528,1152]{1,0:T(8,128)(2,1)}, u32[]{:S(2)}, u32[]{:S(2)}) collective-permute-start(bf16[528,1152]{1,0:T(8,128)(2,1)} %shard.1.refs_0_.refs_2_), channel_id=1, source_target_pairs={{0,8},{8,0},{16,24},{24,16},{1,9},{9,1},{17,25},{25,17},{2,10},{10... | collective-permute-start | bytes 3649544 | tf_op jit(solution)/shard_map/ppermute | solution.py:588
  10.8 2.3 %pick.3 = (bf16[144,1152]{1,0:T(8,128)(2,1)S(1)}, bf16[144,1152]{1,0:T(8,128)(2,1)S(1)}, bf16[144,1152]{1,0:T(8,128)(2,1)S(1)}, bf16[144,1152]{1,0:T(8,128)(2,1)S(1)}) custom-call(s32[5]{0:T(128)S(1)} %stack.63.at_ref, bf16[528,1152]{1,0:T(8,128)(2,1)S(1)} %copy-done.1), custom_call_target="tpu_custom_call" | custom-call | flops 1 | bytes 1 | tf_op jit(solution)/shard_map/pick/pallas_call | solution.py:184
  13.1 1.6 %collective-permute-start.1 = (bf16[144,1152]{1,0:T(8,128)(2,1)S(1)}, bf16[144,1152]{1,0:T(8,128)(2,1)S(1)}, u32[]{:S(2)}, u32[]{:S(2)}) collective-permute-start(bf16[144,1152]{1,0:T(8,128)(2,1)S(1)} %get-tuple-element.53), channel_id=1, source_target_pairs={{0,2},{2,0},{4,6},{6,4},{1,3},{3,1},{5,7},{7,5},{8,10},{10,8},{12,... | collective-permute-start | bytes 995336 | tf_op jit(solution)/shard_map/ppermute | solution.py:578
  14.6 1.5 %collective-permute-start.2 = (bf16[144,1152]{1,0:T(8,128)(2,1)S(1)}, bf16[144,1152]{1,0:T(8,128)(2,1)S(1)}, u32[]{:S(2)}, u32[]{:S(2)}) collective-permute-start(bf16[144,1152]{1,0:T(8,128)(2,1)S(1)} %get-tuple-element.54), channel_id=1, source_target_pairs={{0,4},{2,6},{4,0},{6,2},{1,5},{3,7},{5,1},{7,3},{8,12},{10,14},{12... | collective-permute-start | bytes 995336 | tf_op jit(solution)/shard_map/ppermute | solution.py:578
  16.9 7.0 %collective-permute-done.1.refs_1_ = bf16[144,1152]{1,0:T(8,128)(2,1)S(1)} collective-permute-done((bf16[144,1152]{1,0:T(8,128)(2,1)S(1)}, bf16[144,1152]{1,0:T(8,128)(2,1)S(1)}, u32[]{:S(2)}, u32[]{:S(2)}) %collective-permute-start.1) | collective-permute-done | bytes 331808 | tf_op jit(solution)/shard_map/ppermute | solution.py:578
  23.9 6.6 %collective-permute-done.2.refs_2_ = bf16[144,1152]{1,0:T(8,128)(2,1)S(1)} collective-permute-done((bf16[144,1152]{1,0:T(8,128)(2,1)S(1)}, bf16[144,1152]{1,0:T(8,128)(2,1)S(1)}, u32[]{:S(2)}, u32[]{:S(2)}) %collective-permute-start.2) | collective-permute-done | bytes 331808 | tf_op jit(solution)/shard_map/ppermute | solution.py:578
  32.5 3.7 %collective-permute-done.5.refs_0_ = bf16[528,1152]{1,0:T(8,128)(2,1)} collective-permute-done((bf16[528,1152]{1,0:T(8,128)(2,1)}, bf16[528,1152]{1,0:T(8,128)(2,1)}, u32[]{:S(2)}, u32[]{:S(2)}) %collective-permute-start.5) | collective-permute-done | bytes 1216544 | tf_op jit(solution)/shard_map/ppermute | solution.py:588
  36.9 4.6 %pick.4 = (bf16[272,1152]{1,0:T(8,128)(2,1)S(1)}, bf16[272,1152]{1,0:T(8,128)(2,1)S(1)}, bf16[272,1152]{1,0:T(8,128)(2,1)S(1)}, bf16[272,1152]{1,0:T(8,128)(2,1)S(1)}) custom-call(s32[10]{0:T(128)S(1)} %stack.72.at_ref, bf16[528,1152]{1,0:T(8,128)(2,1)} %collective-permute-done.5.refs_0_, bf16[528,1152]{1,0:T(8,128)(2,1)} %collective-permute-done.refs_1_, ...), custom_call_target="tpu_custom_call" | custom-call | flops 34500001792 | bytes 1 | tf_op jit(solution)/shard_map/pick/pallas_call | solution.py:184
  41.5 1.5 %collective-permute-start.11 = (bf16[272,1152]{1,0:T(8,128)(2,1)S(1)}, bf16[272,1152]{1,0:T(8,128)(2,1)S(1)}, u32[]{:S(2)}, u32[]{:S(2)}) collective-permute-start(bf16[272,1152]{1,0:T(8,128)(2,1)S(1)} %get-tuple-element.59), channel_id=1, source_target_pairs={{0,2},{2,0},{4,6},{6,4},{1,3},{3,1},{5,7},{7,5},{8,10},{10,8},{12,... | collective-permute-start | bytes 1880072 | tf_op jit(solution)/shard_map/ppermute | solution.py:578
  43.1 1.5 %collective-permute-start.12 = (bf16[272,1152]{1,0:T(8,128)(2,1)S(1)}, bf16[272,1152]{1,0:T(8,128)(2,1)S(1)}, u32[]{:S(2)}, u32[]{:S(2)}) collective-permute-start(bf16[272,1152]{1,0:T(8,128)(2,1)S(1)} %get-tuple-element.60), channel_id=1, source_target_pairs={{0,4},{2,6},{4,0},{6,2},{1,5},{3,7},{5,1},{7,3},{8,12},{10,14},{12... | collective-permute-start | bytes 1880072 | tf_op jit(solution)/shard_map/ppermute | solution.py:578
  45.1 3.7 %learn.4 = (f32[1152,768]{1,0:T(8,128)S(1)}, f32[8,768]{1,0:T(8,128)S(1)}) custom-call(s32[2]{0:T(128)S(1)} %pad_add_fusion.at_ref, bf16[144,1152]{1,0:T(8,128)(2,1)S(1)} %get-tuple-element.62.refs_0_, bf16[144,1152]{1,0:T(8,128)(2,1)S(1)} %collective-permute-done.1.refs_1_, bf16[144,1152]{1,0:T(8,128)(2,1)S(1)} %collective-permute-done.2.refs_2_, ...), custom_call_target="tpu_custom_call" | custom-call | flops 1 | bytes 1 | tf_op jit(solution)/shard_map/learn/pallas_call | solution.py:413
  48.9 15.0 %collective-permute-done.4.refs_1_ = bf16[528,1152]{1,0:T(8,128)(2,1)S(1)} collective-permute-done((bf16[528,1152]{1,0:T(8,128)(2,1)}, bf16[528,1152]{1,0:T(8,128)(2,1)S(1)}, u32[]{:S(2)}, u32[]{:S(2)}) %collective-permute-start.4) | collective-permute-done | bytes 1216544 | tf_op jit(solution)/shard_map/ppermute | solution.py:603
  63.9 4.4 %collective-permute-start.7 = (bf16[528,1152]{1,0:T(8,128)(2,1)S(1)}, bf16[528,1152]{1,0:T(8,128)(2,1)S(1)}, u32[]{:S(2)}, u32[]{:S(2)}) collective-permute-start(bf16[528,1152]{1,0:T(8,128)(2,1)S(1)} %pack.1), channel_id=1, source_target_pairs={{0,24},{24,0},{1,25},{25,1},{2,26},{26,2},{3,27},{27,3},{4,28},{28... | collective-permute-start | bytes 3649544 | tf_op jit(solution)/shard_map/ppermute | solution.py:615
  68.3 2.5 %pick.5 = (bf16[144,1152]{1,0:T(8,128)(2,1)S(1)}, bf16[144,1152]{1,0:T(8,128)(2,1)S(1)}, bf16[144,1152]{1,0:T(8,128)(2,1)S(1)}, bf16[144,1152]{1,0:T(8,128)(2,1)S(1)}) custom-call(s32[5]{0:T(128)S(1)} %stack.74.at_ref, bf16[528,1152]{1,0:T(8,128)(2,1)S(1)} %collective-permute-done.6.refs_0_, bf16[528,1152]{1,0:T(8,128)(2,1)S(1)} %collective-permute-done.4.refs_1_), custom_call_target="tpu_custom_call" | custom-call | flops 5750000128 | bytes 1 | tf_op jit(solution)/shard_map/pick/pallas_call | solution.py:184
  72.4 1.5 %collective-permute-start.15 = (bf16[144,1152]{1,0:T(8,128)(2,1)S(1)}, bf16[144,1152]{1,0:T(8,128)(2,1)S(1)}, u32[]{:S(2)}, u32[]{:S(2)}) collective-permute-start(bf16[144,1152]{1,0:T(8,128)(2,1)S(1)} %get-tuple-element.80), channel_id=1, source_target_pairs={{0,4},{2,6},{4,0},{6,2},{1,5},{3,7},{5,1},{7,3},{8,12},{10,14},{12... | collective-permute-start | bytes 995336 | tf_op jit(solution)/shard_map/ppermute | solution.py:578
  74.7 6.0 %learn.6 = (f32[1152,768]{1,0:T(8,128)S(1)}, f32[8,768]{1,0:T(8,128)S(1)}) custom-call(s32[2]{0:T(128)S(1)} %pad_add_fusion.1.at_ref, bf16[272,1152]{1,0:T(8,128)(2,1)S(1)} %get-tuple-element.58.refs_0_, bf16[272,1152]{1,0:T(8,128)(2,1)S(1)} %collective-permute-done.11.refs_1_, bf16[272,1152]{1,0:T(8,128)(2,1)S(1)} %collective-permute-done.12.refs_2_, ...), custom_call_target="tpu_custom_call" | custom-call | flops 5750000128 | bytes 1 | tf_op jit(solution)/shard_map/learn/pallas_call | solution.py:413
  81.9 5.1 %collective-permute-done.15.refs_2_ = bf16[144,1152]{1,0:T(8,128)(2,1)S(1)} collective-permute-done((bf16[144,1152]{1,0:T(8,128)(2,1)S(1)}, bf16[144,1152]{1,0:T(8,128)(2,1)S(1)}, u32[]{:S(2)}, u32[]{:S(2)}) %collective-permute-start.15) | collective-permute-done | bytes 331808 | tf_op jit(solution)/shard_map/ppermute | solution.py:578
  87.0 4.8 %learn.7 = (f32[576,768]{1,0:T(8,128)S(1)}, f32[584,768]{1,0:T(8,128)S(1)}, f32[8,768]{1,0:T(8,128)S(1)}) custom-call(s32[2]{0:T(128)S(1)} %pad_add_fusion.1.at_ref, bf16[144,1152]{1,0:T(8,128)(2,1)S(1)} %get-tuple-element.78.refs_0_, bf16[144,1152]{1,0:T(8,128)(2,1)S(1)} %collective-permute-done.14.refs_1_, ...), custom_call_target="tpu_custom_call" | custom-call | flops 1 | bytes 1 | tf_op jit(solution)/shard_map/learn/pallas_call | solution.py:413
  91.9 2.6 %collective-permute-done.7.refs_0_ = bf16[528,1152]{1,0:T(8,128)(2,1)S(1)} collective-permute-done((bf16[528,1152]{1,0:T(8,128)(2,1)S(1)}, bf16[528,1152]{1,0:T(8,128)(2,1)S(1)}, u32[]{:S(2)}, u32[]{:S(2)}) %collective-permute-start.7) | collective-permute-done | bytes 1216544 | tf_op jit(solution)/shard_map/ppermute | solution.py:615
  94.6 2.7 %learn.5 = (bf16[512,768]{1,0:T(8,128)(2,1)S(1)}, f32[8,768]{1,0:T(8,128)S(1)}) custom-call(s32[2]{0:T(128)S(1)} %pad_add_fusion.1.at_ref, bf16[528,1152]{1,0:T(8,128)(2,1)S(1)} %collective-permute-done.7.refs_0_, bf16[1152,768]{1,0:T(8,128)(2,1)S(1)} %bitcast.18, bf16[1,768]{1,0:T(2,128)(2,1)S(1)} %copy-done.5, bf16[1,768]{1,0:T(2,128)(2,1)S(1)} %copy-done.6), custom_call_target="tpu_custom_call" | custom-call | flops 1 | bytes 1 | tf_op jit(solution)/shard_map/learn/pallas_call | solution.py:413
  100.0 3.3 %weights.1 = (bf16[576,768]{1,0:T(8,128)(2,1)S(1)}, f32[576,768]{1,0:T(8,128)S(1)}) custom-call(s32[1]{0:T(128)} %bitcast.at_ref, bf16[528,1152]{1,0:T(8,128)(2,1)S(1)} %collective-permute-done.8.rows_ref, bf16[512,768]{1,0:T(8,128)(2,1)S(1)} %collective-permute-done.9.low_ref, f32[576,768]{1,0:T(8,128)S(1)} %keep.1.kept, ...), custom_call_target="tpu_custom_call" | custom-call | flops 2300000000 | bytes 1 | tf_op jit(solution)/shard_map/weights/pallas_call | solution.py:502
  103.8 2.5 %moments.1 = (bf16[1,1152,768]{2,1,0:T(8,128)(2,1)}, bf16[1,2,768]{2,1,0:T(2,128)(2,1)}, f32[1,576,768]{2,1,0:T(8,128)}, f32[1,576,768]{2,1,0:T(8,128)}, f32[1,2,768]{2,1,0:T(2,128)}, /*index=5*/f32[1,2,768]{2,1,0:T(2,128)}) custom-call(s32[1]{0:T(128)} %bitcast.at_ref, f32[576,768]{1,0:T(8,128)S(1)} %get-tuple-element.89.grad_ref, ...), custom_call_target="tpu_custom_call" | custom-call | flops 3450000128 | bytes 1 | tf_op jit(solution)/shard_map/moments/pallas_call | solution.py:513
  (50 shorter events, 13.2 us)
Async XLA Ops:
  2.8 28.3 %collective-permute-start = (bf16[528,1152]{1,0:T(8,128)(2,1)}, bf16[528,1152]{1,0:T(8,128)(2,1)}, u32[]{:S(2)}, u32[]{:S(2)}) collective-permute-start(bf16[528,1152]{1,0:T(8,128)(2,1)} %shard.1.refs_0_.refs_2_), channel_id=1, source_target_pairs={{8,16},{16,8},{9,17},{17,9},{10,18},{18,10},{11,19},{19,11},{12,20... | collective-permute-start | bytes 3649544 | tf_op jit(solution)/shard_map/ppermute | solution.py:587
  4.5 31.7 %collective-permute-start.5 = (bf16[528,1152]{1,0:T(8,128)(2,1)}, bf16[528,1152]{1,0:T(8,128)(2,1)}, u32[]{:S(2)}, u32[]{:S(2)}) collective-permute-start(bf16[528,1152]{1,0:T(8,128)(2,1)} %shard.1.refs_0_.refs_2_), channel_id=1, source_target_pairs={{0,8},{8,0},{16,24},{24,16},{1,9},{9,1},{17,25},{25,17},{2,10},{10... | collective-permute-start | bytes 3649544 | tf_op jit(solution)/shard_map/ppermute | solution.py:588
  10.8 26.2 %copy-start.2 = (bf16[528,1152]{1,0:T(8,128)(2,1)S(1)}, bf16[528,1152]{1,0:T(8,128)(2,1)}, u32[]{:S(2)}) copy-start(bf16[528,1152]{1,0:T(8,128)(2,1)} %shard.1.refs_0_.refs_2_) | copy-start | bytes 3649540
  13.1 10.8 %collective-permute-start.1 = (bf16[144,1152]{1,0:T(8,128)(2,1)S(1)}, bf16[144,1152]{1,0:T(8,128)(2,1)S(1)}, u32[]{:S(2)}, u32[]{:S(2)}) collective-permute-start(bf16[144,1152]{1,0:T(8,128)(2,1)S(1)} %get-tuple-element.53), channel_id=1, source_target_pairs={{0,2},{2,0},{4,6},{6,4},{1,3},{3,1},{5,7},{7,5},{8,10},{10,8},{12,... | collective-permute-start | bytes 995336 | tf_op jit(solution)/shard_map/ppermute | solution.py:578
  14.6 15.8 %collective-permute-start.2 = (bf16[144,1152]{1,0:T(8,128)(2,1)S(1)}, bf16[144,1152]{1,0:T(8,128)(2,1)S(1)}, u32[]{:S(2)}, u32[]{:S(2)}) collective-permute-start(bf16[144,1152]{1,0:T(8,128)(2,1)S(1)} %get-tuple-element.54), channel_id=1, source_target_pairs={{0,4},{2,6},{4,0},{6,2},{1,5},{3,7},{5,1},{7,3},{8,12},{10,14},{12... | collective-permute-start | bytes 995336 | tf_op jit(solution)/shard_map/ppermute | solution.py:578
  16.2 14.3 %collective-permute-start.3 = (bf16[144,1152]{1,0:T(8,128)(2,1)S(1)}, bf16[144,1152]{1,0:T(8,128)(2,1)S(1)}, u32[]{:S(2)}, u32[]{:S(2)}) collective-permute-start(bf16[144,1152]{1,0:T(8,128)(2,1)S(1)} %get-tuple-element.55), channel_id=1, source_target_pairs={{0,6},{2,4},{4,2},{6,0},{1,7},{3,5},{5,3},{7,1},{8,14},{10,12},{12... | collective-permute-start | bytes 995336 | tf_op jit(solution)/shard_map/ppermute | solution.py:578
  31.0 14.1 %copy-start = (bf16[1,1152,768]{2,1,0:T(8,128)(2,1)S(1)}, bf16[1,1152,768]{2,1,0:T(8,128)(2,1)}, u32[]{:S(2)}) copy-start(bf16[1,1152,768]{2,1,0:T(8,128)(2,1)} %param.13) | copy-start | bytes 5308420
  31.0 14.1 %copy-start.5 = (bf16[1,768]{1,0:T(2,128)(2,1)S(1)}, bf16[1,768]{1,0:T(2,128)(2,1)}, u32[]{:S(2)}) copy-start(bf16[1,768]{1,0:T(2,128)(2,1)} %bias.1) | copy-start | bytes 4612
  31.1 14.1 %copy-start.6 = (bf16[1,768]{1,0:T(2,128)(2,1)S(1)}, bf16[1,768]{1,0:T(2,128)(2,1)}, u32[]{:S(2)}) copy-start(bf16[1,768]{1,0:T(2,128)(2,1)} %out.1) | copy-start | bytes 4612
  31.1 32.8 %collective-permute-start.4 = (bf16[528,1152]{1,0:T(8,128)(2,1)}, bf16[528,1152]{1,0:T(8,128)(2,1)S(1)}, u32[]{:S(2)}, u32[]{:S(2)}) collective-permute-start(bf16[528,1152]{1,0:T(8,128)(2,1)} %collective-permute-done.refs_1_), channel_id=1, source_target_pairs={{8,0},{16,24},{9,1},{17,25},{10,2},{18,26},{11,3},{19,27},{12,4},{... | collective-permute-start | bytes 3649544 | tf_op jit(solution)/shard_map/ppermute | solution.py:603
  36.2 27.7 %collective-permute-start.6 = (bf16[528,1152]{1,0:T(8,128)(2,1)}, bf16[528,1152]{1,0:T(8,128)(2,1)S(1)}, u32[]{:S(2)}, u32[]{:S(2)}) collective-permute-start(bf16[528,1152]{1,0:T(8,128)(2,1)} %collective-permute-done.5.refs_0_), channel_id=1, source_target_pairs={{8,16},{16,8},{9,17},{17,9},{10,18},{18,10},{11,19},{19,11},{12,20... | collective-permute-start | bytes 3649544 | tf_op jit(solution)/shard_map/ppermute | solution.py:604
  41.5 29.3 %collective-permute-start.11 = (bf16[272,1152]{1,0:T(8,128)(2,1)S(1)}, bf16[272,1152]{1,0:T(8,128)(2,1)S(1)}, u32[]{:S(2)}, u32[]{:S(2)}) collective-permute-start(bf16[272,1152]{1,0:T(8,128)(2,1)S(1)} %get-tuple-element.59), channel_id=1, source_target_pairs={{0,2},{2,0},{4,6},{6,4},{1,3},{3,1},{5,7},{7,5},{8,10},{10,8},{12,... | collective-permute-start | bytes 1880072 | tf_op jit(solution)/shard_map/ppermute | solution.py:578
  43.1 28.1 %collective-permute-start.12 = (bf16[272,1152]{1,0:T(8,128)(2,1)S(1)}, bf16[272,1152]{1,0:T(8,128)(2,1)S(1)}, u32[]{:S(2)}, u32[]{:S(2)}) collective-permute-start(bf16[272,1152]{1,0:T(8,128)(2,1)S(1)} %get-tuple-element.60), channel_id=1, source_target_pairs={{0,4},{2,6},{4,0},{6,2},{1,5},{3,7},{5,1},{7,3},{8,12},{10,14},{12... | collective-permute-start | bytes 1880072 | tf_op jit(solution)/shard_map/ppermute | solution.py:578
  44.6 26.6 %collective-permute-start.13 = (bf16[272,1152]{1,0:T(8,128)(2,1)S(1)}, bf16[272,1152]{1,0:T(8,128)(2,1)S(1)}, u32[]{:S(2)}, u32[]{:S(2)}) collective-permute-start(bf16[272,1152]{1,0:T(8,128)(2,1)S(1)} %get-tuple-element.61), channel_id=1, source_target_pairs={{0,6},{2,4},{4,2},{6,0},{1,7},{3,5},{5,3},{7,1},{8,14},{10,12},{12... | collective-permute-start | bytes 1880072 | tf_op jit(solution)/shard_map/ppermute | solution.py:578
  63.9 30.7 %collective-permute-start.7 = (bf16[528,1152]{1,0:T(8,128)(2,1)S(1)}, bf16[528,1152]{1,0:T(8,128)(2,1)S(1)}, u32[]{:S(2)}, u32[]{:S(2)}) collective-permute-start(bf16[528,1152]{1,0:T(8,128)(2,1)S(1)} %pack.1), channel_id=1, source_target_pairs={{0,24},{24,0},{1,25},{25,1},{2,26},{26,2},{3,27},{27,3},{4,28},{28... | collective-permute-start | bytes 3649544 | tf_op jit(solution)/shard_map/ppermute | solution.py:615
  71.2 10.7 %collective-permute-start.14 = (bf16[144,1152]{1,0:T(8,128)(2,1)S(1)}, bf16[144,1152]{1,0:T(8,128)(2,1)S(1)}, u32[]{:S(2)}, u32[]{:S(2)}) collective-permute-start(bf16[144,1152]{1,0:T(8,128)(2,1)S(1)} %get-tuple-element.79), channel_id=1, source_target_pairs={{0,2},{2,0},{4,6},{6,4},{1,3},{3,1},{5,7},{7,5},{8,10},{10,8},{12,... | collective-permute-start | bytes 995336 | tf_op jit(solution)/shard_map/ppermute | solution.py:578
  72.4 14.6 %collective-permute-start.15 = (bf16[144,1152]{1,0:T(8,128)(2,1)S(1)}, bf16[144,1152]{1,0:T(8,128)(2,1)S(1)}, u32[]{:S(2)}, u32[]{:S(2)}) collective-permute-start(bf16[144,1152]{1,0:T(8,128)(2,1)S(1)} %get-tuple-element.80), channel_id=1, source_target_pairs={{0,4},{2,6},{4,0},{6,2},{1,5},{3,7},{5,1},{7,3},{8,12},{10,14},{12... | collective-permute-start | bytes 995336 | tf_op jit(solution)/shard_map/ppermute | solution.py:578
  73.9 13.1 %collective-permute-start.16 = (bf16[144,1152]{1,0:T(8,128)(2,1)S(1)}, bf16[144,1152]{1,0:T(8,128)(2,1)S(1)}, u32[]{:S(2)}, u32[]{:S(2)}) collective-permute-start(bf16[144,1152]{1,0:T(8,128)(2,1)S(1)} %get-tuple-element.81), channel_id=1, source_target_pairs={{0,6},{2,4},{4,2},{6,0},{1,7},{3,5},{5,3},{7,1},{8,14},{10,12},{12... | collective-permute-start | bytes 995336 | tf_op jit(solution)/shard_map/ppermute | solution.py:578
  91.8 8.0 %collective-permute-start.17 = (f32[584,768]{1,0:T(8,128)S(1)}, f32[584,768]{1,0:T(8,128)S(1)}, u32[]{:S(2)}, u32[]{:S(2)}) collective-permute-start(f32[584,768]{1,0:T(8,128)S(1)} %get-tuple-element.87), channel_id=1, source_target_pairs={{0,1},{1,0},{2,3},{3,2},{4,5},{5,4},{6,7},{7,6},{8,9},{9,8},{10,11... | collective-permute-start | bytes 5382152 | tf_op jit(solution)/shard_map/ppermute | solution.py:629
  94.6 5.3 %collective-permute-start.8 = (bf16[528,1152]{1,0:T(8,128)(2,1)S(1)}, bf16[528,1152]{1,0:T(8,128)(2,1)S(1)}, u32[]{:S(2)}, u32[]{:S(2)}) collective-permute-start(bf16[528,1152]{1,0:T(8,128)(2,1)S(1)} %collective-permute-done.7.refs_0_), channel_id=1, source_target_pairs={{0,1},{1,0},{2,3},{3,2},{4,5},{5,4},{6,7},{7,6},{8,9},{9,8},{10,11... | collective-permute-start | bytes 3649544 | tf_op jit(solution)/shard_map/ppermute | solution.py:630
  97.3 2.5 %collective-permute-start.9 = (bf16[512,768]{1,0:T(8,128)(2,1)S(1)}, bf16[512,768]{1,0:T(8,128)(2,1)S(1)}, u32[]{:S(2)}, u32[]{:S(2)}) collective-permute-start(bf16[512,768]{1,0:T(8,128)(2,1)S(1)} %get-tuple-element.69.refs_1_), channel_id=1, source_target_pairs={{0,1},{1,0},{2,3},{3,2},{4,5},{5,4},{6,7},{7,6},{8,9},{9,8},{10,11... | collective-permute-start | bytes 2359304 | tf_op jit(solution)/shard_map/ppermute | solution.py:633
  97.9 1.9 %collective-permute-start.10 = (f32[8,768]{1,0:T(8,128)S(1)}, f32[8,768]{1,0:T(8,128)S(1)}, u32[]{:S(2)}, u32[]{:S(2)}) collective-permute-start(f32[8,768]{1,0:T(8,128)S(1)} %get-tuple-element.70.vec_far), channel_id=1, source_target_pairs={{0,1},{1,0},{2,3},{3,2},{4,5},{5,4},{6,7},{7,6},{8,9},{9,8},{10,11... | collective-permute-start | bytes 73736 | tf_op jit(solution)/shard_map/ppermute | solution.py:634
  99.2 4.6 %copy-start.7 = (f32[1,2,768]{2,1,0:T(2,128)S(1)}, f32[1,2,768]{2,1,0:T(2,128)}, u32[]{:S(2)}) copy-start(f32[1,2,768]{2,1,0:T(2,128)} %first_vec.1) | copy-start | bytes 18436
  103.3 3.0 %collective-permute-start.18 = (bf16[576,768]{1,0:T(8,128)(2,1)S(1)}, bf16[576,768]{1,0:T(8,128)(2,1)S(1)}, u32[]{:S(2)}, u32[]{:S(2)}) collective-permute-start(bf16[576,768]{1,0:T(8,128)(2,1)S(1)} %get-tuple-element.88.half_rows), channel_id=1, source_target_pairs={{0,1},{1,0},{2,3},{3,2},{4,5},{5,4},{6,7},{7,6},{8,9},{9,8},{10,11... | collective-permute-start | bytes 2654216 | tf_op jit(solution)/shard_map/ppermute | solution.py:512
  (4 other events, 9.8 us)
